TPU v7x, 32 devices: a whole 2x2x4 slice. The times are simulated.
32 devices in a mesh: rows: 16 (over z, y, core), pos: 2 (over x).
Axes of the slice: x: 2, y: 2, z: 4, core: 2. Of those that a mesh axis runs over, the one named last changes fastest.
Arguments:
- tokens: bfloat16 [64, 768, 768], P(('rows', 'pos')), may hold values from -6 to 6
- segments: int32 [64, 768], P(('rows', 'pos')), may hold values from 0 to 1, never falling along the last dimension, each value on 1 to 576 neighbouring positions
- cotangent: bfloat16 [64, 768, 768], P(('rows', 'pos')), may hold values from -6 to 6
- first_gain: float32 [768], replicated, may hold values from 0.5 to 1.5
- first_shift: float32 [768], replicated, may hold values from -1.25 to 1.25
- mixer_weight: bfloat16 [768, 2304], replicated, may hold values from -0.21875 to 0.21875
- mixer_bias: float32 [2304], replicated, may hold values from -1.25 to 1.25
- short_weight: float32 [3, 2304], replicated, may hold values from -3.5 to 3.5
- short_bias: float32 [2304], replicated, may hold values from -1.75 to 1.75
- embed_weight: float32 [33, 64], replicated, may hold values from -1 to 1
- embed_bias: float32 [64], replicated, may hold values from -3 to 3
- embed_omega: float32 [64], replicated, may hold values from 0.25 to 1.75
- inner_weight: float32 [64, 64], replicated, may hold values from -0.75 to 0.75
- inner_bias: float32 [64], replicated, may hold values from -3 to 3
- inner_omega: float32 [64], replicated, may hold values from 0.25 to 1.75
- outer_weight: float32 [64, 64], replicated, may hold values from -0.75 to 0.75
- outer_bias: float32 [64], replicated, may hold values from -3 to 3
- outer_omega: float32 [64], replicated, may hold values from 0.25 to 1.75
- filter_weight: float32 [64, 768], replicated, may hold values from -0.09375 to 0.09375
- skip_gain: float32 [768], replicated, may hold values from -6 to 6
- output_weight: bfloat16 [768, 768], replicated, may hold values from -0.21875 to 0.21875
- output_bias: float32 [768], replicated, may hold values from -1.25 to 1.25
- second_gain: float32 [768], replicated, may hold values from 0.5 to 1.5
- second_shift: float32 [768], replicated, may hold values from -1.25 to 1.25
- expand_weight: bfloat16 [768, 3072], replicated, may hold values from -0.21875 to 0.21875
- expand_bias: float32 [3072], replicated, may hold values from -1.25 to 1.25
- reduce_weight: bfloat16 [3072, 768], replicated, may hold values from -0.109375 to 0.109375
- reduce_bias: float32 [768], replicated, may hold values from -1.25 to 1.25
Outputs:
- block_out: bfloat16 [64, 768, 768], P(('rows', 'pos'))
- tokens_grad: bfloat16 [64, 768, 768], P(('rows', 'pos'))
- first_gain_grad: float32 [768], replicated
- first_shift_grad: float32 [768], replicated
- mixer_weight_grad: float32 [768, 2304], P('rows', 'pos')
- mixer_bias_grad: float32 [2304], replicated
- short_weight_grad: float32 [3, 2304], replicated
- short_bias_grad: float32 [2304], replicated
- embed_weight_grad: float32 [33, 64], replicated
- embed_bias_grad: float32 [64], replicated
- embed_omega_grad: float32 [64], replicated
- inner_weight_grad: float32 [64, 64], replicated
- inner_bias_grad: float32 [64], replicated
- inner_omega_grad: float32 [64], replicated
- outer_weight_grad: float32 [64, 64], replicated
- outer_bias_grad: float32 [64], replicated
- outer_omega_grad: float32 [64], replicated
- filter_weight_grad: float32 [64, 768], replicated
- skip_gain_grad: float32 [768], replicated
- output_weight_grad: float32 [768, 768], P('rows', 'pos')
- output_bias_grad: float32 [768], replicated
- second_gain_grad: float32 [768], replicated
- second_shift_grad: float32 [768], replicated
- expand_weight_grad: float32 [768, 3072], P('rows', 'pos')
- expand_bias_grad: float32 [3072], replicated
- reduce_weight_grad: float32 [3072, 768], P('rows', 'pos')
- reduce_bias_grad: float32 [768], replicated
Inputs may be any that keep to these rules, and one draw needn't show every extreme that they name: `segments`: in each row the ids run through all 2 documents in order, each document holding 1 to 576 tokens.
All inputs are finite; a program needn't handle non-finite values.
Results may differ from a plain program's by a relative error of at most 0.012.
Values may be sent and summed in bfloat16 or wider, within the bound.
A program may use at most 384 MiB of HBM per device.

v0:
```python
import math

import jax
import jax.numpy as jnp
from jax import lax
from jax.sharding import PartitionSpec as P

DOCS = 2
MICRO = 2


EPSILON = 1e-05
HIGHEST = lax.Precision.HIGHEST


def tables(length):
    size = 2 * length
    freqs = jnp.arange(length + 1, dtype=jnp.int32)
    places = jnp.arange(length, dtype=jnp.int32)
    turns = freqs[:, None] * places[None, :] % size
    angle = turns.astype(jnp.float32) * (2.0 * math.pi / size)
    cosine = jnp.cos(angle)
    sine = jnp.sin(angle[1:length])
    forward = jnp.concatenate([cosine, sine], axis=0).astype(jnp.bfloat16)
    weights = jnp.where((freqs == 0) | (freqs == length), 1.0, 2.0).astype(jnp.float32)
    inverse = jnp.concatenate([cosine * weights[:, None], 2.0 * sine], axis=0).T.astype(
        jnp.bfloat16
    )
    return (forward, inverse)


def pad_sine(part):
    zeros = jnp.zeros_like(part[..., :1, :])
    return jnp.concatenate([zeros, part, zeros], axis=-2)


def spectral_product(first, second, length):
    real_one = first[..., : length + 1, :]
    imag_one = pad_sine(first[..., length + 1 :, :])
    real_two = second[..., : length + 1, :]
    imag_two = pad_sine(second[..., length + 1 :, :])
    real = real_one * real_two - imag_one * imag_two
    imag = real_one * imag_two + imag_one * real_two
    return jnp.concatenate([real, imag[..., 1:length, :]], axis=-2)


def filter_values(places, length, params):
    (
        embed_weight,
        embed_bias,
        embed_omega,
        inner_weight,
        inner_bias,
        inner_omega,
        outer_weight,
        outer_bias,
        outer_omega,
        filter_weight,
    ) = params
    bands_count = (embed_weight.shape[0] - 1) // 2
    tnorm = places.astype(jnp.float32) / (length - 1)
    wave = places.astype(jnp.float32) * (2.0 * math.pi / length)
    bands = jnp.linspace(0.0001, bands_count - 1, bands_count).astype(jnp.float32)
    phase = wave[:, None] * bands[None, :]
    embedded = jnp.concatenate([tnorm[:, None], jnp.cos(phase), -jnp.sin(phase)], axis=1)
    state = jnp.sin(embed_omega * (jnp.dot(embedded, embed_weight, precision=HIGHEST) + embed_bias))
    state = jnp.sin(inner_omega * (jnp.dot(state, inner_weight, precision=HIGHEST) + inner_bias))
    state = jnp.sin(outer_omega * (jnp.dot(state, outer_weight, precision=HIGHEST) + outer_bias))
    width = filter_weight.shape[1]
    rates = jnp.abs(jnp.linspace(math.log(0.01) / 1.5, math.log(0.01) / 0.3, width)).astype(
        jnp.float32
    )
    window = jnp.exp(-tnorm[:, None] * rates[None, :])
    return jnp.dot(state, filter_weight, precision=HIGHEST) * window


def layer_norm(value, gain, shift):
    mean = jnp.mean(value, axis=-1, keepdims=True)
    centered = value - mean
    variance = jnp.mean(centered * centered, axis=-1, keepdims=True)
    return centered * lax.rsqrt(variance + EPSILON) * gain + shift


def lag_masks(segment_rows):
    columns = [jnp.ones(segment_rows.shape, jnp.float32)]
    for delay in (1, 2):
        earlier = jnp.pad(segment_rows, ((0, 0), (delay, 0)), constant_values=-1)[:, :-delay]
        columns.append((earlier == segment_rows).astype(jnp.float32))
    return jnp.stack(columns, axis=-1)


def short_conv(proj, same, short_weight, short_bias):
    result = short_bias + short_weight[0] * proj
    for delay in (1, 2):
        moved = jnp.pad(proj, ((0, 0), (delay, 0), (0, 0)))[:, :-delay, :]
        result = result + short_weight[delay] * moved * same[:, :, delay : delay + 1]
    return result


def exact_gelu(value):
    return jax.nn.gelu(value, approximate=False)


def accumulate(totals, update):
    if totals is None:
        return update
    return tuple((left + right for left, right in zip(totals, update)))


def on_device(
    tokens,
    segments,
    cotangent,
    first_gain,
    first_shift,
    mixer_weight,
    mixer_bias,
    short_weight,
    short_bias,
    embed_weight,
    embed_bias,
    embed_omega,
    inner_weight,
    inner_bias,
    inner_omega,
    outer_weight,
    outer_bias,
    outer_omega,
    filter_weight,
    skip_gain,
    output_weight,
    output_bias,
    second_gain,
    second_shift,
    expand_weight,
    expand_bias,
    reduce_weight,
    reduce_bias,
):
    floats = jnp.float32
    halves = jnp.bfloat16
    rows_here, length, width = tokens.shape
    size = 2 * length
    forward, inverse = tables(length)
    filter_params = (
        embed_weight,
        embed_bias,
        embed_omega,
        inner_weight,
        inner_bias,
        inner_omega,
        outer_weight,
        outer_bias,
        outer_omega,
        filter_weight,
    )
    share = length // lax.axis_size("pos")
    places = lax.axis_index("pos") * share + jnp.arange(share, dtype=jnp.int32)

    def make_filter(params):
        return filter_values(places, length, params)

    kernel, filter_pull = jax.vjp(make_filter, filter_params)
    kernel_low = kernel.astype(halves)
    columns = forward
    spectrum = jnp.dot(
        columns,
        lax.all_gather(kernel_low, "pos", axis=0, tiled=True),
        preferred_element_type=floats,
    )

    def product_of(first, second):
        return spectral_product(first, second, length)

    per_section = rows_here // MICRO
    outputs = []
    input_grads = []
    totals = None
    spectrum_grad = jnp.zeros_like(spectrum)
    for section in range(MICRO):
        lower = section * per_section
        inputs = tokens[lower : lower + per_section].astype(floats)
        segment_rows = segments[lower : lower + per_section]
        upstream = cotangent[lower : lower + per_section]
        upstream_wide = upstream.astype(floats)
        same = lag_masks(segment_rows)
        normed, norm_pull = jax.vjp(layer_norm, inputs, first_gain, first_shift)
        normed_low = normed.astype(halves)
        proj = (
            jnp.einsum("rld,de->rle", normed_low, mixer_weight, preferred_element_type=floats)
            + mixer_bias
        )

        def conv_short(values, weights, biases):
            return short_conv(values, same, weights, biases)

        mixed, short_pull = jax.vjp(conv_short, proj, short_weight, short_bias)
        gate_out = mixed[..., :width]
        gate_in = mixed[..., width : 2 * width]
        value = mixed[..., 2 * width :]
        inner = value * gate_in
        inner_low = inner.astype(halves)
        members = [(segment_rows == document).astype(floats)[..., None] for document in range(DOCS)]
        kept_spectra = []
        conv = jnp.zeros_like(inner)
        for document in range(DOCS):
            masked = inner_low * members[document].astype(halves)
            trans = jnp.einsum("ml,rld->rmd", forward, masked, preferred_element_type=floats)
            kept_spectra.append(trans)
            product = spectral_product(trans, spectrum, length).astype(halves)
            conv = conv + members[document] * jnp.einsum(
                "lm,rmd->rld", inverse, product, preferred_element_type=floats
            )
        conv = conv / size
        longconv = conv + skip_gain * inner
        mixer_low = (gate_out * longconv).astype(halves)
        attn = (
            jnp.einsum("rle,ed->rld", mixer_low, output_weight, preferred_element_type=floats)
            + output_bias
        )
        hidden = inputs + attn
        normed2, norm2_pull = jax.vjp(layer_norm, hidden, second_gain, second_shift)
        normed2_low = normed2.astype(halves)
        expand = (
            jnp.einsum("rld,df->rlf", normed2_low, expand_weight, preferred_element_type=floats)
            + expand_bias
        )
        active, gelu_pull = jax.vjp(exact_gelu, expand)
        active_low = active.astype(halves)
        reduced = (
            jnp.einsum("rlf,fd->rld", active_low, reduce_weight, preferred_element_type=floats)
            + reduce_bias
        )
        outputs.append((hidden + reduced).astype(halves))
        reduce_weight_grad = jnp.einsum(
            "rlf,rld->fd", active_low, upstream, preferred_element_type=floats
        )
        reduce_bias_grad = jnp.sum(upstream_wide, axis=(0, 1))
        active_grad = jnp.einsum(
            "rld,fd->rlf", upstream, reduce_weight, preferred_element_type=floats
        )
        (expand_grad,) = gelu_pull(active_grad)
        expand_low = expand_grad.astype(halves)
        expand_weight_grad = jnp.einsum(
            "rld,rlf->df", normed2_low, expand_low, preferred_element_type=floats
        )
        expand_bias_grad = jnp.sum(expand_low.astype(floats), axis=(0, 1))
        normed2_grad = jnp.einsum(
            "rlf,df->rld", expand_low, expand_weight, preferred_element_type=floats
        )
        hidden_part, second_gain_grad, second_shift_grad = norm2_pull(normed2_grad)
        hidden_grad = upstream_wide + hidden_part
        attn_low = hidden_grad.astype(halves)
        output_weight_grad = jnp.einsum(
            "rle,rld->ed", mixer_low, attn_low, preferred_element_type=floats
        )
        output_bias_grad = jnp.sum(attn_low.astype(floats), axis=(0, 1))
        mixer_grad = jnp.einsum(
            "rld,ed->rle", attn_low, output_weight, preferred_element_type=floats
        )
        gate_out_grad = mixer_grad * longconv
        long_grad = mixer_grad * gate_out
        conv_low = long_grad.astype(halves)
        skip_gain_grad = jnp.sum(long_grad * inner, axis=(0, 1))
        inner_grad = long_grad * skip_gain
        for document in range(DOCS):
            masked_grad = conv_low * members[document].astype(halves)
            product_grad = (
                jnp.einsum("lm,rld->rmd", inverse, masked_grad, preferred_element_type=floats)
                / size
            )
            _, product_pull = jax.vjp(product_of, kept_spectra[document], spectrum)
            trans_grad, spectrum_part = product_pull(product_grad)
            spectrum_grad = spectrum_grad + spectrum_part
            inner_part = jnp.einsum(
                "ml,rmd->rld", forward, trans_grad.astype(halves), preferred_element_type=floats
            )
            inner_grad = inner_grad + members[document] * inner_part
        value_grad = inner_grad * gate_in
        gate_in_grad = inner_grad * value
        mixed_grad = jnp.concatenate([gate_out_grad, gate_in_grad, value_grad], axis=-1)
        proj_grad, short_weight_grad, short_bias_grad = short_pull(mixed_grad)
        proj_low = proj_grad.astype(halves)
        mixer_weight_grad = jnp.einsum(
            "rld,rle->de", normed_low, proj_low, preferred_element_type=floats
        )
        mixer_bias_grad = jnp.sum(proj_low.astype(floats), axis=(0, 1))
        normed_grad = jnp.einsum(
            "rle,de->rld", proj_low, mixer_weight, preferred_element_type=floats
        )
        input_part, first_gain_grad, first_shift_grad = norm_pull(normed_grad)
        input_grads.append((input_part + hidden_grad).astype(halves))
        totals = accumulate(
            totals,
            (
                first_gain_grad,
                first_shift_grad,
                mixer_weight_grad,
                mixer_bias_grad,
                short_weight_grad,
                short_bias_grad,
                skip_gain_grad,
                output_weight_grad,
                output_bias_grad,
                second_gain_grad,
                second_shift_grad,
                expand_weight_grad,
                expand_bias_grad,
                reduce_weight_grad,
                reduce_bias_grad,
            ),
        )
    spectrum_low = spectrum_grad.astype(halves)
    columns = forward
    kernel_grad = lax.psum_scatter(
        lax.dot_general(
            columns, spectrum_low, (((0,), (0,)), ((), ())), preferred_element_type=floats
        ),
        "pos",
        scatter_dimension=0,
        tiled=True,
    )
    (filter_grads,) = filter_pull(kernel_grad)
    (
        first_gain_grad,
        first_shift_grad,
        mixer_weight_grad,
        mixer_bias_grad,
        short_weight_grad,
        short_bias_grad,
        skip_gain_grad,
        output_weight_grad,
        output_bias_grad,
        second_gain_grad,
        second_shift_grad,
        expand_weight_grad,
        expand_bias_grad,
        reduce_weight_grad,
        reduce_bias_grad,
    ) = totals
    matrices = (mixer_weight_grad, output_weight_grad, expand_weight_grad, reduce_weight_grad)
    matrices = (
        lax.psum_scatter(matrices[0], "rows", scatter_dimension=0, tiled=True),
        lax.psum_scatter(matrices[1], "rows", scatter_dimension=0, tiled=True),
        lax.psum_scatter(matrices[2], "rows", scatter_dimension=0, tiled=True),
        lax.psum_scatter(matrices[3], "rows", scatter_dimension=0, tiled=True),
    )
    matrices = (
        lax.psum_scatter(matrices[0], "pos", scatter_dimension=1, tiled=True),
        lax.psum_scatter(matrices[1], "pos", scatter_dimension=1, tiled=True),
        lax.psum_scatter(matrices[2], "pos", scatter_dimension=1, tiled=True),
        lax.psum_scatter(matrices[3], "pos", scatter_dimension=1, tiled=True),
    )
    summed = lax.psum(
        (
            first_gain_grad,
            first_shift_grad,
            mixer_bias_grad,
            short_weight_grad,
            short_bias_grad,
            filter_grads[0],
            filter_grads[1],
            filter_grads[2],
            filter_grads[3],
            filter_grads[4],
            filter_grads[5],
            filter_grads[6],
            filter_grads[7],
            filter_grads[8],
            filter_grads[9],
            skip_gain_grad,
            output_bias_grad,
            second_gain_grad,
            second_shift_grad,
            expand_bias_grad,
            reduce_bias_grad,
        ),
        ("rows", "pos"),
    )
    block_out = jnp.concatenate(outputs, axis=0)
    tokens_grad = jnp.concatenate(input_grads, axis=0)
    return (
        block_out,
        tokens_grad,
        summed[0],
        summed[1],
        matrices[0],
        summed[2],
        summed[3],
        summed[4],
        summed[5],
        summed[6],
        summed[7],
        summed[8],
        summed[9],
        summed[10],
        summed[11],
        summed[12],
        summed[13],
        summed[14],
        summed[15],
        matrices[1],
        summed[16],
        summed[17],
        summed[18],
        matrices[2],
        summed[19],
        matrices[3],
        summed[20],
    )


def solution(mesh):
    in_specs = (
        P(("rows", "pos"), None, None),
        P(("rows", "pos"), None),
        P(("rows", "pos"), None, None),
        P(),
        P(),
        P(),
        P(),
        P(),
        P(),
        P(),
        P(),
        P(),
        P(),
        P(),
        P(),
        P(),
        P(),
        P(),
        P(),
        P(),
        P(),
        P(),
        P(),
        P(),
        P(),
        P(),
        P(),
        P(),
    )
    out_specs = (
        P(("rows", "pos"), None, None),
        P(("rows", "pos"), None, None),
        P(),
        P(),
        P("rows", "pos"),
        P(),
        P(),
        P(),
        P(),
        P(),
        P(),
        P(),
        P(),
        P(),
        P(),
        P(),
        P(),
        P(),
        P(),
        P("rows", "pos"),
        P(),
        P(),
        P(),
        P("rows", "pos"),
        P(),
        P("rows", "pos"),
        P(),
    )
    return jax.shard_map(
        on_device, mesh=mesh, in_specs=in_specs, out_specs=out_specs, check_vma=False
    )
```

profile of v0, /device:TPU:0, one launch (start us, length us, event | category | flops | bytes accessed | tf_op | source)
XLA Modules:
  0.0 1251.2 jit_solution(3296906112511360404)
XLA Ops:
  20.4 9.8 fusion.190
  45.4 5.2 fusion.271
  50.7 5.3 fusion.274
  57.4 10.9 add_bitcast_fusion.1
  68.4 17.7 %fusion.21 = (f32[1,768,2304]{2,1,0:T(8,128)S(1)}, f32[1,768,2304]{2,1,0:T(8,128)S(1)}) fusion(f32[768,2304]{1,0:T(8,128)} %fusion.274, f32[1,768,2304]{2,1,0:T(8,128)} %get-tuple-element.225, f32[768]{0:T(1024)} %get-tuple-element.112, f32[2304]{0:T(1024)S(1)} %get-tuple-element.102, f32[768]{0:T(1024)S(1)} %get-tuple-element.111, ...), kind=kLoop, calls=%fused_computation.79 | loop fusion | flops 31850496 | bytes 42525696 | tf_op jit(solution)/shard_map/jvp()/add | solution.py:96
  89.6 8.9 multiply_convert_fusion.5
  98.5 4.5 convolution_bitcast_fusion
  105.4 3.4 fusion.297
  116.8 10.1 multiply_convert_fusion.2
  135.4 4.6 fusion.296
  147.4 4.0 fusion.285
  155.6 12.0 fusion.53
  168.1 7.2 fusion.140
  175.3 9.4 fusion.149
  196.8 28.0 %multiply_convert_fusion = (bf16[768,3072]{1,0:T(8,128)(2,1)}, f32[768,3072]{1,0:T(8,128)}, f32[768,3072]{1,0:T(8,128)}) fusion(f32[3072]{0:T(1024)S(1)} %copy-done.229, bf16[768,3072]{1,0:T(8,128)(2,1)S(1)} %bitcast.421, f32[1,768,768]{1,2,0:T(8,128)S(1)} %get-tuple-element.234, f32[768]{0:T(1024)S(1)} %fusion.244, f32[768]{0:T(1024)S(1)} %broadcast_multiply_fusion, ...), kind=kOutput, calls=%fused_computation.8 | convolution fusion | flops 3782541312 | bytes 30695424 | tf_op jit(solution)/shard_map/rld,df->rlf/dot_general | solution.py:225
  224.8 12.8 %convert_reduce_fusion = (f32[3072]{0:T(1024)}, bf16[768,3072]{1,0:T(8,128)(2,1)}) fusion(f32[768,3072]{1,0:T(8,128)} %get-tuple-element.154, bf16[3072,768]{1,0:T(8,128)(2,1)S(1)} %bitcast.425, bf16[2,768,768]{2,1,0:T(8,128)(2,1)S(1)} %copy-done.112, f32[768,3072]{1,0:T(8,128)} %get-tuple-element.235, f32[3072]{0:T(1024)S(1)} %copy-done.229), kind=kOutput, calls=%fused_computation.4 | convolution fusion | flops 3663983616 | bytes 29515776 | tf_op jit(solution)/shard_map/rld,fd->rlf/dot_general | solution.py:239
  237.6 8.2 fusion.306
  248.8 3.8 fusion.117
  257.1 5.2 multiply_reduce_fusion.4
  271.2 9.5 fusion.44
  280.7 4.7 fusion.148
  297.5 27.8 %multiply_convert_fusion.1 = (bf16[768,3072]{1,0:T(8,128)(2,1)}, f32[768,3072]{1,0:T(8,128)}, f32[768,3072]{1,0:T(8,128)}) fusion(f32[3072]{0:T(1024)S(1)} %copy-done.230, bf16[768,3072]{1,0:T(8,128)(2,1)S(1)} %bitcast.423, f32[1,768,768]{1,2,0:T(8,128)S(1)} %get-tuple-element.237, f32[768]{0:T(1024)S(1)} %copy-done.234, f32[768]{0:T(1024)S(1)} %copy-done.158, ...), kind=kOutput, calls=%fused_computation.21 | convolution fusion | flops 3782541312 | bytes 30695424 | tf_op jit(solution)/shard_map/rld,df->rlf/dot_general | solution.py:225
  325.3 12.6 %convert_reduce_fusion.1 = (f32[3072]{0:T(1024)}, bf16[768,3072]{1,0:T(8,128)(2,1)}) fusion(f32[768,3072]{1,0:T(8,128)} %get-tuple-element.152, bf16[3072,768]{1,0:T(8,128)(2,1)S(1)} %bitcast.427, bf16[2,768,768]{2,1,0:T(8,128)(2,1)S(1)} %copy-done.113, f32[768,3072]{1,0:T(8,128)} %get-tuple-element.238, f32[3072]{0:T(1024)S(1)} %copy-done.230), kind=kOutput, calls=%fused_computation.5 | convolution fusion | flops 3663983616 | bytes 29515776 | tf_op jit(solution)/shard_map/rld,fd->rlf/dot_general | solution.py:239
  338.0 8.3 fusion.305
  349.5 3.8 fusion.118
  359.6 5.1 multiply_reduce_fusion.5
  378.5 7.6 fusion.41
  386.1 10.0 pad_maximum_fusion.4
  396.1 7.9 fusion.42
  404.1 3.6 slice_negate_fusion.1
  410.4 12.9 %multiply_add_fusion.2 = (f32[1,767,768]{1,2,0:T(8,128)}, f32[1,767,768]{1,2,0:T(8,128)S(1)}, f32[1,767,768]{1,2,0:T(8,128)}, f32[1,767,768]{1,2,0:T(8,128)S(1)}) fusion(f32[1,769,768]{1,2,0:T(8,128)} %get-tuple-element.184, f32[1,767,768]{1,2,0:T(8,128)} %copy-done.3, f32[1,769,768]{1,2,0:T(8,128)} %get-tuple-element.187, f32[1,769,768]{1,2,0:T(8,128)} %copy-done.31, ...), kind=kLoop, calls=%fused_computation.287 | loop fusion | flops 7068672 | bytes 32987136 | tf_op jit(solution)/shard_map/transpose(jvp())/add_any | solution.py:42
  423.3 3.7 fusion.84
  427.0 3.7 fusion.78
  437.2 3.5 fusion.94
  447.4 3.5 fusion.90
  450.8 12.9 %fusion.127 = f32[768,768]{1,0:T(8,128)} fusion(f32[769,768]{0,1:T(8,128)} %get-tuple-element.219, f32[767,768]{0,1:T(8,128)} %fusion.90, f32[769,768]{0,1:T(8,128)} %get-tuple-element.169, f32[767,768]{0,1:T(8,128)} %fusion.92, f32[769,768]{0,1:T(8,128)S(1)} %copy-done.106, f32[767,768]{0,1:T(8,128)} %fusion.94, f32[769,768]{0,1:T(8,128)} %get-tuple-element.199, ...), kind=kOutput, calls=%fused_computation.296 | convolution fusion | flops 1826095104 | bytes 23592960 | tf_op jit(solution)/shard_map/dot_general | solution.py:316
  464.4 8.8 slice_multiply_fusion.6
  473.4 11.4 slice_multiply_fusion.9
  484.9 9.7 multiply_reduce_fusion.1
  494.6 9.1 multiply_reduce_fusion.3
  503.7 17.5 %convert_reduce_fusion.3 = (f32[2304]{0:T(1024)}, bf16[1,768,2304]{2,1,0:T(8,128)(2,1)}, f32[2304]{0:T(1024)}, bf16[1,768,2304]{2,1,0:T(8,128)(2,1)}) fusion(f32[1,768,768]{2,1,0:T(8,128)} %get-tuple-element.156, f32[1,768,768]{2,1,0:T(8,128)} %copy-done.20, f32[1,768,768]{2,1,0:T(8,128)} %get-tuple-element.207, f32[2304]{0:T(1024)S(1)} %copy-done.154, ...), kind=kLoop, calls=%fused_computation.85 | loop fusion | flops 28306944 | bytes 49572864 | tf_op jit(solution)/shard_map/reduce_sum | solution.py:287
  521.3 5.3 fusion.25
  526.6 5.4 convolution_add_fusion
  532.1 6.8 fusion.279
  539.0 9.1 convolution_add_fusion.2
  548.2 6.6 fusion.159
  554.9 9.2 convolution_add_fusion.1
  564.1 7.4 fusion.303
  571.6 3.5 copy.98
  575.0 7.0 fusion.304
  585.2 10.3 fusion.18
  612.3 3.7 multiply_reduce_fusion.8
  626.0 3.4 fusion.191
  630.0 110.4 %reduce-scatter.20.cloned.1.call-done = f32[48,3072]{1,0:T(8,128)} async-done(((f32[768,3072]{1,0:T(8,128)}), f32[48,3072]{1,0:T(8,128)}) %reduce-scatter.20.cloned.1.call-update) | async-done | bytes 589840 | tf_op jit(solution)/shard_map/reduce_scatter | solution.py:345
  743.8 4.3 copy.110
  748.1 10.4 fusion.124
  758.5 97.0 %reduce-scatter.24.cloned.1.call-done = f32[192,768]{1,0:T(8,128)} async-done(((f32[3072,768]{1,0:T(8,128)}), f32[192,768]{1,0:T(8,128)}) %reduce-scatter.24.cloned.1.call-update) | async-done | bytes 589840 | tf_op jit(solution)/shard_map/reduce_scatter | solution.py:346
  855.6 8.4 fusion.121
  865.6 4.3 copy.109
  869.9 162.2 %all-reduce.44.cloned.1.call-done = (f32[768]{0:T(1024)}, f32[768]{0:T(1024)}, f32[2304]{0:T(1024)}, f32[3,2304]{1,0:T(4,128)}, f32[2304]{0:T(1024)}, /*index=5*...) async-done(((f32[768]{0:T(1024)}, f32[768]{0:T(1024)}, ...) | async-done | bytes 122640 | tf_op jit(solution)/shard_map/psum | solution.py:354
  1032.1 131.7 %all-reduce.42.cloned.1.call-done = f32[64,768]{1,0:T(8,128)} async-done(((f32[64,768]{1,0:T(8,128)}), f32[64,768]{1,0:T(8,128)}) %all-reduce.42.cloned.1.call-update) | async-done | bytes 196624 | tf_op jit(solution)/shard_map/psum | solution.py:354
  1163.8 17.4 %reduce-scatter.12.cloned.1.call-done = f32[48,1152]{1,0:T(8,128)} async-done(((f32[48,2304]{1,0:T(8,128)}), f32[48,1152]{1,0:T(8,128)}) %reduce-scatter.12.cloned.1.call-update) | async-done | bytes 221200 | tf_op jit(solution)/shard_map/reduce_scatter | solution.py:349
  1181.2 18.1 %reduce-scatter.22.cloned.1.call-done = f32[48,1536]{1,0:T(8,128)} async-done(((f32[48,3072]{1,0:T(8,128)}), f32[48,1536]{1,0:T(8,128)}) %reduce-scatter.22.cloned.1.call-update) | async-done | bytes 294928 | tf_op jit(solution)/shard_map/reduce_scatter | solution.py:351
  1199.3 18.1 %reduce-scatter.26.cloned.1.call-done = f32[192,384]{1,0:T(8,128)} async-done(((f32[192,768]{1,0:T(8,128)}), f32[192,384]{1,0:T(8,128)}) %reduce-scatter.26.cloned.1.call-update) | async-done | bytes 294928 | tf_op jit(solution)/shard_map/reduce_scatter | solution.py:352
  (695 shorter events, 205.5 us)
Async XLA Ops:
  7.2 38.2 %copy-start = (bf16[768,2304]{1,0:T(8,128)(2,1)S(1)}, bf16[768,2304]{1,0:T(8,128)(2,1)}, u32[]{:S(2)}) copy-start(bf16[768,2304]{1,0:T(8,128)(2,1)} %param.33) | copy-start | bytes 10616836
  7.2 140.2 %all-gather.2.cloned.1.call-start = ((), (), s32[]{:S(2)}) async-start(), calls=%async_computation.9 | async-start | bytes 1769472 | tf_op jit(solution)/shard_map/all_gather | solution.py:168
  17.3 12.9 %copy-start.196 = (s32[2,768]{1,0:T(2,128)S(1)}, s32[2,768]{1,0:T(2,128)}, u32[]{:S(2)}) copy-start(s32[2,768]{1,0:T(2,128)} %param.29) | copy-start | bytes 18436
  17.3 594.8 %reduce-scatter.16.cloned.1.call-start = ((), (), s32[]{:S(2)}) async-start(), calls=%async_computation.14 | async-start | bytes 2506752 | tf_op jit(solution)/shard_map/reduce_scatter | solution.py:344
  17.8 14.2 %copy-start.110 = (bf16[2,768,768]{2,1,0:T(8,128)(2,1)S(1)}, bf16[2,768,768]{2,1,0:T(8,128)(2,1)}, u32[]{:S(2)}) copy-start(bf16[2,768,768]{2,1,0:T(8,128)(2,1)} %param.28) | copy-start | bytes 7077892
  37.5 13.2 %copy-start.140 = (f32[768]{0:T(1024)}, f32[768]{0:T(1024)S(1)}, u32[]{:S(2)}) copy-start(f32[768]{0:T(1024)S(1)} %broadcast_multiply_fusion.3) | copy-start | bytes 9220
  56.7 11.6 copy-start.151
  86.0 17.0 %copy-start.16 = (f32[1,768,2304]{2,1,0:T(8,128)}, f32[1,768,2304]{2,1,0:T(8,128)S(1)}, u32[]{:S(2)}) copy-start(f32[1,768,2304]{2,1,0:T(8,128)S(1)} %get-tuple-element.222) | copy-start | bytes 21233668
  86.1 22.7 %copy-start.15 = (f32[1,768,2304]{2,1,0:T(8,128)}, f32[1,768,2304]{2,1,0:T(8,128)S(1)}, u32[]{:S(2)}) copy-start(f32[1,768,2304]{2,1,0:T(8,128)S(1)} %get-tuple-element.221) | copy-start | bytes 21233668
  89.5 13.5 %copy-start.92 = (f32[1,768,768]{2,1,0:T(8,128)}, f32[1,768,768]{2,1,0:T(8,128)S(1)}, u32[]{:S(2)}) copy-start(f32[1,768,768]{2,1,0:T(8,128)S(1)} %slice_multiply_fusion.5) | copy-start | bytes 7077892
  105.4 21.5 %copy-start.34 = (f32[1,1536,768]{1,2,0:T(8,128)}, f32[1,1536,768]{1,2,0:T(8,128)S(1)}, u32[]{:S(2)}) copy-start(f32[1,1536,768]{1,2,0:T(8,128)S(1)} %convolution_bitcast_fusion.1) | copy-start | bytes 14155780
  111.9 16.8 %copy-start.33 = (f32[1,1536,768]{1,2,0:T(8,128)}, f32[1,1536,768]{1,2,0:T(8,128)S(1)}, u32[]{:S(2)}) copy-start(f32[1,1536,768]{1,2,0:T(8,128)S(1)} %convolution_bitcast_fusion.2) | copy-start | bytes 14155780
  151.5 16.1 %copy-start.17 = (f32[1536,768]{0,1:T(8,128)}, f32[1536,768]{0,1:T(8,128)S(1)}, u32[]{:S(2)}) copy-start(f32[1536,768]{0,1:T(8,128)S(1)} %fusion.285) | copy-start | bytes 14155780
  154.0 13.6 %slice-start.8 = ((s8[4718592]{0:T(1024)(128)(4,1)}), s8[4194304]{0:T(1024)(128)(4,1)S(1)}, s32[]{:S(2)}) async-start(s8[4718592]{0:T(1024)(128)(4,1)} %bitcast.414), calls=%async_computation.29 | async-start | bytes 8388608
  154.1 13.6 %slice-start.12 = ((s8[4718592]{0:T(1024)(128)(4,1)}), s8[4194304]{0:T(1024)(128)(4,1)S(1)}, s32[]{:S(2)}) async-start(s8[4718592]{0:T(1024)(128)(4,1)} %bitcast.418), calls=%async_computation.33 | async-start | bytes 8388608
  155.4 19.9 %copy-start.31 = (f32[1,769,768]{1,2,0:T(8,128)}, f32[1,769,768]{1,2,0:T(8,128)S(1)}, u32[]{:S(2)}) copy-start(f32[1,769,768]{1,2,0:T(8,128)S(1)} %fusion.49) | copy-start | bytes 7087108
  155.5 12.1 copy-start.21
  155.5 12.1 slice-start.9
  155.5 12.1 slice-start.13
  155.5 12.6 %copy-start.36 = (f32[1,767,768]{1,2,0:T(8,128)S(1)}, f32[1,767,768]{1,2,0:T(8,128)}, u32[]{:S(2)}) copy-start(f32[1,767,768]{1,2,0:T(8,128)} %get-tuple-element.188) | copy-start | bytes 7068676
  193.1 31.6 %slice-start.18 = ((s8[4718592]{0:T(1024)(128)(4,1)}), s8[4194304]{0:T(1024)(128)(4,1)S(1)}, s32[]{:S(2)}) async-start(s8[4718592]{0:T(1024)(128)(4,1)} %bitcast.424), calls=%async_computation.39 | async-start | bytes 8388608
  194.4 30.3 %copy-start.38 = (f32[1,768,768]{1,2,0:T(8,128)}, f32[1,768,768]{1,2,0:T(8,128)S(1)}, u32[]{:S(2)}) copy-start(f32[1,768,768]{1,2,0:T(8,128)S(1)} %get-tuple-element.234) | copy-start | bytes 7077892
  194.5 58.1 %copy-start.155 = (f32[768]{0:T(1024)}, f32[768]{0:T(1024)S(1)}, u32[]{:S(2)}) copy-start(f32[768]{0:T(1024)S(1)} %broadcast_multiply_fusion) | copy-start | bytes 9220
  196.8 55.9 %copy-start.188 = (f32[768]{0:T(1024)}, f32[768]{0:T(1024)S(1)}, u32[]{:S(2)}) copy-start(f32[768]{0:T(1024)S(1)} %fusion.244) | copy-start | bytes 9220
  196.8 28.0 %copy-start.112 = (bf16[2,768,768]{2,1,0:T(8,128)(2,1)S(1)}, bf16[2,768,768]{2,1,0:T(8,128)(2,1)}, u32[]{:S(2)}) copy-start(bf16[2,768,768]{2,1,0:T(8,128)(2,1)} %param.30) | copy-start | bytes 7077892
  196.8 28.0 %slice-start.19 = ((s8[4718592]{0:T(1024)(128)(4,1)}), s8[524288]{0:T(1024)(128)(4,1)S(1)}, s32[]{:S(2)}) async-start(s8[4718592]{0:T(1024)(128)(4,1)} %bitcast.424), calls=%async_computation.40 | async-start | bytes 1048576
  257.1 11.5 slice-start.4
  268.6 12.0 copy-start.24
  293.9 31.5 %slice-start.20 = ((s8[4718592]{0:T(1024)(128)(4,1)}), s8[4194304]{0:T(1024)(128)(4,1)S(1)}, s32[]{:S(2)}) async-start(s8[4718592]{0:T(1024)(128)(4,1)} %bitcast.426), calls=%async_computation.41 | async-start | bytes 8388608
  295.2 30.2 %copy-start.41 = (f32[1,768,768]{1,2,0:T(8,128)}, f32[1,768,768]{1,2,0:T(8,128)S(1)}, u32[]{:S(2)}) copy-start(f32[1,768,768]{1,2,0:T(8,128)S(1)} %get-tuple-element.237) | copy-start | bytes 7077892
  295.2 58.1 %copy-start.157 = (f32[768]{0:T(1024)}, f32[768]{0:T(1024)S(1)}, u32[]{:S(2)}) copy-start(f32[768]{0:T(1024)S(1)} %broadcast_multiply_fusion.2) | copy-start | bytes 9220
  297.5 55.9 %copy-start.190 = (f32[768]{0:T(1024)}, f32[768]{0:T(1024)S(1)}, u32[]{:S(2)}) copy-start(f32[768]{0:T(1024)S(1)} %fusion.242) | copy-start | bytes 9220
  297.5 27.8 %copy-start.113 = (bf16[2,768,768]{2,1,0:T(8,128)(2,1)S(1)}, bf16[2,768,768]{2,1,0:T(8,128)(2,1)}, u32[]{:S(2)}) copy-start(bf16[2,768,768]{2,1,0:T(8,128)(2,1)} %param.30) | copy-start | bytes 7077892
  297.5 27.8 %slice-start.21 = ((s8[4718592]{0:T(1024)(128)(4,1)}), s8[524288]{0:T(1024)(128)(4,1)S(1)}, s32[]{:S(2)}) async-start(s8[4718592]{0:T(1024)(128)(4,1)} %bitcast.426), calls=%async_computation.42 | async-start | bytes 1048576
  372.5 23.5 %copy-start.5 = (f32[1,767,768]{1,2,0:T(8,128)}, f32[1,767,768]{1,2,0:T(8,128)S(1)}, u32[]{:S(2)}) copy-start(f32[1,767,768]{1,2,0:T(8,128)S(1)} %split.76) | copy-start | bytes 7068676
  374.3 21.8 %copy-start.1 = (f32[1,767,768]{1,2,0:T(8,128)}, f32[1,767,768]{1,2,0:T(8,128)S(1)}, u32[]{:S(2)}) copy-start(f32[1,767,768]{1,2,0:T(8,128)S(1)} %split.91) | copy-start | bytes 7068676
  378.5 17.6 %copy-start.3 = (f32[1,767,768]{1,2,0:T(8,128)}, f32[1,767,768]{1,2,0:T(8,128)S(1)}, u32[]{:S(2)}) copy-start(f32[1,767,768]{1,2,0:T(8,128)S(1)} %split.81) | copy-start | bytes 7068676
  378.5 17.6 %slice-start.6 = ((s8[4718592]{0:T(1024)(128)(4,1)}), s8[4194304]{0:T(1024)(128)(4,1)S(1)}, s32[]{:S(2)}) async-start(s8[4718592]{0:T(1024)(128)(4,1)} %bitcast.406), calls=%async_computation.27 | async-start | bytes 8388608
  410.3 201.9 %reduce-scatter.14.cloned.1.call-start = ((), (), s32[]{:S(2)}) async-start(), calls=%async_computation.12 | async-start | bytes 3538944 | tf_op jit(solution)/shard_map/reduce_scatter | solution.py:315
  410.3 12.9 %copy-start.64 = (bf16[769,768]{1,0:T(8,128)(2,1)S(1)}, bf16[769,768]{1,0:T(8,128)(2,1)}, u32[]{:S(2)}) copy-start(bf16[769,768]{1,0:T(8,128)(2,1)} %fusion.190) | copy-start | bytes 3543556
  410.3 12.9 %copy-start.68 = (bf16[767,768]{1,0:T(8,128)(2,1)S(1)}, bf16[767,768]{1,0:T(8,128)(2,1)}, u32[]{:S(2)}) copy-start(bf16[767,768]{1,0:T(8,128)(2,1)} %copy-done.66) | copy-start | bytes 3534340
  410.4 12.9 %copy-start.107 = (f32[1,769,768]{1,2,0:T(8,128)S(1)}, f32[1,769,768]{1,2,0:T(8,128)}, u32[]{:S(2)}) copy-start(f32[1,769,768]{1,2,0:T(8,128)} %get-tuple-element.170) | copy-start | bytes 7087108
  463.7 165.7 %reduce-scatter.10.cloned.1.call-start = ((), (), s32[]{:S(2)}) async-start(), calls=%async_computation.10 | async-start | bytes 7520256 | tf_op jit(solution)/shard_map/reduce_scatter | solution.py:343
  473.3 30.3 %copy-start.18 = (f32[1,768,768]{2,1,0:T(8,128)}, f32[1,768,768]{2,1,0:T(8,128)S(1)}, u32[]{:S(2)}) copy-start(f32[1,768,768]{2,1,0:T(8,128)S(1)} %get-tuple-element.157) | copy-start | bytes 7077892
  473.3 30.3 %copy-start.19 = (f32[1,768,768]{2,1,0:T(8,128)}, f32[1,768,768]{2,1,0:T(8,128)S(1)}, u32[]{:S(2)}) copy-start(f32[1,768,768]{2,1,0:T(8,128)S(1)} %get-tuple-element.158) | copy-start | bytes 7077892
  473.3 11.5 slice-start.2
  473.4 11.4 slice-start.3
  473.4 11.4 copy-start.152
  503.6 17.5 %copy-start.13 = (bf16[1,768,768]{1,2,0:T(8,128)(2,1)S(1)}, bf16[1,768,768]{1,2,0:T(8,128)(2,1)}, u32[]{:S(2)}) copy-start(bf16[1,768,768]{1,2,0:T(8,128)(2,1)} %copy.124) | copy-start | bytes 3538948
  503.7 17.5 %copy-start.134 = (f32[768]{0:T(1024)S(1)}, f32[768]{0:T(1024)}, u32[]{:S(2)}) copy-start(f32[768]{0:T(1024)} %param.31) | copy-start | bytes 9220
  503.7 17.5 %copy-start.137 = (f32[768]{0:T(1024)S(1)}, f32[768]{0:T(1024)}, u32[]{:S(2)}) copy-start(f32[768]{0:T(1024)} %param.32) | copy-start | bytes 9220
  503.7 17.5 %copy-start.141 = (f32[768]{0:T(1024)S(1)}, f32[768]{0:T(1024)}, u32[]{:S(2)}) copy-start(f32[768]{0:T(1024)} %copy-done.140) | copy-start | bytes 9220
  503.7 17.5 %copy-start.143 = (f32[768]{0:T(1024)S(1)}, f32[768]{0:T(1024)}, u32[]{:S(2)}) copy-start(f32[768]{0:T(1024)} %copy-done.142) | copy-start | bytes 9220
  532.0 208.4 %reduce-scatter.20.cloned.1.call-start = ((), (), s32[]{:S(2)}) async-start(), calls=%async_computation.16 | async-start | bytes 10027008 | tf_op jit(solution)/shard_map/reduce_scatter | solution.py:345
  548.1 307.4 %reduce-scatter.24.cloned.1.call-start = ((), (), s32[]{:S(2)}) async-start(), calls=%async_computation.18 | async-start | bytes 10027008 | tf_op jit(solution)/shard_map/reduce_scatter | solution.py:346
  564.1 305.8 %reduce-scatter.18.cloned.1.call-start = ((), (), s32[]{:S(2)}) async-start(), calls=%async_computation.15 | async-start | bytes 221184 | tf_op jit(solution)/shard_map/reduce_scatter | solution.py:350
  605.4 14.8 %copy-start.212 = (f32[64]{0:T(128)S(1)}, f32[64]{0:T(128)}, u32[]{:S(2)}) copy-start(f32[64]{0:T(128)} %param.42) | copy-start | bytes 772
  605.4 16.8 %copy-start.211 = (f32[384,1]{0,1:T(1,128)S(1)}, f32[384,1]{0,1:T(1,128)}, u32[]{:S(2)}) copy-start(f32[384,1]{0,1:T(1,128)} %copy-done.210) | copy-start | bytes 4612
  612.1 420.0 %all-reduce.44.cloned.1.call-start = ((), (), s32[]{:S(2)}) async-start(), calls=%async_computation.20 | async-start | bytes 382976 | tf_op jit(solution)/shard_map/psum | solution.py:354
  612.2 11.6 copy-start.116
  625.7 538.1 %all-reduce.42.cloned.1.call-start = ((), (), s32[]{:S(2)}) async-start(), calls=%async_computation.13 | async-start | bytes 393216 | tf_op jit(solution)/shard_map/psum | solution.py:354
  629.4 551.8 %reduce-scatter.12.cloned.1.call-start = ((), (), s32[]{:S(2)}) async-start(), calls=%async_computation.11 | async-start | bytes 663552 | tf_op jit(solution)/shard_map/reduce_scatter | solution.py:349
  630.0 569.4 %reduce-scatter.22.cloned.1.call-start = ((), (), s32[]{:S(2)}) async-start(), calls=%async_computation.17 | async-start | bytes 884736 | tf_op jit(solution)/shard_map/reduce_scatter | solution.py:351
  740.4 477.0 %reduce-scatter.26.cloned.1.call-start = ((), (), s32[]{:S(2)}) async-start(), calls=%async_computation.19 | async-start | bytes 884736 | tf_op jit(solution)/shard_map/reduce_scatter | solution.py:352
  (207 other events, 989.6 us)
Sparse Core Ops, SparseCore 0:
  17.4 25.4 all-gather.1
  410.4 65.6 reduce-scatter.15
  478.5 33.7 reduce-scatter.13
  532.1 92.7 reduce-scatter.9
  629.5 110.8 reduce-scatter.19
  744.4 111.1 reduce-scatter.23
  858.4 10.2 reduce-scatter.17
  878.5 153.5 all-reduce.43
  1039.1 124.6 all-reduce.41
  1166.6 14.5 reduce-scatter.11
  1184.0 15.2 reduce-scatter.21
  1202.1 15.2 reduce-scatter.25
where the time goes:
time: 1260 us; the launch traced here: 1250 us
  waiting for transfers between devices  556 us (44%)
  matrix products  301 us (24%)
  other arithmetic  251 us (20%)
  local copies, waits for them, and re-layouts  125 us (10%)
  between operations  17.1 us (1%)
    psum x2, waiting for transfers between devices, on_device(): lax.psum((first_gain_grad, first_shift_grad, mixer_bias_grad, short_weigh...  294 us
    reduce_scatter x1, waiting for transfers between devices, on_device(): lax.psum_scatter(matrices[2], 'rows', scatter_dimension=0, tiled=True)  110 us
    reduce_scatter x1, waiting for transfers between devices, on_device(): lax.psum_scatter(matrices[3], 'rows', scatter_dimension=0, tiled=True)  97 us
    unnamed x545, local copies, waits for them, and re-layouts  84.8 us
    dot_general x2, matrix products, on_device(): jnp.einsum('rld,df->rlf', normed2_low, expand_weight, preferred_element_t...  55.8 us
    add_any x4, other arithmetic, spectral_product(): real = real_one * real_two - imag_one * imag_two  37.9 us
    another operation x5, other arithmetic  34.6 us
    dot_general x4, matrix products, on_device(): jnp.einsum('ml,rmd->rld', forward, trans_grad.astype(halves), preferred_e...  27.6 us
  transfers between devices with their start and end apart: 12, of which 7 were waited for; matrix products, arithmetic and copies ran while one was open for 29% of the time, Pallas kernels for 0%

commit v1 on v0

v1 whole, which is shorter than its diff:
```python
import functools
import math

import jax
import jax.numpy as jnp
import numpy as np
from jax import lax
from jax.experimental import pallas as pl
from jax.experimental.pallas import tpu as pltpu
from jax.sharding import PartitionSpec as P

f32 = jnp.float32
bf = jnp.bfloat16
HI = lax.Precision.HIGHEST
DOCS = 2
EPSILON = 1e-5
ROOT3 = math.sqrt(3.0) / 2
LANES = 128


def nt(a,b,precision=None): return lax.dot_general(a,b,(((1,),(1,)),((),())),precision=precision,preferred_element_type=f32)
def nn(a,b,precision=None): return lax.dot_general(a,b,(((1,),(0,)),((),())),precision=precision,preferred_element_type=f32)
def tn(a,b,precision=None): return lax.dot_general(a,b,(((0,),(0,)),((),())),precision=precision,preferred_element_type=f32)
def norm_stats(x):
    mean=jnp.mean(x,axis=-1,keepdims=True)
    c=x-mean
    var=jnp.mean(c*c,axis=-1,keepdims=True)
    rs=lax.rsqrt(var+EPSILON)
    return c*rs, rs
def sum0(v): return jnp.sum(v,axis=0,keepdims=True)

def radix_tables(length):
    n=length//3; m=2*length
    place=np.arange(n)
    def angle(freqs): return 2*np.pi*((freqs[:,None]*place[None,:])%m)/m
    half=angle(6*np.arange(n//2))
    sine=np.sin(half); sine[0]=np.cos(np.pi*place)
    t0=np.concatenate([np.cos(half),sine],0)
    odd=angle(6*np.arange(n//2)+3)
    t3=np.concatenate([np.cos(odd),np.sin(odd)],0)
    both=[]
    for k in (1,2):
        a=angle(6*np.arange(n)+k)
        c,s=np.cos(a),np.sin(a)
        both.append(np.block([[c,-s],[s,c]]))
    ts=[t0,t3,both[0],both[1]]
    low=lambda v: jnp.asarray(v.astype(np.float32)).astype(bf)
    return [low(t) for t in ts],[low(t.T) for t in ts]

def filter_inputs(length,emb,width):
    bands_count=(emb-1)//2
    places=np.arange(length,dtype=np.float32)
    tn_=places/np.float32(length-1)
    wave=places*np.float32(2.0*math.pi/length)
    bands=np.linspace(0.0001,bands_count-1,bands_count).astype(np.float32)
    phase=(wave[:,None]*bands[None,:]).astype(np.float32)
    z=np.concatenate([tn_[:,None],np.cos(phase),-np.sin(phase)],1).astype(np.float32)
    pad=(-emb)%8
    zt=np.concatenate([z.T,np.zeros((pad,length),np.float32)],0)
    rates=np.abs(np.linspace(math.log(0.01)/1.5,math.log(0.01)/0.3,width)).astype(np.float32)[None,:]
    return jnp.asarray(zt),jnp.asarray(rates)

def sin_cos(x):
    k=jnp.floor(x*(1.0/math.pi)+0.5)
    r=x-k*3.140625
    r=r-k*0.0009670257568359375
    r=r-k*6.2771141529083251953e-07
    odd=k-2.0*jnp.floor(k*0.5)
    sign=1.0-2.0*odd
    q=r*r
    s=1.0+q*(-1/6+q*(1/120+q*(-1/5040+q*(1/362880+q*(-1/39916800+q*(1/6227020800))))))
    c=1.0+q*(-1/2+q*(1/24+q*(-1/720+q*(1/40320+q*(-1/3628800+q*(1/479001600-q*(1/87178291200)))))))
    return r*s*sign, c*sign

def column(row):
    n=row.shape[1]
    i=lax.broadcasted_iota(jnp.int32,(n,n),0); j=lax.broadcasted_iota(jnp.int32,(n,n),1)
    return jnp.sum(jnp.where(i==j,row,0.0),axis=1,keepdims=True)

def spread(x0,x1,x2):
    s=x1+x2; d=x1-x2
    y0=(x0+s).astype(bf); y3=(x0-d).astype(bf)
    y1=jnp.concatenate([(x0+0.5*d).astype(bf),(ROOT3*s).astype(bf)],0)
    y2=jnp.concatenate([(x0-0.5*s).astype(bf),(ROOT3*d).astype(bf)],0)
    return y0,y3,y1,y2
def gather(v0,v3,v1,v2):
    n=v0.shape[0]
    v1r,v1i,v2r,v2i=v1[:n],v1[n:],v2[:n],v2[n:]
    even=v0+v3
    a=0.5*(v1r-v2r); b=ROOT3*(v1i+v2i)
    x0=even+v1r+v2r
    x1=(v0-v3)+a+b
    x2=even-0.5*(v1r+v2r)+ROOT3*(v1i-v2i)
    return x0,x1,x2

def fwd_kernel(rows_here,tok_ref,mask_ref,g1_ref,s1_ref,wg_ref,wi_ref,wv_ref,bg_ref,bi_ref,bv_ref,
        swg_ref,swi_ref,swv_ref,sbg_ref,sbi_ref,sbv_ref,skip_ref,
        zt_ref,ew_ref,eb_ref,eo_ref,iw_ref,ib_ref,io_ref,ow_ref,ob_ref,oo_ref,fw_ref,rate_ref,
        t0,t3,t1,t2,u0,u3,u1,u2,
        proj_ref,mixed_ref,long_ref,mix_ref,trans_ref,spec_ref,state_ref,nt_ref,
        n_s,e_s):
    c=pl.program_id(0)
    L=tok_ref.shape[0]//rows_here
    N=L//3
    @pl.when(c==0)
    def _():
        TT=256
        def body(i,k):
            rows=pl.ds(pl.multiple_of(i*TT,TT),TT)
            xh,_=norm_stats(tok_ref[rows,:].astype(f32))
            n_s[rows,:]=(xh*g1_ref[...]+s1_ref[...]).astype(bf)
            return k
        lax.fori_loop(0,tok_ref.shape[0]//TT,body,0)
        for i in range(tok_ref.shape[0]//TT):
            nt_ref[:,i*TT:(i+1)*TT]=n_s[i*TT:(i+1)*TT,:].T
        e_s[...]=jnp.zeros_like(e_s)
        e_s[0:ew_ref.shape[0],:]=ew_ref[...]
        pre=tn(e_s[...],zt_ref[...],HI)+column(eb_ref[...])
        e1,c1=sin_cos(column(eo_ref[...])*pre)
        state_ref[0]=e1; state_ref[1]=c1; state_ref[2]=pre
        pre=tn(iw_ref[...],e1,HI)+column(ib_ref[...])
        e2,c2=sin_cos(column(io_ref[...])*pre)
        state_ref[3]=e2; state_ref[4]=c2; state_ref[5]=pre
        pre=tn(ow_ref[...],e2,HI)+column(ob_ref[...])
        e3,c3=sin_cos(column(oo_ref[...])*pre)
        state_ref[6]=e3; state_ref[7]=c3; state_ref[8]=pre
    tnorm=lax.broadcasted_iota(jnp.int32,(L,fw_ref.shape[1]),0).astype(f32)*(1.0/(L-1))
    kern=tn(state_ref[6],fw_ref[...],HI)*jnp.exp(-tnorm*rate_ref[...])
    k=kern.astype(bf).astype(f32)
    y0,y3,y1,y2=spread(k[0:N],k[N:2*N],k[2*N:])
    first=lax.broadcasted_iota(jnp.int32,(N//2,fw_ref.shape[1]),0)==0
    half=jnp.where(first,0.5,1.0)
    q0=nn(t0[...],y0); q3=nn(t3[...],y3); q1=nn(t1[...],y1); q2=nn(t2[...],y2)
    H=N//2
    spec_ref[0:H]=q0[0:H]*half
    spec_ref[H:N]=jnp.where(first,0.0,q0[H:])
    spec_ref[6*N:6*N+H]=jnp.where(first,0.5*q0[H:],q0[0:H])
    spec_ref[N:2*N]=q3
    spec_ref[2*N:4*N]=q1
    spec_ref[4*N:6*N]=q2
    def one_row(r,carry):
        rows=pl.ds(pl.multiple_of(r*L,L),L)
        n=n_s[rows,:]
        m0=mask_ref[rows,0:1]; same1=mask_ref[rows,1:2]; same2=mask_ref[rows,2:3]
        m1=1.0-m0
        mixed=[]
        for i,(w,b,sw,sb) in enumerate(((wg_ref,bg_ref,swg_ref,sbg_ref),(wi_ref,bi_ref,swi_ref,sbi_ref),(wv_ref,bv_ref,swv_ref,sbv_ref))):
            p=nn(n,w[...])+b[...]
            proj_ref[i,rows,:]=p.astype(bf)
            m=sb[...]+sw[0:1,:]*p+sw[1:2,:]*(pltpu.roll(p,1,0)*same1)+sw[2:3,:]*(pltpu.roll(p,2,0)*same2)
            mixed_ref[i,rows,:]=m.astype(bf)
            mixed.append(m)
        inner=mixed[2]*mixed[1]
        low=inner.astype(bf).astype(f32)
        xa=low*m0
        conv=None
        for d,(m,x) in enumerate(((m0,xa),(m1,low-xa))):
            y0,y3,y1,y2=spread(x[0:N],x[N:2*N],x[2*N:])
            parts=[]
            for (t,u,y,off,n2) in ((t0,u0,y0,0,H),(t3,u3,y3,N,H),(t1,u1,y1,2*N,N),(t2,u2,y2,4*N,N)):
                p=nn(t[...],y)
                trans_ref[r,d,off:off+2*n2,:]=p.astype(bf)
                pa=p[:n2]; pb=p[n2:]
                qa=spec_ref[off:off+n2]; qb=spec_ref[off+n2:off+2*n2]
                qc=spec_ref[6*N:6*N+n2] if off==0 else qa
                ra=(pa*qa-pb*qb).astype(bf); rb=(pa*qb+pb*qc).astype(bf)
                parts.append(nn(u[...],jnp.concatenate([ra,rb],0)))
            y=jnp.concatenate(gather(*parts),0)
            conv=m*y if conv is None else conv+m*y
        longconv=conv*(2.0/(2*L))+skip_ref[...]*inner
        long_ref[rows,:]=longconv.astype(bf)
        mix_ref[rows,:]=(mixed[0]*longconv).astype(bf)
        return carry
    lax.fori_loop(0,rows_here,one_row,0)

def forward_mixer(tok,mask,g1,s1,wm,mb,sw,sb,skip,filt,zt,rates,tabs,tabst,rows_here,CH=256):
    T,D=tok.shape; L=T//rows_here; N=L//3; J=D//CH
    ew,eb,eo,iw,ib,io,ow,ob,oo,fw=filt
    full=lambda a: pl.BlockSpec(a.shape,lambda j:(0,)*a.ndim,pipeline_mode=pl.Buffered(1))
    col=lambda r,k: pl.BlockSpec((r,CH),lambda j,k=k:(0,k*J+j))
    sds=jax.ShapeDtypeStruct
    F=ew.shape[1]
    ins=[tok,mask,g1,s1,wm,wm,wm,mb,mb,mb,sw,sw,sw,sb,sb,sb,skip,zt,ew,eb,eo,iw,ib,io,ow,ob,oo,fw,rates]+tabs+tabst
    specs=[full(tok),full(mask),full(g1),full(s1)]+[col(D,k) for k in range(3)]+[col(1,k) for k in range(3)]+[col(3,k) for k in range(3)]+[col(1,k) for k in range(3)]+[col(1,0)]
    specs+=[full(a) for a in (zt,ew,eb,eo,iw,ib,io,ow,ob,oo)]+[col(F,0),col(1,0)]+[full(a) for a in tabs+tabst]
    return pl.pallas_call(functools.partial(fwd_kernel,rows_here),grid=(J,),in_specs=specs,
      out_specs=[pl.BlockSpec((3,T,CH),lambda j:(0,0,j)),pl.BlockSpec((3,T,CH),lambda j:(0,0,j)),col(T,0),col(T,0),
        pl.BlockSpec((rows_here,DOCS,2*L,CH),lambda j:(0,0,0,j)),col(2*L+N//2,0),pl.BlockSpec((9,F,L),lambda j:(0,0,0)),pl.BlockSpec((D,T),lambda j:(0,0))],
      out_shape=[sds((3,T,D),bf),sds((3,T,D),bf),sds((T,D),bf),sds((T,D),bf),sds((rows_here,DOCS,2*L,D),bf),sds((2*L+N//2,D),f32),sds((9,F,L),f32),sds((D,T),bf)],
      scratch_shapes=[pltpu.VMEM((T,D),bf),pltpu.VMEM((zt.shape[0],F),f32)],
      compiler_params=pltpu.CompilerParams(vmem_limit_bytes=62*2**20),
      cost_estimate=pl.CostEstimate(flops=10*T*D*D+T*D*6000,bytes_accessed=40*2**20,transcendentals=L*D),name="mixer_forward")(*ins)

def bwd_kernel(rows_here,dat_ref,tok_ref,mask_ref,g1_ref,wo_ref,long_ref,mixed_ref,proj_ref,trans_ref,spec_ref,nt_ref,
        wg_ref,wi_ref,wv_ref,swg_ref,swi_ref,swv_ref,skip_ref,
        state_ref,zt_ref,iw_ref,ow_ref,eo_ref,io_ref,oo_ref,fw_ref,rate_ref,
        t0,t3,t1,t2,u0,u3,u1,u2,
        tg_ref,wgrad_ref,sg_ref,vec_ref,gew_ref,giw_ref,gow_ref,gfw_ref,gsm_ref,
        dn,de3,dp_s,ds_s):
    c=pl.program_id(0); J=pl.num_programs(0)
    T=tok_ref.shape[0]; L=T//rows_here; N=L//3; H=N//2; CH=long_ref.shape[1]
    @pl.when(c==0)
    def _():
        dn[...]=jnp.zeros_like(dn); de3[...]=jnp.zeros_like(de3)
    ds_s[...]=jnp.zeros_like(ds_s); sg_ref[...]=jnp.zeros_like(sg_ref)
    def add(off,v): ds_s[off:off+v.shape[0],:]+=v
    def one_row(r,carry):
        rows=pl.ds(pl.multiple_of(r*L,L),L)
        m0=mask_ref[rows,0:1]; same1=mask_ref[rows,1:2]; same2=mask_ref[rows,2:3]
        m1=1.0-m0
        dm=nt(dat_ref[rows,:],wo_ref[...])
        gate_out=mixed_ref[0,rows,:].astype(f32); gate_in=mixed_ref[1,rows,:].astype(f32); value=mixed_ref[2,rows,:].astype(f32)
        d_go=dm*long_ref[rows,:].astype(f32)
        d_long=dm*gate_out
        sg_ref[0,5:6,:]+=sum0(d_long*(value*gate_in))
        xa=d_long*m0
        d_conv=None
        for d,(m,x) in enumerate(((m0,xa),(m1,d_long-xa))):
            y0,y3,y1,y2=spread(x[0:N],x[N:2*N],x[2*N:])
            parts=[]
            for s,(t,u,y,off,n2) in enumerate(((t0,u0,y0,0,H),(t3,u3,y3,N,H),(t1,u1,y1,2*N,N),(t2,u2,y2,4*N,N))):
                g=nn(t[...],y)
                ga=g[:n2]; gb=g[n2:]
                qa=spec_ref[off:off+n2]; qb=spec_ref[off+n2:off+2*n2]
                qc=spec_ref[6*N:6*N+n2] if off==0 else qa
                pa=trans_ref[r,d,off:off+n2,:].astype(f32); pb=trans_ref[r,d,off+n2:off+2*n2,:].astype(f32)
                da=(ga*qa+gb*qb).astype(bf); db=(gb*qc-ga*qb).astype(bf)
                if s==0:
                    add(0,ga*pa); add(6*N,gb*pb)
                else:
                    add(off,ga*pa+gb*pb)
                add(off+n2,gb*pa-ga*pb)
                parts.append(nn(u[...],jnp.concatenate([da,db],0)))
            y=jnp.concatenate(gather(*parts),0)
            d_conv=m*y if d_conv is None else d_conv+m*y
        d_inner=skip_ref[...]*d_long+d_conv*(2.0/(2*L))
        for i,(dmx,w,sw) in enumerate(((d_go,wg_ref,swg_ref),(d_inner*value,wi_ref,swi_ref),(d_inner*gate_in,wv_ref,swv_ref))):
            a1=pltpu.roll(dmx*same1,L-1,0); a2=pltpu.roll(dmx*same2,L-2,0)
            dp=(sw[0:1,:]*dmx+sw[1:2,:]*a1+sw[2:3,:]*a2).astype(bf)
            p=proj_ref[i,rows,:].astype(f32)
            for k,v in enumerate((p*dmx,p*a1,p*a2,dmx,dp.astype(f32))):
                sg_ref[i,k:k+1,:]+=sum0(v)
            dp_s[i,rows,:]=dp
            dn[rows,:]+=nt(dp,w[...])
        return carry
    lax.fori_loop(0,rows_here,one_row,0)
    for i in range(3):
        part=nn(nt_ref[...],dp_s[i]).astype(bf)
        for h in range(CH//LANES): wgrad_ref[i,h]=part[:,h*LANES:(h+1)*LANES]
    first=lax.broadcasted_iota(jnp.int32,(H,CH),0)==0
    half=jnp.where(first,0.5,1.0)
    d8=ds_s[6*N:6*N+H]
    z0=half*(ds_s[0:H]+jnp.where(first,0.0,d8))
    z1=jnp.where(first,0.5*d8,ds_s[H:N])
    scale=2.0/(2*L)
    low=lambda a: (a*scale).astype(bf)
    parts=[nn(u0[...],low(jnp.concatenate([z0,z1],0))),nn(u3[...],low(ds_s[N:2*N])),nn(u1[...],low(ds_s[2*N:4*N])),nn(u2[...],low(ds_s[4*N:6*N]))]
    tnorm=lax.broadcasted_iota(jnp.int32,(L,CH),0).astype(f32)*(1.0/(L-1))
    gk=jnp.concatenate(gather(*parts),0)*jnp.exp(-tnorm*rate_ref[...])
    gfw_ref[...]=nn(state_ref[6],gk,HI)
    de3[...]+=nt(fw_ref[...],gk,HI)
    @pl.when(c==J-1)
    def _():
        TT=256
        def body(i,k):
            rows=pl.ds(pl.multiple_of(i*TT,TT),TT)
            xh,rs=norm_stats(tok_ref[rows,:].astype(f32))
            d=dn[rows,:]
            gd=d*g1_ref[...]
            a=jnp.mean(gd,axis=-1,keepdims=True); b=jnp.mean(gd*xh,axis=-1,keepdims=True)
            tg_ref[rows,:]=(dat_ref[rows,:].astype(f32)+rs*(gd-a-xh*b)).astype(bf)
            return (k[0]+sum0(d*xh),k[1]+sum0(d))
        z=jnp.zeros((1,tok_ref.shape[1]),f32)
        a,b=lax.fori_loop(0,T//TT,body,(z,z))
        vec_ref[pl.ds(0,1),:]=a; vec_ref[pl.ds(1,1),:]=b
        ones=jnp.ones((8,L),f32)
        flat=lambda v: nt(ones,v,HI)
        g=de3[...]*state_ref[7]
        gsm_ref[0]=flat(g*state_ref[8])
        g=g*column(oo_ref[...])
        gsm_ref[1]=flat(g)
        gow_ref[...]=nt(state_ref[3],g,HI)
        g=nn(ow_ref[...],g,HI)*state_ref[4]
        gsm_ref[2]=flat(g*state_ref[5])
        g=g*column(io_ref[...])
        gsm_ref[3]=flat(g)
        giw_ref[...]=nt(state_ref[0],g,HI)
        g=nn(iw_ref[...],g,HI)*state_ref[1]
        gsm_ref[4]=flat(g*state_ref[2])
        g=g*column(eo_ref[...])
        gsm_ref[5]=flat(g)
        gew_ref[...]=nt(zt_ref[...],g,HI)

def backward_mixer(dat,tok,mask,g1,wo,longc,mixed,proj,trans,spec,ntr,wm,sw,skip,state,filt,zt,rates,tabs,tabst,rows_here,CH=256):
    T,D=tok.shape; L=T//rows_here; N=L//3; J=D//CH
    ew,eb,eo,iw,ib,io,ow,ob,oo,fw=filt
    F=ew.shape[1]; sds=jax.ShapeDtypeStruct
    full=lambda a: pl.BlockSpec(a.shape,lambda j:(0,)*a.ndim,pipeline_mode=pl.Buffered(1))
    col=lambda r,k: pl.BlockSpec((r,CH),lambda j,k=k:(0,k*J+j))
    cube=lambda a: pl.BlockSpec(a.shape[:-1]+(CH,),lambda j:(0,)*(a.ndim-1)+(j,))
    one=lambda *s: pl.BlockSpec(s,lambda j:(0,)*len(s))
    ins=[dat,tok,mask,g1,wo,longc,mixed,proj,trans,spec,ntr,wm,wm,wm,sw,sw,sw,skip,state,zt,iw,ow,eo,io,oo,fw,rates]+tabs+tabst
    specs=[full(dat),full(tok),full(mask),full(g1),pl.BlockSpec((CH,D),lambda j:(j,0)),col(T,0),cube(mixed),cube(proj),cube(trans),cube(spec),full(ntr)]
    specs+=[col(D,k) for k in range(3)]+[col(3,k) for k in range(3)]+[col(1,0)]
    specs+=[full(a) for a in (state,zt,iw,ow,eo,io,oo)]+[col(F,0),col(1,0)]+[full(a) for a in tabs+tabst]
    return pl.pallas_call(functools.partial(bwd_kernel,rows_here),grid=(J,),in_specs=specs,
      out_specs=[one(T,D),pl.BlockSpec((3,CH//LANES,D,LANES),lambda j:(0,j,0,0)),pl.BlockSpec((3,8,CH),lambda j:(0,0,j)),one(8,D),one(zt.shape[0],F),one(F,F),one(F,F),col(F,0),one(6,8,F)],
      out_shape=[sds((T,D),bf),sds((3,D//LANES,D,LANES),bf),sds((3,8,D),f32),sds((8,D),f32),sds((zt.shape[0],F),f32),sds((F,F),f32),sds((F,F),f32),sds((F,D),f32),sds((6,8,F),f32)],
      scratch_shapes=[pltpu.VMEM((T,D),f32),pltpu.VMEM((F,L),f32),pltpu.VMEM((3,T,CH),bf),pltpu.VMEM((6*N+N//2,CH),f32)],
      compiler_params=pltpu.CompilerParams(vmem_limit_bytes=62*2**20),
      cost_estimate=pl.CostEstimate(flops=16*T*D*D+T*D*7000,bytes_accessed=50*2**20,transcendentals=L*D),name="mixer_backward")(*ins)


def gelu_parts(e):
    u=jnp.abs(e)
    d=1.0+(0.3275911/math.sqrt(2))*u
    t=pl.reciprocal(d,approx=True)
    t=t*(2.0-d*t)
    ex=jnp.exp(e*e*(-0.5))
    poly=t*(0.5*0.254829592+t*(0.5*-0.284496736+t*(0.5*1.421413741+t*(0.5*-1.453152027+t*(0.5*1.061405429)))))
    q=poly*ex
    phi=jnp.where(e>=0,1.0-q,q)
    return phi, phi+e*ex*(1/math.sqrt(2*math.pi))
def mlp_kernel(FC,TT,mix_ref,tok_ref,cot_ref,wo_ref,bo_ref,g2_ref,s2_ref,we_ref,be_ref,wr_ref,br_ref,
           out_ref,dat_ref,wog_ref,weg_ref,wrg_ref,beg_ref,vec_ref,
           hid,acc,dn2,n2,n2t,cott,act,de):
    j=pl.program_id(0); J=pl.num_programs(0)
    T=tok_ref.shape[0]; D=tok_ref.shape[1]
    nt_tiles=T//TT
    @pl.when(j==0)
    def _():
        def body(i,c):
            rows=pl.ds(pl.multiple_of(i*TT,TT),TT)
            h=tok_ref[rows,:].astype(f32)+nn(mix_ref[rows,:],wo_ref[...])+bo_ref[...]
            hid[rows,:]=h
            xh,rs=norm_stats(h)
            n=(xh*g2_ref[...]+s2_ref[...]).astype(bf)
            n2[rows,:]=n
            acc[rows,:]=h+br_ref[...]
            dn2[rows,:]=jnp.zeros((TT,D),f32)
            return c
        lax.fori_loop(0,nt_tiles,body,0)
        for i in range(nt_tiles):
            rows=pl.ds(i*TT,TT)
            n2t[:,rows]=n2[rows,:].T
            cott[:,rows]=cot_ref[rows,:].T
    def tile(i,c):
        rows=pl.ds(pl.multiple_of(i*TT,TT),TT)
        e=nn(n2[rows,:],we_ref[...])+be_ref[...]
        da=nt(cot_ref[rows,:],wr_ref[...])
        phi,dphi=gelu_parts(e)
        a=(e*phi).astype(bf)
        dd=(da*dphi).astype(bf)
        act[rows,:]=a
        de[rows,:]=dd
        acc[rows,:]+=nn(a,wr_ref[...])
        dn2[rows,:]+=nt(dd,we_ref[...])
        return c+jnp.sum(dd.astype(f32),axis=0,keepdims=True)
    beg_ref[...]=lax.fori_loop(0,nt_tiles,tile,jnp.zeros((1,FC),f32))
    def grads(i,c):
        rows=pl.ds(pl.multiple_of(i*256,256),256)
        back=nn(cott[rows,:],act[...]).astype(bf).T
        for h in range(256//LANES): wrg_ref[i*(256//LANES)+h]=back[:,h*LANES:(h+1)*LANES]
        ahead=nn(n2t[rows,:],de[...]).astype(bf)
        for h in range(FC//LANES): weg_ref[h,rows,:]=ahead[:,h*LANES:(h+1)*LANES]
        return c
    lax.fori_loop(0,D//256,grads,0)
    @pl.when(j==J-1)
    def _():
        def body(i,c):
            rows=pl.ds(pl.multiple_of(i*TT,TT),TT)
            out_ref[rows,:]=acc[rows,:].astype(bf)
            xh,rs=norm_stats(hid[rows,:])
            dn=dn2[rows,:]
            gd=dn*g2_ref[...]
            m1=jnp.mean(gd,axis=-1,keepdims=True)
            m2=jnp.mean(gd*xh,axis=-1,keepdims=True)
            cot=cot_ref[rows,:].astype(f32)
            dh=cot+rs*(gd-m1-xh*m2)
            dl=dh.astype(bf)
            dat_ref[rows,:]=dl
            dlf=dl.astype(f32)
            s=lambda v: jnp.sum(v,axis=0,keepdims=True)
            return (c[0]+s(dn*xh),c[1]+s(dn),c[2]+s(dlf),c[3]+s(cot))
        z=jnp.zeros((1,D),f32)
        r=lax.fori_loop(0,nt_tiles,body,(z,z,z,z))
        for k in range(4): vec_ref[pl.ds(k,1),:]=r[k]
        for i in range(nt_tiles):
            rows=pl.ds(i*TT,TT)
            n2t[:,rows]=mix_ref[rows,:].T
        def og(i,c):
            rows=pl.ds(pl.multiple_of(i*256,256),256)
            part=nn(n2t[rows,:],dat_ref[...]).astype(bf)
            for h in range(D//LANES): wog_ref[h,rows,:]=part[:,h*LANES:(h+1)*LANES]
            return c
        lax.fori_loop(0,D//256,og,0)
def mlp(mix,tok,cot,wo,bo,g2,s2,we,be,wr,br,FC=1024,TT=512):
    T,D=tok.shape; FF=we.shape[1]; J=FF//FC
    full=lambda a: pl.BlockSpec(a.shape,lambda j:(0,0),pipeline_mode=pl.Buffered(1))
    one=lambda r,c: pl.BlockSpec((r,c),lambda j:(0,0))
    return pl.pallas_call(functools.partial(mlp_kernel,FC,TT),grid=(J,),
      in_specs=[full(mix),full(tok),full(cot),full(wo),full(bo),full(g2),full(s2),
        pl.BlockSpec((D,FC),lambda j:(0,j)),pl.BlockSpec((1,FC),lambda j:(0,j)),pl.BlockSpec((FC,D),lambda j:(j,0)),full(br)],
      out_specs=[one(T,D),one(T,D),pl.BlockSpec((D//LANES,D,LANES),lambda j:(0,0,0)),pl.BlockSpec((FC//LANES,D,LANES),lambda j:(j,0,0)),pl.BlockSpec((D//LANES,FC,LANES),lambda j:(0,j,0)),pl.BlockSpec((1,FC),lambda j:(0,j)),one(8,D)],
      out_shape=[jax.ShapeDtypeStruct((T,D),bf),jax.ShapeDtypeStruct((T,D),bf),jax.ShapeDtypeStruct((D//LANES,D,LANES),bf),
        jax.ShapeDtypeStruct((FF//LANES,D,LANES),bf),jax.ShapeDtypeStruct((D//LANES,FF,LANES),bf),jax.ShapeDtypeStruct((1,FF),f32),jax.ShapeDtypeStruct((8,D),f32)],
      scratch_shapes=[pltpu.VMEM((T,D),f32),pltpu.VMEM((T,D),f32),pltpu.VMEM((T,D),f32),pltpu.VMEM((T,D),bf),
        pltpu.VMEM((D,T),bf),pltpu.VMEM((D,T),bf),pltpu.VMEM((T,FC),bf),pltpu.VMEM((T,FC),bf)],
      compiler_params=pltpu.CompilerParams(vmem_limit_bytes=62*2**20),
      cost_estimate=pl.CostEstimate(flops=54*T*D*FF//4,bytes_accessed=40*2**20,transcendentals=T*FF),
      name="mlp")(mix,tok,cot,wo,bo,g2,s2,we,be,wr,br)


ROWS_WIDE = 384


def pack_plan(width, hidden, emb, ff, filt_rows):
    return None


def reduce_kernel(sizes, pieces, *refs):
    count = len(pieces)
    ins = refs[:count]
    out_ref, pk, rbuf, red, gath, ss1, rs1, ss2, rs2 = refs[count:]
    rows_n, pos_n = sizes
    n = rows_n * pos_n
    total = pk.shape[0]
    chunk = total // n
    me = lax.axis_index("rows") * pos_n + lax.axis_index("pos") if pos_n > 1 else lax.axis_index("rows")

    def ident(t):
        if pos_n > 1:
            return {"rows": t // pos_n, "pos": t % pos_n}
        return {"rows": t}

    barrier = pltpu.get_barrier_semaphore()

    def greet(k, carry):
        t = lax.rem(me + k, n)
        pl.semaphore_signal(barrier, inc=1, device_id=ident(t), device_id_type=pl.DeviceIdType.MESH)
        return carry

    lax.fori_loop(1, n, greet, 0)
    pk[...] = jnp.zeros_like(pk)
    for ref, place in zip(ins, pieces):
        place(ref, pk)
    pl.semaphore_wait(barrier, n - 1)

    def part(t):
        return pl.ds(pl.multiple_of(t * chunk, chunk), chunk)

    def scatter(t, src_t, slot):
        return pltpu.make_async_remote_copy(
            src_ref=pk.at[part(src_t), :], dst_ref=rbuf.at[slot], send_sem=ss1.at[src_t],
            recv_sem=rs1.at[slot], device_id=ident(t), device_id_type=pl.DeviceIdType.MESH)

    def send1(k, carry):
        t = lax.rem(me + k, n)
        scatter(t, t, me).start()
        return carry

    lax.fori_loop(1, n, send1, 0)
    rbuf[me] = pk[part(me), :]

    def wait1(k, carry):
        t = lax.rem(me + k, n)
        scatter(t, t, t).wait()
        return carry

    lax.fori_loop(1, n, wait1, 0)
    acc = rbuf[0]
    for s in range(1, n):
        acc = acc + rbuf[s]
    red[...] = acc
    gath[part(me), :] = acc

    def spread_copy(t, slot):
        return pltpu.make_async_remote_copy(
            src_ref=red, dst_ref=gath.at[part(slot), :], send_sem=ss2.at[t],
            recv_sem=rs2.at[slot], device_id=ident(t), device_id_type=pl.DeviceIdType.MESH)

    def send2(k, carry):
        t = lax.rem(me + k, n)
        spread_copy(t, me).start()
        return carry

    lax.fori_loop(1, n, send2, 0)

    def wait2(k, carry):
        t = lax.rem(me + k, n)
        spread_copy(t, t).wait()
        return carry

    lax.fori_loop(1, n, wait2, 0)
    out_ref[...] = gath[...]


def layout_of(width, hidden, emb, ff):
    per = width // ROWS_WIDE
    at = {}
    row = 0
    at["filter"] = row
    row += hidden * per
    at["square"] = row
    row += hidden
    for name, vectors in (("vec1", 2), ("vec2", 4), ("sgrad", 3 * 5), ("skip", 1), ("ebias", ff // width)):
        at[name] = row
        row += vectors * per
    at["small"] = row
    row += 6
    return at, row


def all_reduce_small(sizes, beg, vec2, sgrad, vec1, gew, giw, gow, gfw, gsm):
    width = vec1.shape[1]
    hidden = giw.shape[0]
    per = width // ROWS_WIDE
    at, used = layout_of(width, hidden, gew.shape[0], beg.shape[1])
    n = sizes[0] * sizes[1]
    total = -(-used // (8 * n)) * 8 * n

    def put(pk, row, value):
        for h in range(per):
            pk[row + h:row + h + 1, :] = value[:, h * ROWS_WIDE:(h + 1) * ROWS_WIDE]

    def p_beg(ref, pk):
        for k in range(ref.shape[1] // width):
            put(pk, at["ebias"] + k * per, ref[:, k * width:(k + 1) * width])

    def p_vec2(ref, pk):
        for k in range(4):
            put(pk, at["vec2"] + k * per, ref[k:k + 1, :])

    def p_sg(ref, pk):
        for i in range(3):
            for k in range(5):
                put(pk, at["sgrad"] + (i * 5 + k) * per, ref[i, k:k + 1, :])
        put(pk, at["skip"], ref[0, 5:6, :])

    def p_vec1(ref, pk):
        for k in range(2):
            put(pk, at["vec1"] + k * per, ref[k:k + 1, :])

    def square(lane):
        def place(ref, pk):
            r = min(ref.shape[0], hidden)
            pk[at["square"]:at["square"] + r, lane:lane + hidden] = ref[0:r, :]
        return place

    def p_fw(ref, pk):
        for h in range(per):
            pk[at["filter"] + h * hidden:at["filter"] + (h + 1) * hidden, :] = ref[:, h * ROWS_WIDE:(h + 1) * ROWS_WIDE]

    def p_small(ref, pk):
        for k in range(6):
            pk[at["small"] + k:at["small"] + k + 1, 0:hidden] = ref[k, 0:1, :]

    places = (p_beg, p_vec2, p_sg, p_vec1, square(0), square(128), square(256), p_fw, p_small)
    args = (beg, vec2, sgrad, vec1, gew, giw, gow, gfw, gsm)
    vm = pl.BlockSpec(memory_space=pltpu.VMEM)
    chunk = total // n
    return pl.pallas_call(
        functools.partial(reduce_kernel, sizes, places),
        out_shape=jax.ShapeDtypeStruct((total, ROWS_WIDE), f32),
        in_specs=[vm] * len(args), out_specs=vm,
        scratch_shapes=[pltpu.VMEM((total, ROWS_WIDE), f32), pltpu.VMEM((n, chunk, ROWS_WIDE), f32),
            pltpu.VMEM((chunk, ROWS_WIDE), f32), pltpu.VMEM((total, ROWS_WIDE), f32)]
            + [pltpu.SemaphoreType.DMA((n,))] * 4,
        compiler_params=pltpu.CompilerParams(collective_id=0, has_side_effects=True, vmem_limit_bytes=32 * 2**20),
        name="sum_small")(*args)


def unpack_small(packed, width, hidden, emb, ff):
    per = width // ROWS_WIDE
    at, _ = layout_of(width, hidden, emb, ff)

    def kernel(pk, *outs):
        (fg, fs, mb, sw, sb, ew, eb, eo, iw, ib, io, ow, ob, oo, fw, sk, obias, sg, ss, eb2, rb) = outs

        def get(ref, r, lane, row):
            for h in range(per):
                ref[r:r + 1, lane + h * ROWS_WIDE:lane + (h + 1) * ROWS_WIDE] = pk[row + h:row + h + 1, :]

        get(fg, 0, 0, at["vec1"]); get(fs, 0, 0, at["vec1"] + per)
        for i in range(3):
            base = at["sgrad"] + i * 5 * per
            for k in range(3):
                get(sw, k, i * width, base + k * per)
            get(sb, 0, i * width, base + 3 * per)
            get(mb, 0, i * width, base + 4 * per)
        q = at["square"]
        ew[...] = pk[q:q + emb, 0:hidden]
        iw[...] = pk[q:q + hidden, 128:128 + hidden]
        ow[...] = pk[q:q + hidden, 256:256 + hidden]
        for k, ref in enumerate((oo, ob, io, ib, eo, eb)):
            ref[...] = pk[at["small"] + k:at["small"] + k + 1, 0:hidden]
        for h in range(per):
            fw[:, h * ROWS_WIDE:(h + 1) * ROWS_WIDE] = pk[at["filter"] + h * hidden:at["filter"] + (h + 1) * hidden, :]
        get(sk, 0, 0, at["skip"])
        for k, ref in enumerate((sg, ss, obias, rb)):
            get(ref, 0, 0, at["vec2"] + k * per)
        for k in range(ff // width):
            get(eb2, 0, k * width, at["ebias"] + k * per)

    s = lambda *d: jax.ShapeDtypeStruct(d, f32)
    shapes = [s(1, width), s(1, width), s(1, 3 * width), s(3, 3 * width), s(1, 3 * width), s(emb, hidden), s(1, hidden), s(1, hidden),
        s(hidden, hidden), s(1, hidden), s(1, hidden), s(hidden, hidden), s(1, hidden), s(1, hidden), s(hidden, width),
        s(1, width), s(1, width), s(1, width), s(1, width), s(1, ff), s(1, width)]
    vm = pl.BlockSpec(memory_space=pltpu.VMEM)
    return pl.pallas_call(kernel, out_shape=shapes, in_specs=[vm], out_specs=[vm] * len(shapes), name="unpack_small")(packed)


def bits_of(n):
    return n.bit_length() - 1


def scatter_blocks(grad, rows_n, pos_n, order):
    blocks, height, wide = grad.shape
    if blocks % pos_n:
        flat = grad.transpose(1, 0, 2).reshape(height, blocks * wide)
        wide = blocks * wide // pos_n
        blocks = pos_n
        grad = flat.reshape(height, blocks, wide).transpose(1, 0, 2)
    high = height // rows_n
    rbits, pbits = bits_of(rows_n), bits_of(pos_n)
    acc = grad.reshape((2,) * pbits + (blocks // pos_n,) + (2,) * rbits + (high, wide))
    alive = [("pos", b) for b in reversed(range(pbits))] + [None] + [("rows", b) for b in reversed(range(rbits))]
    stages = [s for s in order(rbits, pbits)]
    for count, (axis, bit) in enumerate(stages):
        dim = alive.index((axis, bit))
        mine = (lax.axis_index(axis) >> bit) & 1
        size = rows_n if axis == "rows" else pos_n
        send = lax.dynamic_index_in_dim(acc, 1 - mine, dim, keepdims=False)
        keep = lax.dynamic_index_in_dim(acc, mine, dim, keepdims=False)
        got = lax.ppermute(send, axis, [(i, i ^ (1 << bit)) for i in range(size)])
        acc = keep.astype(f32) + got.astype(f32)
        if count < len(stages) - 1:
            acc = acc.astype(bf)
        alive.pop(dim)
    acc = acc.astype(f32)
    return acc.transpose(1, 0, 2).reshape(high, -1)


def order_a(rbits, pbits):
    rest = [("rows", b) for b in range(1, rbits)]
    return [("rows", 0)] + [("pos", b) for b in range(pbits)] + rest


def order_b(rbits, pbits):
    rest = [("rows", b) for b in range(2, rbits)]
    return [("rows", 0), ("rows", 1)] + [("pos", b) for b in range(pbits)] + rest


def lag_columns(segments):
    earlier = lambda k: jnp.pad(segments, ((0, 0), (k, 0)), constant_values=-1)[:, :-k] == segments
    first = segments == 0
    stack = jnp.stack([first, earlier(1), earlier(2)] + [first] * 5, axis=-1)
    return stack.astype(f32).reshape(-1, 8)


def on_device(sizes, tokens, segments, cotangent, first_gain, first_shift, mixer_weight, mixer_bias, short_weight, short_bias,
        embed_weight, embed_bias, embed_omega, inner_weight, inner_bias, inner_omega, outer_weight, outer_bias, outer_omega,
        filter_weight, skip_gain, output_weight, output_bias, second_gain, second_shift, expand_weight, expand_bias,
        reduce_weight, reduce_bias):
    rows_n, pos_n = sizes
    rows_here, length, width = tokens.shape
    emb, hidden = embed_weight.shape
    ff = expand_weight.shape[1]
    row = lambda a: a.reshape(1, -1)
    tok = tokens.reshape(-1, width)
    cot = cotangent.reshape(-1, width)
    mask = lag_columns(segments)
    filt = [embed_weight, row(embed_bias), row(embed_omega), inner_weight, row(inner_bias), row(inner_omega), outer_weight,
        row(outer_bias), row(outer_omega), filter_weight]
    tabs, tabst = radix_tables(length)
    zt, rates = filter_inputs(length, emb, width)
    proj, mixed, longc, mix, trans, spec, state, ntr = forward_mixer(
        tok, mask, row(first_gain), row(first_shift), mixer_weight, row(mixer_bias), short_weight, row(short_bias),
        row(skip_gain), filt, zt, rates, tabs, tabst, rows_here)
    out, dat, wog, weg, wrg, beg, vec2 = mlp(
        mix, tok, cot, output_weight, row(output_bias), row(second_gain), row(second_shift), expand_weight,
        row(expand_bias), reduce_weight, row(reduce_bias))
    tgrad, wmg, sgrad, vec1, gew, giw, gow, gfw, gsm = backward_mixer(
        dat, tok, mask, row(first_gain), output_weight, longc, mixed, proj, trans, spec, ntr, mixer_weight, short_weight,
        row(skip_gain), state, filt, zt, rates, tabs, tabst, rows_here)
    group = sizes if rows_n * pos_n <= 32 else (rows_n, 1)
    packed = all_reduce_small(group, beg, vec2, sgrad, vec1, gew, giw, gow, gfw, gsm)
    if group != tuple(sizes):
        packed = lax.psum(packed, "pos")
    (fg, fs, mb, sw, sb, ew, eb, eo, iw, ib, io, ow, ob, oo, fw, sk, obias, sg, ss, eb2, rb) = unpack_small(
        packed, width, hidden, emb, ff)
    flat = lambda a: a.reshape(-1)
    e_grad = scatter_blocks(weg, rows_n, pos_n, order_a)
    r_grad = scatter_blocks(wrg, rows_n, pos_n, order_b)
    o_grad = scatter_blocks(wog, rows_n, pos_n, order_a)
    blocks = wmg.shape[0] * wmg.shape[1]
    m_grad = scatter_blocks(wmg.reshape(blocks, width, -1), rows_n, pos_n, order_b)
    return (out.reshape(tokens.shape), tgrad.reshape(tokens.shape), flat(fg), flat(fs), m_grad, flat(mb), sw, flat(sb), ew,
        flat(eb), flat(eo), iw, flat(ib), flat(io), ow, flat(ob), flat(oo), fw, flat(sk), o_grad, flat(obias), flat(sg),
        flat(ss), e_grad, flat(eb2), r_grad, flat(rb))


def solution(mesh):
    both = ("rows", "pos")
    rows3 = P(both, None, None)
    grid = P("rows", "pos")
    in_specs = (rows3, P(both, None), rows3) + (P(),) * 25
    out_specs = (rows3, rows3, P(), P(), grid) + (P(),) * 14 + (grid, P(), P(), P(), grid, P(), grid, P())
    sizes = (mesh.shape["rows"], mesh.shape["pos"])
    return jax.shard_map(
        functools.partial(on_device, sizes), mesh=mesh, in_specs=in_specs, out_specs=out_specs, check_vma=False)
```

time: 1260 us -> 376 us (0.30)
  waiting for transfers between devices: 556 us -> 58.4 us
  matrix products: 301 us -> 0 us
  Pallas kernels: 0 us -> 225 us
  other arithmetic: 251 us -> 27.8 us
  local copies, waits for them, and re-layouts: 125 us -> 25.7 us
  starting transfers between devices: 1.12 us -> 30 us
  between operations: 17.1 us -> 1.56 us
    dot_general x53 -> x0, matrix products: 301 us -> none  [the longest x2 55.8 us: on_device(): jnp.einsum('rld,df->rlf', normed2_low, expand_weight, preferred_element_t...]
    psum x2 -> x0, waiting for transfers between devices: 294 us -> none  [on_device(): lax.psum((first_gain_grad, first_shift_grad, mixer_bias_grad, short_weigh...]
    reduce_scatter x9 -> x0, waiting for transfers between devices: 261 us -> none  [the longest x1 110 us: on_device(): lax.psum_scatter(matrices[2], 'rows', scatter_dimension=0, tiled=True)]
    pallas_call x0 -> x5, Pallas kernels: none -> 225 us  [the longest x1 76.5 us: mlp(): pl.pallas_call(functools.partial(mlp_kernel, FC, TT), grid=(J,), in_specs...]
    unnamed x545 -> x25, local copies, waits for them, and re-layouts: 84.8 us -> 0.86 us
    reduce_sum x20 -> x0, other arithmetic: 71.8 us -> none  [the longest x2 18.7 us: short_conv(): result = result + short_weight[delay] * moved * same[:, :, delay:delay + 1]]
    ppermute x0 -> x20, waiting for transfers between devices: none -> 58.4 us  [scatter_blocks(): got = lax.ppermute(send, axis, [(i, i ^ 1 << bit) for i in range(size)])]
    add_any x4 -> x0, other arithmetic: 37.9 us -> none  [spectral_product(): real = real_one * real_two - imag_one * imag_two]
  transfers between devices with their start and end apart: 12 -> 20, of which waited for: 7 -> 10; matrix products, arithmetic and copies ran while one was open for 29% -> 10% of each run, Pallas kernels for 0% -> 27%
where the time goes in v1:
time: 376 us; the launch traced here: 369 us
  Pallas kernels  225 us (60%)
  waiting for transfers between devices  58.4 us (16%)
  starting transfers between devices  30 us (8%)
  other arithmetic  27.8 us (7%)
  local copies, waits for them, and re-layouts  25.7 us (7%)
    pallas_call x1, Pallas kernels, mlp(): pl.pallas_call(functools.partial(mlp_kernel, FC, TT), grid=(J,), in_specs...  76.5 us
    pallas_call x1, Pallas kernels, backward_mixer(): pl.pallas_call(functools.partial(bwd_kernel, rows_here), grid=(J,), in_sp...  65.3 us
    ppermute x20, waiting for transfers between devices, scatter_blocks(): got = lax.ppermute(send, axis, [(i, i ^ 1 << bit) for i in range(size)])  58.4 us
    pallas_call x1, Pallas kernels, forward_mixer(): pl.pallas_call(functools.partial(fwd_kernel, rows_here), grid=(J,), in_sp...  48.2 us
    pallas_call x1, Pallas kernels, all_reduce_small(): pl.pallas_call(functools.partial(reduce_kernel, sizes, places), out_shape...  33.6 us
    ppermute x20, starting transfers between devices, scatter_blocks(): got = lax.ppermute(send, axis, [(i, i ^ 1 << bit) for i in range(size)])  30 us
    squeeze x20, local copies, waits for them, and re-layouts, scatter_blocks(): send = lax.dynamic_index_in_dim(acc, 1 - mine, dim, keepdims=False)  12.9 us
    pallas_call x9, other arithmetic, unpack_small(): pl.pallas_call(kernel, out_shape=shapes, in_specs=[vm], out_specs=[vm] *...  11.6 us
  transfers between devices with their start and end apart: 20, of which 10 were waited for; matrix products, arithmetic and copies ran while one was open for 10% of the time, Pallas kernels for 27%

profile of v1, /device:TPU:0, one launch (start us, length us, event | category | flops | bytes accessed | tf_op | source)
XLA Modules:
  0.0 368.9 jit_solution(7223312558533625490)
XLA Ops:
  0.7 0.9 compare_bitcast_fusion
  2.1 1.0 convert_element_type.256.mask_ref
  3.0 1.3 reshape.243.g1_ref
  4.3 1.3 reshape.247.skip_ref
  5.6 1.3 reshape.245.bg_ref.bi_ref.bv_ref
  6.9 1.3 reshape.246.sbg_ref.sbi_ref.sbv_ref
  8.2 1.3 reshape.244.s1_ref
  9.5 1.3 reshape.255.bo_ref
  10.7 1.3 reshape.256.g2_ref
  12.0 1.3 reshape.257.s2_ref
  13.3 1.3 reshape.259.br_ref
  14.5 48.2 %mixer_forward.1 = (bf16[3,1536,768]{2,1,0:T(8,128)(2,1)}, bf16[3,1536,768]{2,1,0:T(8,128)(2,1)}, bf16[1536,768]{1,0:T(8,128)(2,1)}, bf16[1536,768]{1,0:T(8,128)...) custom-call(bf16[1536,768]{1,0:T(8,128)(2,1)} %bitcast.190, ...), custom_call_target="tpu_custom_call" | custom-call | flops 16137584640 | bytes 41943040 | tf_op jit(solution)/shard_map/mixer_forward/pallas_call | solution.py:186
  62.7 76.5 %mlp.1 = (bf16[1536,768]{1,0:T(8,128)(2,1)}, bf16[1536,768]{1,0:T(8,128)(2,1)}, bf16[6,768,128]{2,1,0:T(8,128)(2,1)}, bf16[24,768,128]{2,1,0:T(8,128)(2,1)}, bf1...) custom-call(bf16[1536,768]{1,0:T(8,128)(2,1)} %get-tuple-element.72.mix_ref, ...), custom_call_target="tpu_custom_call" | custom-call | flops 48922361856 | bytes 41943040 | tf_op jit(solution)/shard_map/mlp/pallas_call | solution.py:401
  139.2 1.1 dynamic-slice_bitcast_fusion.8
  140.8 65.3 %mixer_backward.1 = (bf16[1536,768]{1,0:T(8,128)(2,1)}, bf16[3,6,768,128]{3,2,1,0:T(8,128)(2,1)}, f32[3,8,768]{2,1,0:T(8,128)}, f32[8,768]{1,0:T(8,128)}, f32[40...) custom-call(bf16[1536,768]{1,0:T(8,128)(2,1)} %get-tuple-element.74.dat_ref, ...), custom_call_target="tpu_custom_call" | custom-call | flops 22753050624 | bytes 52428800 | tf_op jit(solution)/shard_map/mixer_backward/pallas_call | solution.py:306
  206.2 3.1 dynamic-slice_bitcast_fusion.2
  209.4 3.5 dynamic-slice_bitcast_fusion
  213.5 2.7 collective-permute-start.6
  216.2 3.7 dynamic-slice_bitcast_fusion.1
  220.0 3.7 %collective-permute-done.6 = bf16[3,2,2,2,48,128]{5,4,3,2,1,0:T(8,128)(2,1)S(1)} collective-permute-done((bf16[3,2,2,2,48,128]{5,4,3,2,1,0:T(8,128)(2,1)S(1)}, bf16[3,2,2,2,48,128]{5,4,3,2,1,0:T(8,128)(2,1)S(1)}, u32[]{:S(2)}, u32[]{:S(2)}) %collective-permute-start.6) | collective-permute-done | bytes 294944 | tf_op jit(solution)/shard_map/ppermute | solution.py:635
  223.9 1.9 collective-permute-start.7
  225.7 3.8 %collective-permute-done.7 = bf16[3,2,2,48,128]{4,3,2,1,0:T(8,128)(2,1)S(1)} collective-permute-done((bf16[3,2,2,48,128]{4,3,2,1,0:T(8,128)(2,1)S(1)}, bf16[3,2,2,48,128]{4,3,2,1,0:T(8,128)(2,1)S(1)}, u32[]{:S(2)}, u32[]{:S(2)}) %collective-permute-start.7) | collective-permute-done | bytes 147488 | tf_op jit(solution)/shard_map/ppermute | solution.py:635
  229.7 1.7 collective-permute-start.8
  231.4 2.7 fusion.2
  234.2 1.0 dynamic-slice_bitcast_fusion.5
  235.2 1.5 collective-permute-start.1
  236.7 33.6 %sum_small.1.pk = f32[256,384]{1,0:T(8,128)S(1)} custom-call(f32[1,3072]{1,0:T(1,128)S(1)} %copy-done.9, f32[8,768]{1,0:T(8,128)S(1)} %copy-done.5, f32[3,8,768]{2,1,0:T(8,128)S(1)} %copy-done.2, f32[8,768]{1,0:T(8,128)S(1)} %copy-done.6, f32[40,64]{1,0:T(8,128)S(1)} %copy-done.8, f32[64,64]{1,0:T(8,128)S(1)} %copy-done.3, f32[64,64]{1,0:T(8,128)S(1)} %copy-done.4, ...), custom_call_target="tpu_custom_call" | custom-call | tf_op jit(solution)/shard_map/sum_small/pallas_call | solution.py:562
  270.4 0.8 copy-done
  271.2 1.8 unpack_small.1
  272.9 1.3 reduce.2
  274.3 1.3 reduce.3
  275.6 1.3 reduce
  276.9 1.3 reduce.1
  278.2 1.3 reduce.4
  279.5 1.3 reduce.5
  280.8 1.3 reduce.6
  282.0 1.3 reduce.7
  283.3 1.3 reduce.8
  284.7 2.2 collective-permute-start.9
  286.9 3.4 fusion
  290.4 1.3 collective-permute-start.16
  292.0 1.5 collective-permute-start.2
  293.5 3.4 fusion.1
  297.1 0.6 collective-permute-start.11
  297.7 7.5 %collective-permute-done.2 = bf16[9,2,2,48,128]{4,3,2,1,0:T(8,128)(2,1)S(1)} collective-permute-done((bf16[9,2,2,48,128]{4,3,2,1,0:T(8,128)(2,1)S(1)}, bf16[9,2,2,48,128]{4,3,2,1,0:T(8,128)(2,1)S(1)}, u32[]{:S(2)}, u32[]{:S(2)}) %collective-permute-start.2) | collective-permute-done | bytes 442400 | tf_op jit(solution)/shard_map/ppermute | solution.py:635
  305.3 2.3 collective-permute-start.3
  307.6 0.6 copy_bitcast_fusion.3
  308.2 3.3 collective-permute-done.3
  311.6 2.4 collective-permute-start.4
  314.0 4.0 %collective-permute-done.16 = bf16[2,3,2,2,192,128]{5,4,3,2,1,0:T(8,128)(2,1)S(1)} collective-permute-done((bf16[2,3,2,2,192,128]{5,4,3,2,1,0:T(8,128)(2,1)S(1)}, bf16[2,3,2,2,192,128]{5,4,3,2,1,0:T(8,128)(2,1)S(1)}, u32[]{:S(2)}, u32[]{:S(2)}) %collective-permute-start.16) | collective-permute-done | bytes 1179680 | tf_op jit(solution)/shard_map/ppermute | solution.py:635
  318.5 1.5 collective-permute-start.17
  320.0 10.4 %collective-permute-done.11 = bf16[12,2,2,2,48,128]{5,4,3,2,1,0:T(8,128)(2,1)S(1)} collective-permute-done((bf16[12,2,2,2,48,128]{5,4,3,2,1,0:T(8,128)(2,1)S(1)}, bf16[12,2,2,2,48,128]{5,4,3,2,1,0:T(8,128)(2,1)S(1)}, u32[]{:S(2)}, u32[]{:S(2)}) %collective-permute-start.11) | collective-permute-done | bytes 1179680 | tf_op jit(solution)/shard_map/ppermute | solution.py:635
  330.8 0.9 collective-permute-start.12
  331.7 0.7 copy_bitcast_fusion.2
  332.5 9.1 %collective-permute-done.17 = bf16[3,2,2,192,128]{4,3,2,1,0:T(8,128)(2,1)S(1)} collective-permute-done((bf16[3,2,2,192,128]{4,3,2,1,0:T(8,128)(2,1)S(1)}, bf16[3,2,2,192,128]{4,3,2,1,0:T(8,128)(2,1)S(1)}, u32[]{:S(2)}, u32[]{:S(2)}) %collective-permute-start.17) | collective-permute-done | bytes 589856 | tf_op jit(solution)/shard_map/ppermute | solution.py:635
  341.8 2.3 collective-permute-start.18
  344.3 1.5 collective-permute-start.13
  345.8 6.2 %collective-permute-done.18 = bf16[3,2,192,128]{3,2,1,0:T(8,128)(2,1)S(1)} collective-permute-done((bf16[3,2,192,128]{3,2,1,0:T(8,128)(2,1)S(1)}, bf16[3,2,192,128]{3,2,1,0:T(8,128)(2,1)S(1)}, u32[]{:S(2)}, u32[]{:S(2)}) %collective-permute-start.18) | collective-permute-done | bytes 294944 | tf_op jit(solution)/shard_map/ppermute | solution.py:635
  352.2 2.7 collective-permute-start.19
  354.8 4.2 %collective-permute-done.13 = bf16[12,2,48,128]{3,2,1,0:T(8,128)(2,1)S(1)} collective-permute-done((bf16[12,2,48,128]{3,2,1,0:T(8,128)(2,1)S(1)}, bf16[12,2,48,128]{3,2,1,0:T(8,128)(2,1)S(1)}, u32[]{:S(2)}, u32[]{:S(2)}) %collective-permute-start.13) | collective-permute-done | bytes 294944 | tf_op jit(solution)/shard_map/ppermute | solution.py:635
  359.2 1.7 collective-permute-start.14
  360.9 0.7 copy_bitcast_fusion
  361.6 6.1 %collective-permute-done.14 = bf16[12,48,128]{2,1,0:T(8,128)(2,1)S(1)} collective-permute-done((bf16[12,48,128]{2,1,0:T(8,128)(2,1)S(1)}, bf16[12,48,128]{2,1,0:T(8,128)(2,1)S(1)}, u32[]{:S(2)}, u32[]{:S(2)}) %collective-permute-start.14) | collective-permute-done | bytes 147488 | tf_op jit(solution)/shard_map/ppermute | solution.py:635
  367.8 0.7 copy_bitcast_fusion.1
  (68 shorter events, 4.2 us)
Async XLA Ops:
  140.3 73.0 %collective-permute-start.5 = (bf16[2,3,2,2,2,48,128]{6,5,4,3,2,1,0:T(8,128)(2,1)S(1)}, bf16[2,3,2,2,2,48,128]{6,5,4,3,2,1,0:T(8,128)(2,1)S(1)}, u32[]{:S(2)}, u32[]{:S(2)}) collective-permute-start(bf16[2,3,2,2,2,48,128]{6,5,4,3,2,1,0:T(8,128)(2,1)S(1)} %dynamic-slice_bitcast_fusion.8), channel_id=1, source_target_pairs={{0,2},{2,0},{4,6},{6,4},{8,10},{10,8},{12,14},{14,12},{16,18},{18,... | collective-permute-start | bytes 1769480 | tf_op jit(solution)/shard_map/ppermute | solution.py:635
  209.3 22.1 %collective-permute-start = (bf16[2,9,2,2,2,48,128]{6,5,4,3,2,1,0:T(8,128)(2,1)}, bf16[2,9,2,2,2,48,128]{6,5,4,3,2,1,0:T(8,128)(2,1)}, u32[]{:S(2)}, u32[]{:S(2)}) collective-permute-start(bf16[2,9,2,2,2,48,128]{6,5,4,3,2,1,0:T(8,128)(2,1)} %dynamic-slice_bitcast_fusion.2), channel_id=1, source_target_pairs={{0,2},{2,0},{4,6},{6,4},{8,10},{10,8},{12,14},{14,12},{16,18},{18,... | collective-permute-start | bytes 5308424 | tf_op jit(solution)/shard_map/ppermute | solution.py:635
  209.4 3.9 %copy-start.10 = (bf16[6,768,128]{2,1,0:T(8,128)(2,1)S(1)}, bf16[6,768,128]{2,1,0:T(8,128)(2,1)}, u32[]{:S(2)}) copy-start(bf16[6,768,128]{2,1,0:T(8,128)(2,1)} %get-tuple-element.109) | copy-start | bytes 3538948
  212.9 74.0 %collective-permute-start.15 = (bf16[2,3,2,2,2,192,128]{6,5,4,3,2,1,0:T(8,128)(2,1)}, bf16[2,3,2,2,2,192,128]{6,5,4,3,2,1,0:T(8,128)(2,1)}, u32[]{:S(2)}, u32[]{:S(2)}) collective-permute-start(bf16[2,3,2,2,2,192,128]{6,5,4,3,2,1,0:T(8,128)(2,1)} %dynamic-slice_bitcast_fusion), channel_id=1, source_target_pairs={{0,2},{2,0},{4,6},{6,4},{8,10},{10,8},{12,14},{14,12},{16,18},{18,... | collective-permute-start | bytes 7077896 | tf_op jit(solution)/shard_map/ppermute | solution.py:635
  213.5 10.3 %collective-permute-start.6 = (bf16[3,2,2,2,48,128]{5,4,3,2,1,0:T(8,128)(2,1)S(1)}, bf16[3,2,2,2,48,128]{5,4,3,2,1,0:T(8,128)(2,1)S(1)}, u32[]{:S(2)}, u32[]{:S(2)}) collective-permute-start(bf16[3,2,2,2,48,128]{5,4,3,2,1,0:T(8,128)(2,1)S(1)} %dynamic-slice_bitcast_fusion.12), channel_id=1, source_target_pairs={{0,1},{1,0},{2,3},{3,2},{4,5},{5,4},{6,7},{7,6},{8,9},{9,8},{10,11... | collective-permute-start | bytes 884744 | tf_op jit(solution)/shard_map/ppermute | solution.py:635
  219.9 73.7 %collective-permute-start.10 = (bf16[2,12,2,2,2,48,128]{6,5,4,3,2,1,0:T(8,128)(2,1)}, bf16[2,12,2,2,2,48,128]{6,5,4,3,2,1,0:T(8,128)(2,1)}, u32[]{:S(2)}, u32[]{:S(2)}) collective-permute-start(bf16[2,12,2,2,2,48,128]{6,5,4,3,2,1,0:T(8,128)(2,1)} %dynamic-slice_bitcast_fusion.1), channel_id=1, source_target_pairs={{0,2},{2,0},{4,6},{6,4},{8,10},{10,8},{12,14},{14,12},{16,18},{18,... | collective-permute-start | bytes 7077896 | tf_op jit(solution)/shard_map/ppermute | solution.py:635
  223.9 5.6 %collective-permute-start.7 = (bf16[3,2,2,48,128]{4,3,2,1,0:T(8,128)(2,1)S(1)}, bf16[3,2,2,48,128]{4,3,2,1,0:T(8,128)(2,1)S(1)}, u32[]{:S(2)}, u32[]{:S(2)}) collective-permute-start(bf16[3,2,2,48,128]{4,3,2,1,0:T(8,128)(2,1)S(1)} %dynamic-slice_bitcast_fusion.16), channel_id=1, source_target_pairs={{0,4},{2,6},{4,0},{6,2},{8,12},{10,14},{12,8},{14,10},{16,20},{18,... | collective-permute-start | bytes 442376 | tf_op jit(solution)/shard_map/ppermute | solution.py:635
  229.6 7.1 %copy-start.1 = (f32[64,768]{1,0:T(8,128)S(1)}, f32[64,768]{1,0:T(8,128)}, u32[]{:S(2)}) copy-start(f32[64,768]{1,0:T(8,128)} %get-tuple-element.90.refs_7_) | copy-start | bytes 589828
  229.6 7.1 %copy-start.2 = (f32[3,8,768]{2,1,0:T(8,128)S(1)}, f32[3,8,768]{2,1,0:T(8,128)}, u32[]{:S(2)}) copy-start(f32[3,8,768]{2,1,0:T(8,128)} %get-tuple-element.85.refs_2_) | copy-start | bytes 221188
  229.6 7.1 %copy-start.3 = (f32[64,64]{1,0:T(8,128)S(1)}, f32[64,64]{1,0:T(8,128)}, u32[]{:S(2)}) copy-start(f32[64,64]{1,0:T(8,128)} %get-tuple-element.88.refs_5_) | copy-start | bytes 49156
  229.6 7.1 %copy-start.4 = (f32[64,64]{1,0:T(8,128)S(1)}, f32[64,64]{1,0:T(8,128)}, u32[]{:S(2)}) copy-start(f32[64,64]{1,0:T(8,128)} %get-tuple-element.89.refs_6_) | copy-start | bytes 49156
  229.6 7.1 %copy-start.5 = (f32[8,768]{1,0:T(8,128)S(1)}, f32[8,768]{1,0:T(8,128)}, u32[]{:S(2)}) copy-start(f32[8,768]{1,0:T(8,128)} %get-tuple-element.84.refs_1_) | copy-start | bytes 73732
  229.6 7.1 %copy-start.6 = (f32[8,768]{1,0:T(8,128)S(1)}, f32[8,768]{1,0:T(8,128)}, u32[]{:S(2)}) copy-start(f32[8,768]{1,0:T(8,128)} %get-tuple-element.86.refs_3_) | copy-start | bytes 73732
  229.7 7.1 %copy-start.7 = (f32[6,8,64]{2,1,0:T(8,128)S(1)}, f32[6,8,64]{2,1,0:T(8,128)}, u32[]{:S(2)}) copy-start(f32[6,8,64]{2,1,0:T(8,128)} %get-tuple-element.91.refs_8_) | copy-start | bytes 36868
  229.7 7.1 %copy-start.8 = (f32[40,64]{1,0:T(8,128)S(1)}, f32[40,64]{1,0:T(8,128)}, u32[]{:S(2)}) copy-start(f32[40,64]{1,0:T(8,128)} %get-tuple-element.87.refs_4_) | copy-start | bytes 30724
  229.7 7.1 %copy-start.9 = (f32[1,3072]{1,0:T(1,128)S(1)}, f32[1,3072]{1,0:T(1,128)}, u32[]{:S(2)}) copy-start(f32[1,3072]{1,0:T(1,128)} %get-tuple-element.83.refs_0_) | copy-start | bytes 36868
  229.7 54.9 %collective-permute-start.8 = (bf16[3,2,48,128]{3,2,1,0:T(8,128)(2,1)S(1)}, bf16[3,2,48,128]{3,2,1,0:T(8,128)(2,1)S(1)}, u32[]{:S(2)}, u32[]{:S(2)}) collective-permute-start(bf16[3,2,48,128]{3,2,1,0:T(8,128)(2,1)S(1)} %dynamic-slice_bitcast_fusion.18), channel_id=1, source_target_pairs={{0,8},{2,10},{4,12},{6,14},{8,0},{10,2},{12,4},{14,6},{16,24},{18,... | collective-permute-start | bytes 221192 | tf_op jit(solution)/shard_map/ppermute | solution.py:635
  235.2 56.5 %collective-permute-start.1 = (bf16[2,9,2,2,48,128]{5,4,3,2,1,0:T(8,128)(2,1)}, bf16[2,9,2,2,48,128]{5,4,3,2,1,0:T(8,128)(2,1)S(1)}, u32[]{:S(2)}, u32[]{:S(2)}) collective-permute-start(bf16[2,9,2,2,48,128]{5,4,3,2,1,0:T(8,128)(2,1)} %dynamic-slice_bitcast_fusion.5), channel_id=1, source_target_pairs={{0,4},{2,6},{4,0},{6,2},{8,12},{10,14},{12,8},{14,10},{16,20},{18,... | collective-permute-start | bytes 2654216 | tf_op jit(solution)/shard_map/ppermute | solution.py:635
  270.4 0.8 copy-start
  284.7 22.9 %collective-permute-start.9 = (bf16[3,48,128]{2,1,0:T(8,128)(2,1)S(1)}, bf16[3,48,128]{2,1,0:T(8,128)(2,1)S(1)}, u32[]{:S(2)}, u32[]{:S(2)}) collective-permute-start(bf16[3,48,128]{2,1,0:T(8,128)(2,1)S(1)} %dynamic-slice_bitcast_fusion.19), channel_id=1, source_target_pairs={{0,16},{2,18},{4,20},{6,22},{8,24},{10,26},{12,28},{14,30},{16,0},... | collective-permute-start | bytes 110600 | tf_op jit(solution)/shard_map/ppermute | solution.py:635
  290.4 27.7 %collective-permute-start.16 = (bf16[2,3,2,2,192,128]{5,4,3,2,1,0:T(8,128)(2,1)S(1)}, bf16[2,3,2,2,192,128]{5,4,3,2,1,0:T(8,128)(2,1)S(1)}, u32[]{:S(2)}, u32[]{:S(2)}) collective-permute-start(bf16[2,3,2,2,192,128]{5,4,3,2,1,0:T(8,128)(2,1)S(1)} %dynamic-slice_bitcast_fusion.3), channel_id=1, source_target_pairs={{0,4},{2,6},{4,0},{6,2},{8,12},{10,14},{12,8},{14,10},{16,20},{18,... | collective-permute-start | bytes 3538952 | tf_op jit(solution)/shard_map/ppermute | solution.py:635
  292.0 13.2 %collective-permute-start.2 = (bf16[9,2,2,48,128]{4,3,2,1,0:T(8,128)(2,1)S(1)}, bf16[9,2,2,48,128]{4,3,2,1,0:T(8,128)(2,1)S(1)}, u32[]{:S(2)}, u32[]{:S(2)}) collective-permute-start(bf16[9,2,2,48,128]{4,3,2,1,0:T(8,128)(2,1)S(1)} %dynamic-slice_bitcast_fusion.9), channel_id=1, source_target_pairs={{0,1},{1,0},{2,3},{3,2},{4,5},{5,4},{6,7},{7,6},{8,9},{9,8},{10,11... | collective-permute-start | bytes 1327112 | tf_op jit(solution)/shard_map/ppermute | solution.py:635
  297.1 33.4 %collective-permute-start.11 = (bf16[12,2,2,2,48,128]{5,4,3,2,1,0:T(8,128)(2,1)S(1)}, bf16[12,2,2,2,48,128]{5,4,3,2,1,0:T(8,128)(2,1)S(1)}, u32[]{:S(2)}, u32[]{:S(2)}) collective-permute-start(bf16[12,2,2,2,48,128]{5,4,3,2,1,0:T(8,128)(2,1)S(1)} %dynamic-slice_bitcast_fusion.4), channel_id=1, source_target_pairs={{0,1},{1,0},{2,3},{3,2},{4,5},{5,4},{6,7},{7,6},{8,9},{9,8},{10,11... | collective-permute-start | bytes 3538952 | tf_op jit(solution)/shard_map/ppermute | solution.py:635
  305.3 6.2 %collective-permute-start.3 = (bf16[9,2,48,128]{3,2,1,0:T(8,128)(2,1)S(1)}, bf16[9,2,48,128]{3,2,1,0:T(8,128)(2,1)S(1)}, u32[]{:S(2)}, u32[]{:S(2)}) collective-permute-start(bf16[9,2,48,128]{3,2,1,0:T(8,128)(2,1)S(1)} %dynamic-slice_bitcast_fusion.13), channel_id=1, source_target_pairs={{0,8},{2,10},{4,12},{6,14},{8,0},{10,2},{12,4},{14,6},{16,24},{18,... | collective-permute-start | bytes 663560 | tf_op jit(solution)/shard_map/ppermute | solution.py:635
  311.6 20.1 %collective-permute-start.4 = (bf16[9,48,128]{2,1,0:T(8,128)(2,1)S(1)}, bf16[9,48,128]{2,1,0:T(8,128)(2,1)S(1)}, u32[]{:S(2)}, u32[]{:S(2)}) collective-permute-start(bf16[9,48,128]{2,1,0:T(8,128)(2,1)S(1)} %dynamic-slice_bitcast_fusion.17), channel_id=1, source_target_pairs={{0,16},{2,18},{4,20},{6,22},{8,24},{10,26},{12,28},{14,30},{16,0},... | collective-permute-start | bytes 331784 | tf_op jit(solution)/shard_map/ppermute | solution.py:635
  318.5 23.1 %collective-permute-start.17 = (bf16[3,2,2,192,128]{4,3,2,1,0:T(8,128)(2,1)S(1)}, bf16[3,2,2,192,128]{4,3,2,1,0:T(8,128)(2,1)S(1)}, u32[]{:S(2)}, u32[]{:S(2)}) collective-permute-start(bf16[3,2,2,192,128]{4,3,2,1,0:T(8,128)(2,1)S(1)} %dynamic-slice_bitcast_fusion.6), channel_id=1, source_target_pairs={{0,1},{1,0},{2,3},{3,2},{4,5},{5,4},{6,7},{7,6},{8,9},{9,8},{10,11... | collective-permute-start | bytes 1769480 | tf_op jit(solution)/shard_map/ppermute | solution.py:635
  330.8 13.3 %collective-permute-start.12 = (bf16[12,2,2,48,128]{4,3,2,1,0:T(8,128)(2,1)S(1)}, bf16[12,2,2,48,128]{4,3,2,1,0:T(8,128)(2,1)S(1)}, u32[]{:S(2)}, u32[]{:S(2)}) collective-permute-start(bf16[12,2,2,48,128]{4,3,2,1,0:T(8,128)(2,1)S(1)} %dynamic-slice_bitcast_fusion.7), channel_id=1, source_target_pairs={{0,4},{2,6},{4,0},{6,2},{8,12},{10,14},{12,8},{14,10},{16,20},{18,... | collective-permute-start | bytes 1769480 | tf_op jit(solution)/shard_map/ppermute | solution.py:635
  341.8 10.3 %collective-permute-start.18 = (bf16[3,2,192,128]{3,2,1,0:T(8,128)(2,1)S(1)}, bf16[3,2,192,128]{3,2,1,0:T(8,128)(2,1)S(1)}, u32[]{:S(2)}, u32[]{:S(2)}) collective-permute-start(bf16[3,2,192,128]{3,2,1,0:T(8,128)(2,1)S(1)} %dynamic-slice_bitcast_fusion.10), channel_id=1, source_target_pairs={{0,8},{2,10},{4,12},{6,14},{8,0},{10,2},{12,4},{14,6},{16,24},{18,... | collective-permute-start | bytes 884744 | tf_op jit(solution)/shard_map/ppermute | solution.py:635
  344.3 14.7 %collective-permute-start.13 = (bf16[12,2,48,128]{3,2,1,0:T(8,128)(2,1)S(1)}, bf16[12,2,48,128]{3,2,1,0:T(8,128)(2,1)S(1)}, u32[]{:S(2)}, u32[]{:S(2)}) collective-permute-start(bf16[12,2,48,128]{3,2,1,0:T(8,128)(2,1)S(1)} %dynamic-slice_bitcast_fusion.11), channel_id=1, source_target_pairs={{0,8},{2,10},{4,12},{6,14},{8,0},{10,2},{12,4},{14,6},{16,24},{18,... | collective-permute-start | bytes 884744 | tf_op jit(solution)/shard_map/ppermute | solution.py:635
  352.2 8.7 %collective-permute-start.19 = (bf16[3,192,128]{2,1,0:T(8,128)(2,1)S(1)}, bf16[3,192,128]{2,1,0:T(8,128)(2,1)S(1)}, u32[]{:S(2)}, u32[]{:S(2)}) collective-permute-start(bf16[3,192,128]{2,1,0:T(8,128)(2,1)S(1)} %dynamic-slice_bitcast_fusion.14), channel_id=1, source_target_pairs={{0,16},{2,18},{4,20},{6,22},{8,24},{10,26},{12,28},{14,30},{16,0},... | collective-permute-start | bytes 442376 | tf_op jit(solution)/shard_map/ppermute | solution.py:635
  359.2 8.6 %collective-permute-start.14 = (bf16[12,48,128]{2,1,0:T(8,128)(2,1)S(1)}, bf16[12,48,128]{2,1,0:T(8,128)(2,1)S(1)}, u32[]{:S(2)}, u32[]{:S(2)}) collective-permute-start(bf16[12,48,128]{2,1,0:T(8,128)(2,1)S(1)} %dynamic-slice_bitcast_fusion.15), channel_id=1, source_target_pairs={{0,16},{2,18},{4,20},{6,22},{8,24},{10,26},{12,28},{14,30},{16,0},... | collective-permute-start | bytes 442376 | tf_op jit(solution)/shard_map/ppermute | solution.py:635

commit v2 on v0

v2 whole, which is shorter than its diff:
```python
import functools
import math

import jax
import jax.numpy as jnp
import numpy as np
from jax import lax
from jax.experimental import pallas as pl
from jax.experimental.pallas import tpu as pltpu
from jax.sharding import PartitionSpec as P

f32 = jnp.float32
bf = jnp.bfloat16
HI = lax.Precision.HIGHEST
MESH = pl.DeviceIdType.MESH
DOCS = 2
EPSILON = 1e-5
ROOT3 = math.sqrt(3.0) / 2
LANES = 128
CHUNK = 256
PACK = 384
VMEM_BYTES = 62 * 2**20


def nt(a, b, precision=None):
    return lax.dot_general(a, b, (((1,), (1,)), ((), ())), precision=precision, preferred_element_type=f32)


def nn(a, b, precision=None):
    return lax.dot_general(a, b, (((1,), (0,)), ((), ())), precision=precision, preferred_element_type=f32)


def tn(a, b, precision=None):
    return lax.dot_general(a, b, (((0,), (0,)), ((), ())), precision=precision, preferred_element_type=f32)


def norm_stats(x):
    mean = jnp.mean(x, axis=-1, keepdims=True)
    centered = x - mean
    variance = jnp.mean(centered * centered, axis=-1, keepdims=True)
    scale = lax.rsqrt(variance + EPSILON)
    return centered * scale, scale


def sum0(v):
    return jnp.sum(v, axis=0, keepdims=True)


def as_row(ref):
    return ref[...].reshape(1, -1)


def radix_tables(length):
    n = length // 3
    m = 2 * length
    place = np.arange(n)

    def angle(freqs):
        return 2 * np.pi * ((freqs[:, None] * place[None, :]) % m) / m

    even = angle(6 * np.arange(n // 2))
    sine = np.sin(even)
    sine[0] = np.cos(np.pi * place)
    odd = angle(6 * np.arange(n // 2) + 3)
    out = [np.concatenate([np.cos(even), sine], 0), np.concatenate([np.cos(odd), np.sin(odd)], 0)]
    for k in (1, 2):
        turn = angle(6 * np.arange(n) + k)
        c, s = np.cos(turn), np.sin(turn)
        out.append(np.block([[c, -s], [s, c]]))
    low = lambda v: jnp.asarray(v.astype(np.float32)).astype(bf)
    return [low(t) for t in out], [low(t.T) for t in out]


def spread(x0, x1, x2):
    s = x1 + x2
    d = x1 - x2
    y0 = (x0 + s).astype(bf)
    y3 = (x0 - d).astype(bf)
    y1 = jnp.concatenate([(x0 + 0.5 * d).astype(bf), (ROOT3 * s).astype(bf)], 0)
    y2 = jnp.concatenate([(x0 - 0.5 * s).astype(bf), (ROOT3 * d).astype(bf)], 0)
    return y0, y3, y1, y2


def gather(v0, v3, v1, v2):
    n = v0.shape[0]
    v1r, v1i, v2r, v2i = v1[:n], v1[n:], v2[:n], v2[n:]
    even = v0 + v3
    a = 0.5 * (v1r - v2r)
    b = ROOT3 * (v1i + v2i)
    x0 = even + v1r + v2r
    x1 = (v0 - v3) + a + b
    x2 = even - 0.5 * (v1r + v2r) + ROOT3 * (v1i - v2i)
    return x0, x1, x2


def filter_inputs(length, emb, width):
    bands_count = (emb - 1) // 2
    places = np.arange(length, dtype=np.float32)
    tnorm = places / np.float32(length - 1)
    wave = places * np.float32(2.0 * math.pi / length)
    bands = np.linspace(0.0001, bands_count - 1, bands_count).astype(np.float32)
    phase = (wave[:, None] * bands[None, :]).astype(np.float32)
    z = np.concatenate([tnorm[:, None], np.cos(phase), -np.sin(phase)], 1).astype(np.float32)
    zt = np.concatenate([z.T, np.zeros(((-emb) % 8, length), np.float32)], 0)
    rates = np.abs(np.linspace(math.log(0.01) / 1.5, math.log(0.01) / 0.3, width)).astype(np.float32)[None, :]
    return jnp.asarray(zt), jnp.asarray(rates)


def window(length, rate):
    tnorm = lax.broadcasted_iota(jnp.int32, (length, rate.shape[1]), 0).astype(f32) * (1.0 / (length - 1))
    return jnp.exp(-tnorm * rate)


def sin_cos(x):
    k = jnp.floor(x * (1.0 / math.pi) + 0.5)
    r = x - k * 3.140625
    r = r - k * 0.0009670257568359375
    r = r - k * 6.2771141529083251953e-07
    sign = 1.0 - 2.0 * (k - 2.0 * jnp.floor(k * 0.5))
    q = r * r
    s = 1.0 + q * (-1 / 6 + q * (1 / 120 + q * (-1 / 5040 + q * (1 / 362880 + q * (-1 / 39916800 + q * (1 / 6227020800))))))
    c = 1.0 + q * (-1 / 2 + q * (1 / 24 + q * (-1 / 720 + q * (1 / 40320 + q * (-1 / 3628800 + q * (1 / 479001600 - q * (1 / 87178291200)))))))
    return r * s * sign, c * sign


def column(ref):
    v = as_row(ref)
    n = v.shape[1]
    i = lax.broadcasted_iota(jnp.int32, (n, n), 0)
    j = lax.broadcasted_iota(jnp.int32, (n, n), 1)
    return jnp.sum(jnp.where(i == j, v, 0.0), axis=1, keepdims=True)


def token_masks(seg, length, wide):
    edge = jnp.sum((seg == 0).astype(jnp.int32), axis=1, keepdims=True)
    t = lax.broadcasted_iota(jnp.int32, (length, wide), 0)
    one = jnp.logical_and(t != 0, t != edge)
    two = jnp.logical_and(jnp.logical_and(one, t != 1), t != edge + 1)
    return t < edge, one, two


def specs_of(length, n):
    return ((0, 0, n // 2), (1, n, n // 2), (2, 2 * n, n), (3, 4 * n, n))


def forward_kernel(tok_ref, seg_ref, g1_ref, s1_ref, wg_ref, wi_ref, wv_ref, mb_ref, swg_ref, swi_ref, swv_ref, sb_ref,
        skip_ref, zt_ref, ew_ref, eb_ref, eo_ref, iw_ref, ib_ref, io_ref, ow_ref, ob_ref, oo_ref, fw_ref, rate_ref,
        t0, t3, t1, t2, u0, u3, u1, u2,
        proj_ref, mixed_ref, long_ref, mix_ref, trans_ref, spec_ref, state_ref, nt_ref, normed, padded):
    c = pl.program_id(0)
    r = pl.program_id(1)
    length, width = tok_ref.shape
    n = length // 3
    half = n // 2
    wide = fw_ref.shape[1]
    rows = pl.ds(pl.multiple_of(r * length, length), length)
    tables = ((t0, u0), (t3, u3), (t1, u1), (t2, u2))

    @pl.when(c == 0)
    def _():
        step = 256
        for i in range(length // step):
            part = slice(i * step, (i + 1) * step)
            xhat, _ = norm_stats(tok_ref[part, :].astype(f32))
            low = (xhat * as_row(g1_ref) + as_row(s1_ref)).astype(bf)
            normed[pl.ds(pl.multiple_of(r * length + i * step, step), step), :] = low
            nt_ref[:, part] = low.T

    @pl.when(jnp.logical_and(c == 0, r == 0))
    def _():
        padded[...] = jnp.zeros_like(padded)
        padded[0:ew_ref.shape[0], :] = ew_ref[...]
        pre = tn(padded[...], zt_ref[...], HI) + column(eb_ref)
        e1, c1 = sin_cos(column(eo_ref) * pre)
        state_ref[0] = e1
        state_ref[1] = c1
        state_ref[2] = pre
        pre = tn(iw_ref[...], e1, HI) + column(ib_ref)
        e2, c2 = sin_cos(column(io_ref) * pre)
        state_ref[3] = e2
        state_ref[4] = c2
        state_ref[5] = pre
        pre = tn(ow_ref[...], e2, HI) + column(ob_ref)
        e3, c3 = sin_cos(column(oo_ref) * pre)
        state_ref[6] = e3
        state_ref[7] = c3
        state_ref[8] = pre

    @pl.when(r == 0)
    def _():
        kernel = tn(state_ref[6], fw_ref[...], HI) * window(length, rate_ref[...])
        k = kernel.astype(bf).astype(f32)
        y0, y3, y1, y2 = spread(k[0:n], k[n:2 * n], k[2 * n:])
        first = lax.broadcasted_iota(jnp.int32, (half, wide), 0) == 0
        q0 = nn(t0[...], y0)
        spec_ref[0:half] = q0[0:half] * jnp.where(first, 0.5, 1.0)
        spec_ref[half:n] = jnp.where(first, 0.0, q0[half:])
        spec_ref[6 * n:6 * n + half] = jnp.where(first, 0.5 * q0[half:], q0[0:half])
        spec_ref[n:2 * n] = nn(t3[...], y3)
        spec_ref[2 * n:4 * n] = nn(t1[...], y1)
        spec_ref[4 * n:6 * n] = nn(t2[...], y2)

    edge, one, two = token_masks(seg_ref[pl.ds(r, 1), :], length, wide)
    low = normed[rows, :]
    mixed = []
    for i, (w, sw) in enumerate(((wg_ref, swg_ref), (wi_ref, swi_ref), (wv_ref, swv_ref))):
        at = pl.ds(pl.multiple_of(i * width + c * wide, wide), wide)
        p = nn(low, w[...]) + mb_ref[at].reshape(1, wide)
        proj_ref[i] = p.astype(bf)
        m = (sb_ref[at].reshape(1, wide) + sw[0:1, :] * p + sw[1:2, :] * jnp.where(one, pltpu.roll(p, 1, 0), 0.0)
            + sw[2:3, :] * jnp.where(two, pltpu.roll(p, 2, 0), 0.0))
        mixed_ref[i] = m.astype(bf)
        mixed.append(m)
    inner = mixed[2] * mixed[1]
    inner_low = inner.astype(bf).astype(f32)
    conv = None
    for d in range(DOCS):
        x = jnp.where(edge, inner_low, 0.0) if d == 0 else jnp.where(edge, 0.0, inner_low)
        ys = spread(x[0:n], x[n:2 * n], x[2 * n:])
        parts = []
        for s, off, m in specs_of(length, n):
            t, u = tables[s]
            p = nn(t[...], ys[s])
            trans_ref[0, d, off:off + 2 * m, :] = p.astype(bf)
            pa, pb = p[:m], p[m:]
            qa, qb = spec_ref[off:off + m], spec_ref[off + m:off + 2 * m]
            qc = spec_ref[6 * n:6 * n + m] if s == 0 else qa
            prod = jnp.concatenate([(pa * qa - pb * qb).astype(bf), (pa * qb + pb * qc).astype(bf)], 0)
            parts.append(nn(u[...], prod))
        y = jnp.concatenate(gather(*parts), 0)
        conv = y if d == 0 else jnp.where(edge, conv, y)
    longconv = conv * (1.0 / length) + skip_ref[pl.ds(pl.multiple_of(c * wide, wide), wide)].reshape(1, wide) * inner
    long_ref[...] = longconv.astype(bf)
    mix_ref[...] = (mixed[0] * longconv).astype(bf)


def whole_spec(a):
    return pl.BlockSpec(a.shape, lambda *_: (0,) * a.ndim, pipeline_mode=pl.Buffered(1))


def fixed_spec(*shape):
    return pl.BlockSpec(shape, lambda *_: (0,) * len(shape))


def column_spec(rows, k, count):
    return pl.BlockSpec((rows, CHUNK), lambda c, r: (0, k * count + c))


def part_spec(length):
    return pl.BlockSpec((length, CHUNK), lambda c, r: (r, c))


def stack_spec(count, length):
    return pl.BlockSpec((count, length, CHUNK), lambda c, r: (0, r, c))


def vector_chunk():
    return pl.BlockSpec((CHUNK,), lambda c, r: (c,))


def forward_mixer(tok, segments, g1, s1, wm, mb, sw, sb, skip, filt, zt, rates, tabs, tabst):
    rows_here, length = segments.shape
    total, width = tok.shape
    n = length // 3
    count = width // CHUNK
    fw = filt[-1]
    hidden = fw.shape[0]
    sds = jax.ShapeDtypeStruct
    ins = [tok, segments, g1, s1, wm, wm, wm, mb, sw, sw, sw, sb, skip, zt, *filt, rates, *tabs, *tabst]
    specs = [pl.BlockSpec((length, width), lambda c, r: (jnp.where(c == 0, r, rows_here - 1), 0))]
    specs += [whole_spec(a) for a in (segments, g1, s1)]
    specs += [column_spec(width, k, count) for k in range(3)] + [whole_spec(mb)] + [column_spec(3, k, count) for k in range(3)]
    specs += [whole_spec(sb), whole_spec(skip), whole_spec(zt)] + [whole_spec(a) for a in filt[:-1]]
    specs += [column_spec(hidden, 0, count), column_spec(1, 0, count)] + [whole_spec(a) for a in (*tabs, *tabst)]
    return pl.pallas_call(
        forward_kernel, grid=(count, rows_here), in_specs=specs,
        out_specs=[stack_spec(3, length), stack_spec(3, length), part_spec(length), part_spec(length),
            pl.BlockSpec((1, DOCS, 2 * length, CHUNK), lambda c, r: (r, 0, 0, c)), column_spec(2 * length + n // 2, 0, count),
            fixed_spec(9, hidden, length),
            pl.BlockSpec((width, length), lambda c, r: (0, jnp.where(c == 0, r, rows_here - 1)))],
        out_shape=[sds((3, total, width), bf), sds((3, total, width), bf), sds((total, width), bf), sds((total, width), bf),
            sds((rows_here, DOCS, 2 * length, width), bf), sds((2 * length + n // 2, width), f32),
            sds((9, hidden, length), f32), sds((width, total), bf)],
        scratch_shapes=[pltpu.VMEM((total, width), bf), pltpu.VMEM((zt.shape[0], hidden), f32)],
        compiler_params=pltpu.CompilerParams(vmem_limit_bytes=VMEM_BYTES),
        cost_estimate=pl.CostEstimate(
            flops=total * width * (6 * width + 4 * 2 * 5 * n), bytes_accessed=40 * total * width, transcendentals=0),
        name="mixer_forward")(*ins)


def gelu_parts(e):
    d = 1.0 + (0.3275911 / math.sqrt(2)) * jnp.abs(e)
    t = pl.reciprocal(d, approx=True)
    t = t * (2.0 - d * t)
    bell = jnp.exp(e * e * (-0.5))
    poly = t * (0.5 * 0.254829592 + t * (0.5 * -0.284496736 + t * (0.5 * 1.421413741 + t * (0.5 * -1.453152027 + t * (0.5 * 1.061405429)))))
    tail = poly * bell
    phi = jnp.where(e >= 0, 1.0 - tail, tail)
    return phi, phi + e * bell * (1 / math.sqrt(2 * math.pi))


def mlp_kernel(mix_ref, tok_ref, cot_ref, wo_ref, bo_ref, g2_ref, s2_ref, we_ref, be_ref, wr_ref, br_ref,
        out_ref, dat_ref, wog_ref, weg_ref, wrg_ref, beg_ref, vec_ref, hid, acc, dn2, n2, n2t, cott, act, de):
    j = pl.program_id(0)
    total, width = tok_ref.shape
    part_ff = we_ref.shape[1]
    step = 512
    steps = total // step

    def at(i, size=step):
        return pl.ds(pl.multiple_of(i * size, size), size)

    @pl.when(j == 0)
    def _():
        def body(i, carry):
            rows = at(i)
            h = tok_ref[rows, :].astype(f32) + nn(mix_ref[rows, :], wo_ref[...]) + as_row(bo_ref)
            hid[rows, :] = h
            xhat, _ = norm_stats(h)
            n2[rows, :] = (xhat * as_row(g2_ref) + as_row(s2_ref)).astype(bf)
            acc[rows, :] = h + as_row(br_ref)
            dn2[rows, :] = jnp.zeros((step, width), f32)
            return carry

        lax.fori_loop(0, steps, body, 0)
        for i in range(steps):
            rows = slice(i * step, (i + 1) * step)
            n2t[:, rows] = n2[rows, :].T
            cott[:, rows] = cot_ref[rows, :].T

    def tile(i, carry):
        rows = at(i)
        e = nn(n2[rows, :], we_ref[...]) + be_ref[pl.ds(pl.multiple_of(j * part_ff, part_ff), part_ff)].reshape(1, part_ff)
        da = nt(cot_ref[rows, :], wr_ref[...])
        phi, slope = gelu_parts(e)
        a = (e * phi).astype(bf)
        d = (da * slope).astype(bf)
        act[rows, :] = a
        de[rows, :] = d
        acc[rows, :] += nn(a, wr_ref[...])
        dn2[rows, :] += nt(d, we_ref[...])
        return carry + sum0(d.astype(f32))

    beg_ref[...] = lax.fori_loop(0, steps, tile, jnp.zeros((1, part_ff), f32))

    def grads(i, carry):
        rows = at(i, 256)
        back = nn(cott[rows, :], act[...]).astype(bf).T
        for h in range(256 // LANES):
            wrg_ref[i * (256 // LANES) + h] = back[:, h * LANES:(h + 1) * LANES]
        ahead = nn(n2t[rows, :], de[...]).astype(bf)
        for h in range(part_ff // LANES):
            weg_ref[h, rows, :] = ahead[:, h * LANES:(h + 1) * LANES]
        return carry

    lax.fori_loop(0, width // 256, grads, 0)

    @pl.when(j == pl.num_programs(0) - 1)
    def _():
        def body(i, carry):
            rows = at(i)
            out_ref[rows, :] = acc[rows, :].astype(bf)
            xhat, scale = norm_stats(hid[rows, :])
            dn = dn2[rows, :]
            gd = dn * as_row(g2_ref)
            m1 = jnp.mean(gd, axis=-1, keepdims=True)
            m2 = jnp.mean(gd * xhat, axis=-1, keepdims=True)
            cot = cot_ref[rows, :].astype(f32)
            low = (cot + scale * (gd - m1 - xhat * m2)).astype(bf)
            dat_ref[rows, :] = low
            return (carry[0] + sum0(dn * xhat), carry[1] + sum0(dn), carry[2] + sum0(low.astype(f32)), carry[3] + sum0(cot))

        zero = jnp.zeros((1, width), f32)
        sums = lax.fori_loop(0, steps, body, (zero,) * 4)
        for k in range(4):
            vec_ref[k:k + 1, :] = sums[k]
        for i in range(steps):
            rows = slice(i * step, (i + 1) * step)
            n2t[:, rows] = mix_ref[rows, :].T

        def weights(i, carry):
            rows = at(i, 256)
            part = nn(n2t[rows, :], dat_ref[...]).astype(bf)
            for h in range(width // LANES):
                wog_ref[h, rows, :] = part[:, h * LANES:(h + 1) * LANES]
            return carry

        lax.fori_loop(0, width // 256, weights, 0)


def mlp(mix, tok, cot, wo, bo, g2, s2, we, be, wr, br, part_ff=1024):
    total, width = tok.shape
    ff = we.shape[1]
    part_ff = min(part_ff, ff)
    sds = jax.ShapeDtypeStruct
    blocks = width // LANES
    return pl.pallas_call(
        mlp_kernel, grid=(ff // part_ff,),
        in_specs=[whole_spec(a) for a in (mix, tok, cot, wo, bo, g2, s2)]
            + [pl.BlockSpec((width, part_ff), lambda j: (0, j)), whole_spec(be), pl.BlockSpec((part_ff, width), lambda j: (j, 0)),
                whole_spec(br)],
        out_specs=[fixed_spec(total, width), fixed_spec(total, width), fixed_spec(blocks, width, LANES),
            pl.BlockSpec((part_ff // LANES, width, LANES), lambda j: (j, 0, 0)),
            pl.BlockSpec((blocks, part_ff, LANES), lambda j: (0, j, 0)), pl.BlockSpec((1, part_ff), lambda j: (0, j)),
            fixed_spec(8, width)],
        out_shape=[sds((total, width), bf), sds((total, width), bf), sds((blocks, width, LANES), bf),
            sds((ff // LANES, width, LANES), bf), sds((blocks, ff, LANES), bf), sds((1, ff), f32), sds((8, width), f32)],
        scratch_shapes=[pltpu.VMEM((total, width), f32)] * 3 + [pltpu.VMEM((total, width), bf)]
            + [pltpu.VMEM((width, total), bf)] * 2 + [pltpu.VMEM((total, part_ff), bf)] * 2,
        compiler_params=pltpu.CompilerParams(vmem_limit_bytes=VMEM_BYTES),
        cost_estimate=pl.CostEstimate(
            flops=12 * total * width * ff + 4 * total * width * width, bytes_accessed=30 * total * width,
            transcendentals=total * ff),
        name="mlp")(mix, tok, cot, wo, bo, g2, s2, we, be, wr, br)


def backward_kernel(dat_ref, tok_ref, seg_ref, g1_ref, wo_ref, long_ref, mixed_ref, proj_ref, trans_ref, spec_ref, nt_ref,
        wg_ref, wi_ref, wv_ref, swg_ref, swi_ref, swv_ref, skip_ref, state_ref, zt_ref, iw_ref, ow_ref, eo_ref, io_ref,
        oo_ref, fw_ref, rate_ref, t0, t3, t1, t2, u0, u3, u1, u2,
        tg_ref, wgrad_ref, sg_ref, vec_ref, gew_ref, giw_ref, gow_ref, gfw_ref, gsm_ref, dn, de3, dp_s, ds_s):
    c = pl.program_id(0)
    r = pl.program_id(1)
    chunks = pl.num_programs(0)
    last_row = pl.num_programs(1) - 1
    length, wide = long_ref.shape
    n = length // 3
    half = n // 2
    rows = pl.ds(pl.multiple_of(r * length, length), length)
    tables = ((t0, u0), (t3, u3), (t1, u1), (t2, u2))

    @pl.when(r == 0)
    def _():
        ds_s[...] = jnp.zeros_like(ds_s)
        sg_ref[...] = jnp.zeros_like(sg_ref)

    @pl.when(jnp.logical_and(c == 0, r == 0))
    def _():
        dn[...] = jnp.zeros_like(dn)
        de3[...] = jnp.zeros_like(de3)
        vec_ref[...] = jnp.zeros_like(vec_ref)

    def add(off, v):
        ds_s[off:off + v.shape[0], :] += v

    edge, one, two = token_masks(seg_ref[pl.ds(r, 1), :], length, wide)
    dm = nt(dat_ref[rows, :], wo_ref[...])
    gate_out = mixed_ref[0].astype(f32)
    gate_in = mixed_ref[1].astype(f32)
    value = mixed_ref[2].astype(f32)
    d_gate = dm * long_ref[...].astype(f32)
    d_long = dm * gate_out
    sg_ref[0, 5:6, :] += sum0(d_long * (value * gate_in))
    d_conv = None
    for d in range(DOCS):
        x = jnp.where(edge, d_long, 0.0) if d == 0 else jnp.where(edge, 0.0, d_long)
        ys = spread(x[0:n], x[n:2 * n], x[2 * n:])
        parts = []
        for s, off, m in specs_of(length, n):
            t, u = tables[s]
            g = nn(t[...], ys[s])
            ga, gb = g[:m], g[m:]
            qa, qb = spec_ref[off:off + m], spec_ref[off + m:off + 2 * m]
            qc = spec_ref[6 * n:6 * n + m] if s == 0 else qa
            pa, pb = trans_ref[0, d, off:off + m, :].astype(f32), trans_ref[0, d, off + m:off + 2 * m, :].astype(f32)
            back = jnp.concatenate([(ga * qa + gb * qb).astype(bf), (gb * qc - ga * qb).astype(bf)], 0)
            if s == 0:
                add(0, ga * pa)
                add(6 * n, gb * pb)
            else:
                add(off, ga * pa + gb * pb)
            add(off + m, gb * pa - ga * pb)
            parts.append(nn(u[...], back))
        y = jnp.concatenate(gather(*parts), 0)
        d_conv = y if d == 0 else jnp.where(edge, d_conv, y)
    d_inner = skip_ref[pl.ds(pl.multiple_of(c * wide, wide), wide)].reshape(1, wide) * d_long + d_conv * (1.0 / length)
    grads = (d_gate, d_inner * value, d_inner * gate_in)
    for i, (dmx, w, sw) in enumerate(zip(grads, (wg_ref, wi_ref, wv_ref), (swg_ref, swi_ref, swv_ref))):
        a1 = pltpu.roll(jnp.where(one, dmx, 0.0), length - 1, 0)
        a2 = pltpu.roll(jnp.where(two, dmx, 0.0), length - 2, 0)
        dp = (sw[0:1, :] * dmx + sw[1:2, :] * a1 + sw[2:3, :] * a2).astype(bf)
        p = proj_ref[i].astype(f32)
        for k, v in enumerate((p * dmx, p * a1, p * a2, dmx, dp.astype(f32))):
            sg_ref[i, k:k + 1, :] += sum0(v)
        dp_s[i, rows, :] = dp
        dn[rows, :] += nt(dp, w[...])

    @pl.when(r == last_row)
    def _():
        for i in range(3):
            part = nn(nt_ref[...], dp_s[i]).astype(bf)
            for h in range(wide // LANES):
                wgrad_ref[i, h] = part[:, h * LANES:(h + 1) * LANES]
        first = lax.broadcasted_iota(jnp.int32, (half, wide), 0) == 0
        extra = ds_s[6 * n:6 * n + half]
        ds_s[0:half] = jnp.where(first, 0.5, 1.0) * (ds_s[0:half] + jnp.where(first, 0.0, extra))
        ds_s[half:n] = jnp.where(first, 0.5 * extra, ds_s[half:n])
        parts = [nn(tables[s][1][...], (ds_s[off:off + 2 * m] * (1.0 / length)).astype(bf)) for s, off, m in specs_of(length, n)]
        gk = jnp.concatenate(gather(*parts), 0) * window(length, rate_ref[...])
        gfw_ref[...] = nn(state_ref[6], gk, HI)
        de3[...] += nt(fw_ref[...], gk, HI)

    @pl.when(c == chunks - 1)
    def _():
        step = 256
        g1 = as_row(g1_ref)
        for i in range(length // step):
            part = slice(i * step, (i + 1) * step)
            there = pl.ds(pl.multiple_of(r * length + i * step, step), step)
            xhat, scale = norm_stats(tok_ref[part, :].astype(f32))
            d = dn[there, :]
            gd = d * g1
            a = jnp.mean(gd, axis=-1, keepdims=True)
            b = jnp.mean(gd * xhat, axis=-1, keepdims=True)
            tg_ref[part, :] = (dat_ref[there, :].astype(f32) + scale * (gd - a - xhat * b)).astype(bf)
            vec_ref[0:1, :] += sum0(d * xhat)
            vec_ref[1:2, :] += sum0(d)

    @pl.when(jnp.logical_and(c == chunks - 1, r == last_row))
    def _():
        ones = jnp.ones((8, length), f32)
        flat = lambda v: nt(ones, v, HI)
        g = de3[...] * state_ref[7]
        gsm_ref[0] = flat(g * state_ref[8])
        g = g * column(oo_ref)
        gsm_ref[1] = flat(g)
        gow_ref[...] = nt(state_ref[3], g, HI)
        g = nn(ow_ref[...], g, HI) * state_ref[4]
        gsm_ref[2] = flat(g * state_ref[5])
        g = g * column(io_ref)
        gsm_ref[3] = flat(g)
        giw_ref[...] = nt(state_ref[0], g, HI)
        g = nn(iw_ref[...], g, HI) * state_ref[1]
        gsm_ref[4] = flat(g * state_ref[2])
        g = g * column(eo_ref)
        gsm_ref[5] = flat(g)
        gew_ref[...] = nt(zt_ref[...], g, HI)


def backward_mixer(dat, tok, segments, g1, wo, longc, mixed, proj, trans, spec, ntr, wm, sw, skip, state, filt, zt, rates,
        tabs, tabst):
    rows_here, length = segments.shape
    total, width = tok.shape
    n = length // 3
    count = width // CHUNK
    ew, eb, eo, iw, ib, io, ow, ob, oo, fw = filt
    hidden = fw.shape[0]
    sds = jax.ShapeDtypeStruct
    late = lambda c, r: (jnp.where(c == count - 1, r, 0), 0)
    ins = [dat, tok, segments, g1, wo, longc, mixed, proj, trans, spec, ntr, wm, wm, wm, sw, sw, sw, skip, state, zt,
        iw, ow, eo, io, oo, fw, rates, *tabs, *tabst]
    specs = [whole_spec(dat), pl.BlockSpec((length, width), late), whole_spec(segments), whole_spec(g1),
        pl.BlockSpec((CHUNK, width), lambda c, r: (c, 0)), part_spec(length), stack_spec(3, length), stack_spec(3, length),
        pl.BlockSpec((1, DOCS, 2 * length, CHUNK), lambda c, r: (r, 0, 0, c)), column_spec(2 * length + n // 2, 0, count),
        whole_spec(ntr)]
    specs += [column_spec(width, k, count) for k in range(3)] + [column_spec(3, k, count) for k in range(3)]
    specs += [whole_spec(a) for a in (skip, state, zt, iw, ow, eo, io, oo)]
    specs += [column_spec(hidden, 0, count), column_spec(1, 0, count)] + [whole_spec(a) for a in (*tabs, *tabst)]
    return pl.pallas_call(
        backward_kernel, grid=(count, rows_here), in_specs=specs,
        out_specs=[pl.BlockSpec((length, width), late),
            pl.BlockSpec((3, CHUNK // LANES, width, LANES), lambda c, r: (0, c, 0, 0)),
            pl.BlockSpec((3, 8, CHUNK), lambda c, r: (0, 0, c)), fixed_spec(8, width), fixed_spec(zt.shape[0], hidden),
            fixed_spec(hidden, hidden), fixed_spec(hidden, hidden), column_spec(hidden, 0, count), fixed_spec(6, 8, hidden)],
        out_shape=[sds((total, width), bf), sds((3, width // LANES, width, LANES), bf), sds((3, 8, width), f32),
            sds((8, width), f32), sds((zt.shape[0], hidden), f32), sds((hidden, hidden), f32), sds((hidden, hidden), f32),
            sds((hidden, width), f32), sds((6, 8, hidden), f32)],
        scratch_shapes=[pltpu.VMEM((total, width), f32), pltpu.VMEM((hidden, length), f32), pltpu.VMEM((3, total, CHUNK), bf),
            pltpu.VMEM((6 * n + n // 2, CHUNK), f32)],
        compiler_params=pltpu.CompilerParams(vmem_limit_bytes=VMEM_BYTES),
        cost_estimate=pl.CostEstimate(
            flops=total * width * (14 * width + 4 * 2 * 5 * n), bytes_accessed=50 * total * width, transcendentals=0),
        name="mixer_backward")(*ins)


def bits_of(n):
    return n.bit_length() - 1


def order_of(rows_n, pos_n, first):
    rows = [("rows", b) for b in range(1, bits_of(rows_n))]
    pos = [("pos", b) for b in range(bits_of(pos_n))]
    return [("rows", 0)] + (pos + rows if first == "pos" else rows[:1] + pos + rows[1:])


def scatter_blocks(grad, rows_n, pos_n, first):
    blocks, height, wide = grad.shape
    if blocks % pos_n:
        flat = grad.transpose(1, 0, 2).reshape(height, blocks * wide)
        wide = blocks * wide // pos_n
        blocks = pos_n
        grad = flat.reshape(height, blocks, wide).transpose(1, 0, 2)
    high = height // rows_n
    rbits, pbits = bits_of(rows_n), bits_of(pos_n)
    acc = grad.reshape((2,) * pbits + (blocks // pos_n,) + (2,) * rbits + (high, wide))
    alive = [("pos", b) for b in reversed(range(pbits))] + [None] + [("rows", b) for b in reversed(range(rbits))]
    for axis, bit in order_of(rows_n, pos_n, first):
        dim = alive.index((axis, bit))
        mine = (lax.axis_index(axis) >> bit) & 1
        size = rows_n if axis == "rows" else pos_n
        send = lax.dynamic_index_in_dim(acc, 1 - mine, dim, keepdims=False)
        keep = lax.dynamic_index_in_dim(acc, mine, dim, keepdims=False)
        got = lax.ppermute(send, axis, [(i, i ^ (1 << bit)) for i in range(size)])
        acc = (keep.astype(f32) + got.astype(f32)).astype(bf)
        alive.pop(dim)
    return acc


def pack_places(width, hidden, emb, ff):
    per = width // PACK
    at = {"filter": 0, "square": hidden * per}
    row = at["square"] + hidden
    for name, vectors in (("vec1", 2), ("vec2", 4), ("sgrad", 15), ("skip", 1), ("ebias", ff // width)):
        at[name] = row
        row += vectors * per
    at["small"] = row
    return at, row + 6


def pack_small(at, pk, beg, vec2, sgrad, vec1, gew, giw, gow, gfw, gsm):
    width = vec1.shape[1]
    hidden = giw.shape[0]
    per = width // PACK

    def put(row, value):
        for h in range(per):
            pk[row + h:row + h + 1, :] = value[:, h * PACK:(h + 1) * PACK]

    for k in range(beg.shape[1] // width):
        put(at["ebias"] + k * per, beg[:, k * width:(k + 1) * width])
    for k in range(4):
        put(at["vec2"] + k * per, vec2[k:k + 1, :])
    for i in range(3):
        for k in range(5):
            put(at["sgrad"] + (i * 5 + k) * per, sgrad[i, k:k + 1, :])
    put(at["skip"], sgrad[0, 5:6, :])
    for k in range(2):
        put(at["vec1"] + k * per, vec1[k:k + 1, :])
    for lane, ref in ((0, gew), (128, giw), (256, gow)):
        high = min(ref.shape[0], hidden)
        pk[at["square"]:at["square"] + high, lane:lane + hidden] = ref[0:high, :]
    for h in range(per):
        pk[at["filter"] + h * hidden:at["filter"] + (h + 1) * hidden, :] = gfw[:, h * PACK:(h + 1) * PACK]
    for k in range(6):
        pk[at["small"] + k:at["small"] + k + 1, 0:hidden] = gsm[k, 0:1, :]


class Halving:
    def __init__(self, ref, blocks, alive, order, got, sums, send_sem, recv_sem):
        self.ref, self.blocks, self.alive, self.order = ref, blocks, list(alive), order
        self.got, self.sums, self.send_sem, self.recv_sem = got, sums, send_sem, recv_sem
        self.copy = None

    def pick(self, dim, which):
        start, count = self.blocks
        index = [slice(None)] * len(self.alive)
        index[self.alive.index(None)] = pl.ds(start, count)
        index[dim] = which
        return tuple(index)

    def start(self, stage):
        axis, bit = self.order[stage]
        dim = self.alive.index((axis, bit))
        place = lax.axis_index(axis)
        mine = (place // (1 << bit)) % 2
        self.keep = self.pick(dim, mine)
        self.copy = pltpu.make_async_remote_copy(
            src_ref=self.ref.at[self.pick(dim, 1 - mine)], dst_ref=self.got[stage], send_sem=self.send_sem.at[stage],
            recv_sem=self.recv_sem.at[stage], device_id={axis: place + (1 - 2 * mine) * (1 << bit)}, device_id_type=MESH)
        self.copy.start()
        self.alive.pop(dim)

    def finish(self, stage):
        self.copy.wait()
        kept, got, out = self.ref.at[self.keep], self.got[stage], self.sums[stage]
        split = self.alive.index(None)

        def add(lead):
            def body(b, carry):
                at = lead + (b,)
                out[at] = (kept[at].astype(f32) + got[at].astype(f32)).astype(bf)
                return carry

            lax.fori_loop(0, self.blocks[1], body, 0)

        leads = [()]
        for d in range(split):
            leads = [lead + (k,) for lead in leads for k in range(2)]
        for lead in leads:
            add(lead)
        self.ref, self.blocks = out, (0, self.blocks[1])


def job_shapes(shape, blocks, alive, order):
    dims = list(alive)
    now = [blocks if d is None else 2 for d in dims] + list(shape[-2:])
    out = []
    for step in order:
        k = dims.index(step)
        dims.pop(k)
        now.pop(k)
        out.append(tuple(now))
    return out


def exchange_kernel(sizes, at, plan, count, *refs):
    rows_n, pos_n = sizes
    n = rows_n * pos_n
    small = refs[:9]
    grads = refs[9:9 + count]
    pos = 9 + count
    packed_out = refs[pos]
    outs = refs[pos + 1:pos + 1 + len(plan)]
    scratch = list(refs[pos + 1 + len(plan):])
    pk, rbuf, red, gath, ss1, rs1, ss2, rs2 = scratch[:8]
    rest = scratch[8:]
    jobs = []
    for (src, blocks, alive, order), out in zip(plan, outs):
        m = len(order)
        got, sums = rest[:m], rest[m:2 * m - 1] + [out]
        jobs.append(Halving(grads[src], blocks, alive, order, got, sums, rest[2 * m - 1], rest[2 * m]))
        rest = rest[2 * m + 1:]
    me = lax.axis_index("rows") * pos_n + lax.axis_index("pos")
    chunk = pk.shape[0] // n

    def ident(t):
        return {"rows": t // pos_n, "pos": t % pos_n}

    def each(f):
        def body(k, carry):
            f(lax.rem(me + k, n))
            return carry

        lax.fori_loop(1, n, body, 0)

    def part(t):
        return pl.ds(pl.multiple_of(t * chunk, chunk), chunk)

    barrier = pltpu.get_barrier_semaphore()
    each(lambda t: pl.semaphore_signal(barrier, inc=1, device_id=ident(t), device_id_type=MESH))
    pk[...] = jnp.zeros_like(pk)
    pack_small(at, pk, *small)
    pl.semaphore_wait(barrier, n - 1)

    def scatter(t, slot):
        return pltpu.make_async_remote_copy(
            src_ref=pk.at[part(t), :], dst_ref=rbuf.at[slot], send_sem=ss1.at[t], recv_sem=rs1.at[slot], device_id=ident(t),
            device_id_type=MESH)

    def publish(t, slot):
        return pltpu.make_async_remote_copy(
            src_ref=red, dst_ref=gath.at[part(slot), :], send_sem=ss2.at[t], recv_sem=rs2.at[slot], device_id=ident(t),
            device_id_type=MESH)

    for job in jobs:
        job.start(0)
    each(lambda t: scatter(t, me).start())
    rbuf[me] = pk[part(me), :]
    stages = max(len(job.order) for job in jobs)
    for stage in range(stages):
        for job in jobs:
            if stage < len(job.order):
                job.finish(stage)
                if stage + 1 < len(job.order):
                    job.start(stage + 1)
        if stage == 0:
            each(lambda t: scatter(t, t).wait())
            total = rbuf[0]
            for s in range(1, n):
                total = total + rbuf[s]
            red[...] = total
            gath[part(me), :] = total
            each(lambda t: publish(t, me).start())
    each(lambda t: publish(t, t).wait())
    packed_out[...] = gath[...]


def exchange(sizes, at, used, small, grads, plan):
    rows_n, pos_n = sizes
    n = rows_n * pos_n
    total = -(-used // (8 * n)) * 8 * n
    chunk = total // n
    vm = pl.BlockSpec(memory_space=pltpu.VMEM)
    scratch = [pltpu.VMEM((total, PACK), f32), pltpu.VMEM((n, chunk, PACK), f32), pltpu.VMEM((chunk, PACK), f32),
        pltpu.VMEM((total, PACK), f32)] + [pltpu.SemaphoreType.DMA((n,))] * 4
    shapes = [jax.ShapeDtypeStruct((total, PACK), f32)]
    for src, (start, blocks), alive, order in plan:
        left = job_shapes(grads[src].shape, blocks, alive, order)
        shapes.append(jax.ShapeDtypeStruct(left[-1], bf))
        scratch += [pltpu.VMEM(s, bf) for s in left] + [pltpu.VMEM(s, bf) for s in left[:-1]]
        scratch += [pltpu.SemaphoreType.DMA((len(order),))] * 2
    return pl.pallas_call(
        functools.partial(exchange_kernel, sizes, at, plan, len(grads)), out_shape=shapes,
        in_specs=[vm] * (9 + len(grads)), out_specs=[vm] * len(shapes), scratch_shapes=scratch,
        compiler_params=pltpu.CompilerParams(collective_id=0, has_side_effects=True, vmem_limit_bytes=VMEM_BYTES),
        name="exchange")(*small, *grads)


def unpack(at, packed, blocks, width, hidden, emb, ff):
    per = width // PACK
    counts = [len(parts) for parts in blocks]
    flat = [p for parts in blocks for p in parts]

    def kernel(pk, *refs):
        ins = list(refs[:len(flat)])
        fg, fs, mb, sw, sb, ew, eb, eo, iw, ib, io, ow, ob, oo, fw, sk, obias, sg, ss, eb2, rb = refs[len(flat):len(flat) + 21]
        outs = refs[len(flat) + 21:]

        def get(ref, lane, row):
            for h in range(per):
                ref[lane + h * PACK:lane + (h + 1) * PACK] = pk[row + h, :]

        get(fg, 0, at["vec1"])
        get(fs, 0, at["vec1"] + per)
        for i in range(3):
            base = at["sgrad"] + i * 5 * per
            for k in range(3):
                for h in range(per):
                    lane = i * width + h * PACK
                    sw[k:k + 1, lane:lane + PACK] = pk[base + k * per + h:base + k * per + h + 1, :]
            get(sb, i * width, base + 3 * per)
            get(mb, i * width, base + 4 * per)
        q = at["square"]
        ew[...] = pk[q:q + emb, 0:hidden]
        iw[...] = pk[q:q + hidden, 128:128 + hidden]
        ow[...] = pk[q:q + hidden, 256:256 + hidden]
        for k, ref in enumerate((oo, ob, io, ib, eo, eb)):
            ref[...] = pk[at["small"] + k, 0:hidden]
        for h in range(per):
            fw[:, h * PACK:(h + 1) * PACK] = pk[at["filter"] + h * hidden:at["filter"] + (h + 1) * hidden, :]
        get(sk, 0, at["skip"])
        for k, ref in enumerate((sg, ss, obias, rb)):
            get(ref, 0, at["vec2"] + k * per)
        for k in range(ff // width):
            get(eb2, k * width, at["ebias"] + k * per)
        for parts, out in zip(counts, outs):
            lane = 0
            for _ in range(parts):
                src = ins.pop(0)
                for b in range(src.shape[0]):
                    out[:, lane:lane + src.shape[2]] = src[b].astype(f32)
                    lane += src.shape[2]

    s = lambda *d: jax.ShapeDtypeStruct(d, f32)
    shapes = [s(width), s(width), s(3 * width), s(3, 3 * width), s(3 * width), s(emb, hidden), s(hidden), s(hidden),
        s(hidden, hidden), s(hidden), s(hidden), s(hidden, hidden), s(hidden), s(hidden), s(hidden, width), s(width), s(width),
        s(width), s(width), s(ff), s(width)]
    shapes += [s(parts[0].shape[1], sum(p.shape[0] for p in parts) * parts[0].shape[2]) for parts in blocks]
    vm = pl.BlockSpec(memory_space=pltpu.VMEM)
    return pl.pallas_call(
        kernel, out_shape=shapes, in_specs=[vm] * (1 + len(flat)), out_specs=[vm] * len(shapes), name="unpack")(packed, *flat)


def on_device(sizes, tokens, segments, cotangent, first_gain, first_shift, mixer_weight, mixer_bias, short_weight, short_bias,
        embed_weight, embed_bias, embed_omega, inner_weight, inner_bias, inner_omega, outer_weight, outer_bias, outer_omega,
        filter_weight, skip_gain, output_weight, output_bias, second_gain, second_shift, expand_weight, expand_bias,
        reduce_weight, reduce_bias):
    rows_n, pos_n = sizes
    length, width = tokens.shape[1:]
    emb, hidden = embed_weight.shape
    ff = expand_weight.shape[1]
    tok = tokens.reshape(-1, width)
    cot = cotangent.reshape(-1, width)
    filt = [embed_weight, embed_bias, embed_omega, inner_weight, inner_bias, inner_omega, outer_weight, outer_bias, outer_omega,
        filter_weight]
    tabs, tabst = radix_tables(length)
    zt, rates = filter_inputs(length, emb, width)
    proj, mixed, longc, mix, trans, spec, state, ntr = forward_mixer(
        tok, segments, first_gain, first_shift, mixer_weight, mixer_bias, short_weight, short_bias, skip_gain, filt, zt, rates,
        tabs, tabst)
    out, dat, wog, weg, wrg, beg, vec2 = mlp(
        mix, tok, cot, output_weight, output_bias, second_gain, second_shift, expand_weight, expand_bias, reduce_weight,
        reduce_bias)
    tgrad, wmg, sgrad, vec1, gew, giw, gow, gfw, gsm = backward_mixer(
        dat, tok, segments, first_gain, output_weight, longc, mixed, proj, trans, spec, ntr, mixer_weight, short_weight,
        skip_gain, state, filt, zt, rates, tabs, tabst)
    wmg = wmg.reshape(3 * width // LANES, width, LANES)
    grads = [wmg, wog, weg, wrg]
    small = (beg, vec2, sgrad, vec1, gew, giw, gow, gfw, gsm)
    at, used = pack_places(width, hidden, emb, ff)
    direct = rows_n * pos_n <= 32 and all(g.shape[0] % pos_n == 0 and g.shape[1] % (16 * rows_n) == 0 for g in grads)
    if direct:
        rbits, pbits = bits_of(rows_n), bits_of(pos_n)
        alive = [("pos", b) for b in reversed(range(pbits))] + [None] + [("rows", b) for b in reversed(range(rbits))]
        grads = [g.reshape((2,) * pbits + (g.shape[0] // pos_n,) + (2,) * rbits + (g.shape[1] // rows_n, LANES)) for g in grads]
        by_pos, by_rows = order_of(rows_n, pos_n, "pos"), order_of(rows_n, pos_n, "rows")
        count = [g.shape[pbits] for g in grads]
        cut = (count[0] + 1) // 2
        plan = [(0, (0, cut), alive, by_pos), (0, (cut, count[0] - cut), alive, by_rows), (1, (0, count[1]), alive, by_rows),
            (2, (0, count[2]), alive, by_pos), (3, (0, count[3]), alive, by_rows)]
        packed, m_a, m_b, o_part, e_part, r_part = exchange(sizes, at, used, small, grads, plan)
        blocks = [[m_a, m_b], [o_part], [e_part], [r_part]]
    else:
        packed = lax.psum(pack_only(at, used, small), ("rows", "pos"))
        blocks = [[scatter_blocks(g, rows_n, pos_n, f)] for g, f in zip(grads, ("pos", "rows", "pos", "rows"))]
    (fg, fs, mb, sw, sb, ew, eb, eo, iw, ib, io, ow, ob, oo, fw, sk, obias, sg, ss, eb2, rb, m_grad, o_grad, e_grad, r_grad) = unpack(
        at, packed, blocks, width, hidden, emb, ff)
    return (out.reshape(tokens.shape), tgrad.reshape(tokens.shape), fg, fs, m_grad, mb, sw, sb, ew, eb, eo, iw, ib, io, ow, ob,
        oo, fw, sk, o_grad, obias, sg, ss, e_grad, eb2, r_grad, rb)


def pack_only(at, used, small):
    def kernel(*refs):
        refs[-1][...] = jnp.zeros_like(refs[-1])
        pack_small(at, refs[-1], *refs[:-1])

    vm = pl.BlockSpec(memory_space=pltpu.VMEM)
    return pl.pallas_call(
        kernel, out_shape=jax.ShapeDtypeStruct((used, PACK), f32), in_specs=[vm] * len(small), out_specs=vm, name="pack")(*small)


def solution(mesh):
    both = ("rows", "pos")
    split = P(both, None, None)
    grid = P("rows", "pos")
    in_specs = (split, P(both, None), split) + (P(),) * 25
    out_specs = (split, split, P(), P(), grid) + (P(),) * 14 + (grid, P(), P(), P(), grid, P(), grid, P())
    sizes = (mesh.shape["rows"], mesh.shape["pos"])
    return jax.shard_map(
        functools.partial(on_device, sizes), mesh=mesh, in_specs=in_specs, out_specs=out_specs, check_vma=False)
```

time: 1260 us -> 303 us (0.24)
  waiting for transfers between devices: 556 us -> 0 us
  Pallas kernels: 0 us -> 302 us
  matrix products: 301 us -> 0 us
  other arithmetic: 251 us -> 0 us
  local copies, waits for them, and re-layouts: 125 us -> 0 us
  between operations: 17.1 us -> 0.87 us
    pallas_call x0 -> x5, Pallas kernels: none -> 302 us  [the longest x1 113 us: exchange(): pl.pallas_call(functools.partial(exchange_kernel, sizes, at, plan, len(gr...]
    dot_general x53 -> x0, matrix products: 301 us -> none  [the longest x2 55.8 us: on_device(): jnp.einsum('rld,df->rlf', normed2_low, expand_weight, preferred_element_t...]
    psum x2 -> x0, waiting for transfers between devices: 294 us -> none  [on_device(): lax.psum((first_gain_grad, first_shift_grad, mixer_bias_grad, short_weigh...]
    reduce_scatter x9 -> x0, waiting for transfers between devices: 261 us -> none  [the longest x1 110 us: on_device(): lax.psum_scatter(matrices[2], 'rows', scatter_dimension=0, tiled=True)]
    unnamed x545 -> x0, local copies, waits for them, and re-layouts: 84.8 us -> none
    reduce_sum x20 -> x0, other arithmetic: 71.8 us -> none  [the longest x2 18.7 us: short_conv(): result = result + short_weight[delay] * moved * same[:, :, delay:delay + 1]]
    add_any x4 -> x0, other arithmetic: 37.9 us -> none  [spectral_product(): real = real_one * real_two - imag_one * imag_two]
    concatenate x7 -> x0, other arithmetic: 36.3 us -> none  [the longest x3 21.3 us: spectral_product(): return jnp.concatenate([real, imag[..., 1:length, :]], axis=-2)]
  transfers between devices with their start and end apart: 12 -> 0, of which waited for: 7 -> 0; matrix products, arithmetic and copies ran while one was open for 29% -> 0% of each run, Pallas kernels for 0% -> 0%
where the time goes in v2:
time: 303 us
  Pallas kernels  302 us (100%)
    pallas_call x1, Pallas kernels, exchange(): pl.pallas_call(functools.partial(exchange_kernel, sizes, at, plan, len(gr...  113 us
    pallas_call x1, Pallas kernels, mlp(): pl.pallas_call(mlp_kernel, grid=(ff // part_ff,), in_specs=[whole_spec(a)...  76.6 us
    pallas_call x1, Pallas kernels, backward_mixer(): pl.pallas_call(backward_kernel, grid=(count, rows_here), in_specs=specs,...  62.9 us
    pallas_call x1, Pallas kernels, forward_mixer(): pl.pallas_call(forward_kernel, grid=(count, rows_here), in_specs=specs, o...  47.7 us

profile of v2, /device:TPU:0, one launch (start us, length us, event | category | flops | bytes accessed | tf_op | source)
XLA Modules:
  0.0 303.0 jit_solution(6498591179018709383)
XLA Ops:
  0.7 47.7 %mixer_forward.1 = (bf16[3,1536,768]{2,1,0:T(8,128)(2,1)}, bf16[3,1536,768]{2,1,0:T(8,128)(2,1)}, bf16[1536,768]{1,0:T(8,128)(2,1)}, bf16[1536,768]{1,0:T(8,128)...) custom-call(bf16[1536,768]{1,0:T(8,128)(2,1)} %bitcast.13, ...), custom_call_target="tpu_custom_call" | custom-call | flops 17515413504 | bytes 47185920 | tf_op jit(solution)/shard_map/mixer_forward/pallas_call | solution.py:275
  48.4 76.6 %mlp.1 = (bf16[1536,768]{1,0:T(8,128)(2,1)}, bf16[1536,768]{1,0:T(8,128)(2,1)}, bf16[6,768,128]{2,1,0:T(8,128)(2,1)}, bf16[24,768,128]{2,1,0:T(8,128)(2,1)}, bf1...) custom-call(bf16[1536,768]{1,0:T(8,128)(2,1)} %get-tuple-element.82.mix_ref, ...), custom_call_target="tpu_custom_call" | custom-call | flops 47110422528 | bytes 35389440 | tf_op jit(solution)/shard_map/mlp/pallas_call | solution.py:397
  125.0 62.9 %mixer_backward.1 = (bf16[1536,768]{1,0:T(8,128)(2,1)}, bf16[3,6,768,128]{3,2,1,0:T(8,128)(2,1)}, f32[3,8,768]{2,1,0:T(8,128)}, f32[8,768]{1,0:T(8,128)}, f32[40...) custom-call(bf16[1536,768]{1,0:T(8,128)(2,1)} %get-tuple-element.84.dat_ref, ...), custom_call_target="tpu_custom_call" | custom-call | flops 24763170816 | bytes 58982400 | tf_op jit(solution)/shard_map/mixer_backward/pallas_call | solution.py:558
  187.9 112.6 %exchange.1 = (f32[256,384]{1,0:T(8,128)}, bf16[5,48,128]{2,1,0:T(8,128)(2,1)}, bf16[4,48,128]{2,1,0:T(8,128)(2,1)}, bf16[3,48,128]{2,1,0:T(8,128)(2,1)}, bf16[1...) custom-call(f32[1,3072]{1,0:T(1,128)} %get-tuple-element.93.refs_0_, f32[8,768]{1,0:T(8,128)} %get-tuple-element.94.refs_1_, ...), custom_call_target="tpu_custom_call" | custom-call | tf_op jit(solution)/shard_map/exchange/pallas_call | solution.py:791
  300.5 2.3 unpack.1

commit v3 on v2

--- a/solution.py
+++ b/solution.py
@@ -19,7 +19,7 @@
 LANES = 128
 CHUNK = 256
 PACK = 384
-VMEM_BYTES = 62 * 2**20
+VMEM_BYTES = 63 * 2**20
 
 
 def nt(a, b, precision=None):
@@ -141,6 +141,116 @@
 
 def specs_of(length, n):
     return ((0, 0, n // 2), (1, n, n // 2), (2, 2 * n, n), (3, 4 * n, n))
+
+
+def bits_of(n):
+    return n.bit_length() - 1
+
+
+def order_of(rows_n, pos_n, first):
+    rows = [("rows", b) for b in range(1, bits_of(rows_n))]
+    pos = [("pos", b) for b in range(bits_of(pos_n))]
+    return [("rows", 0)] + (pos + rows if first == "pos" else rows[:1] + pos + rows[1:])
+
+
+def alive_dims(rows_n, pos_n):
+    pos = [("pos", b) for b in reversed(range(bits_of(pos_n)))]
+    return pos + [None] + [("rows", b) for b in reversed(range(bits_of(rows_n)))]
+
+
+def partner(step):
+    axis, bit = step
+    place = lax.axis_index(axis)
+    mine = (place // (1 << bit)) % 2
+    return mine, {axis: place + (1 - 2 * mine) * (1 << bit)}
+
+
+def meet(steps):
+    barrier = pltpu.get_barrier_semaphore()
+    for step in steps:
+        pl.semaphore_signal(barrier, inc=1, device_id=partner(step)[1], device_id_type=MESH)
+    pl.semaphore_wait(barrier, len(steps))
+
+
+class Halving:
+    def __init__(self, ref, blocks, alive, order, refs, near=None):
+        m = len(order)
+        self.near = near
+        got, sums, self.send_sem, self.recv_sem = refs[:m], refs[m:2 * m], refs[2 * m], refs[2 * m + 1]
+        self.order, self.got, self.sums = order, got, sums
+        self.stages = []
+        alive = list(alive)
+        for k, step in enumerate(order):
+            self.stages.append((ref, blocks, tuple(alive), alive.index(step)))
+            alive.remove(step)
+            ref, blocks = sums[k], (0, blocks[1])
+
+    def pick(self, stage, which):
+        ref, (start, count), alive, dim = self.stages[stage]
+        index = [slice(None)] * len(alive)
+        index[alive.index(None)] = pl.ds(start, count)
+        index[dim] = which
+        return ref.at[tuple(index)]
+
+    def copy(self, stage):
+        mine, there = partner(self.order[stage])
+        return pltpu.make_async_remote_copy(
+            src_ref=self.pick(stage, 1 - mine), dst_ref=self.got[stage], send_sem=self.send_sem.at[stage],
+            recv_sem=self.recv_sem.at[stage], device_id=there, device_id_type=MESH)
+
+    def fetch(self):
+        return pltpu.make_async_copy(self.pick(0, partner(self.order[0])[0]), self.sums[0], self.near)
+
+    def start(self, stage):
+        self.copy(stage).start()
+        if stage == 0 and self.near is not None:
+            self.fetch().start()
+
+    def finish(self, stage):
+        self.copy(stage).wait()
+        if stage == 0 and self.near is not None:
+            self.fetch().wait()
+        _, (_, count), alive, dim = self.stages[stage]
+        kept, got, out = self.pick(stage, partner(self.order[stage])[0]), self.got[stage], self.sums[stage]
+        if stage == 0 and self.near is not None:
+            kept = out
+        split = [d for k, d in enumerate(alive) if k != dim].index(None)
+
+        def add(lead):
+            def body(b, carry):
+                at = lead + (b,)
+                out[at] = (kept[at].astype(f32) + got[at].astype(f32)).astype(bf)
+                return carry
+
+            lax.fori_loop(0, count, body, 0)
+
+        leads = [()]
+        for _ in range(split):
+            leads = [lead + (k,) for lead in leads for k in range(2)]
+        for lead in leads:
+            add(lead)
+
+
+def job_shapes(shape, blocks, alive, order):
+    dims = list(alive)
+    now = [blocks if d is None else 2 for d in dims] + list(shape[-2:])
+    out = []
+    for step in order:
+        k = dims.index(step)
+        dims.pop(k)
+        now.pop(k)
+        out.append(tuple(now))
+    return out
+
+
+def job_scratch(left, last):
+    sums = left if last else left[:-1]
+    return [pltpu.VMEM(s, bf) for s in left] + [pltpu.VMEM(s, bf) for s in sums] + [pltpu.SemaphoreType.DMA((len(left),))] * 2
+
+
+def grad_shape(blocks, rows, rows_n, pos_n, cores):
+    rbits, pbits = bits_of(rows_n), bits_of(pos_n)
+    return (2,) * pbits + (blocks // pos_n,) + (2,) * (rbits - (0 if cores else 1)) + (rows // rows_n, LANES)
 
 
 def forward_kernel(tok_ref, seg_ref, g1_ref, s1_ref, wg_ref, wi_ref, wv_ref, mb_ref, swg_ref, swi_ref, swv_ref, sb_ref,
@@ -299,9 +409,10 @@
     return phi, phi + e * bell * (1 / math.sqrt(2 * math.pi))
 
 
-def mlp_kernel(mix_ref, tok_ref, cot_ref, wo_ref, bo_ref, g2_ref, s2_ref, we_ref, be_ref, wr_ref, br_ref,
-        out_ref, dat_ref, wog_ref, weg_ref, wrg_ref, beg_ref, vec_ref, hid, acc, dn2, n2, n2t, cott, act, de):
+def mlp_kernel(links, mix_ref, tok_ref, cot_ref, wo_ref, bo_ref, g2_ref, s2_ref, we_ref, be_ref, wr_ref, br_ref,
+        out_ref, dat_ref, wog_ref, weg_ref, wrg_ref, beg_ref, vec_ref, hid, acc, dn2, n2, n2t, cott, act, de, *pair):
     j = pl.program_id(0)
+    last = pl.num_programs(0) - 1
     total, width = tok_ref.shape
     part_ff = we_ref.shape[1]
     step = 512
@@ -310,8 +421,38 @@
     def at(i, size=step):
         return pl.ds(pl.multiple_of(i * size, size), size)
 
+    core = ("rows", 0)
+    if links:
+        ahead_s, back_s, ahead_got, back_got, send_sem, recv_sem = pair
+
+        def copies(k):
+            mine, there = partner(core)
+            slot = lax.rem(k, 2)
+            return [
+                pltpu.make_async_remote_copy(
+                    src_ref=src.at[1 - mine], dst_ref=dst.at[slot], send_sem=send_sem.at[w], recv_sem=recv_sem.at[w, slot],
+                    device_id=there, device_id_type=MESH)
+                for w, (src, dst) in enumerate(((ahead_s, ahead_got), (back_s, back_got)))]
+
+        def finish(k):
+            for copy in copies(k):
+                copy.wait()
+            mine, _ = partner(core)
+            slot = lax.rem(k, 2)
+            count = ahead_s.shape[1]
+
+            def add(b, carry):
+                weg_ref[k * count + b] = (ahead_s[mine, b].astype(f32) + ahead_got[slot, b].astype(f32)).astype(bf)
+                wrg_ref[b, k] = (back_s[mine, b].astype(f32) + back_got[slot, b].astype(f32)).astype(bf)
+                return carry
+
+            lax.fori_loop(0, count, add, 0)
+
     @pl.when(j == 0)
     def _():
+        if links:
+            meet([core])
+
         def body(i, carry):
             rows = at(i)
             h = tok_ref[rows, :].astype(f32) + nn(mix_ref[rows, :], wo_ref[...]) + as_row(bo_ref)
@@ -344,18 +485,42 @@
     beg_ref[...] = lax.fori_loop(0, steps, tile, jnp.zeros((1, part_ff), f32))
 
     def grads(i, carry):
-        rows = at(i, 256)
+        rows = at(i, 384)
         back = nn(cott[rows, :], act[...]).astype(bf).T
-        for h in range(256 // LANES):
-            wrg_ref[i * (256 // LANES) + h] = back[:, h * LANES:(h + 1) * LANES]
         ahead = nn(n2t[rows, :], de[...]).astype(bf)
-        for h in range(part_ff // LANES):
-            weg_ref[h, rows, :] = ahead[:, h * LANES:(h + 1) * LANES]
+        blocks = 384 // LANES
+        if links:
+            tall = back_s.shape[3]
+            for h in range(blocks):
+                for y in range(back_s.shape[2]):
+                    for k in range(2):
+                        top = (2 * y + k) * tall
+                        back_s[k, i * blocks + h, y] = back[top:top + tall, h * LANES:(h + 1) * LANES]
+            tall = ahead_s.shape[3]
+            groups = 384 // (2 * tall)
+            for h in range(part_ff // LANES):
+                for g in range(groups):
+                    for k in range(2):
+                        top = (2 * g + k) * tall
+                        ahead_s[k, h, i * groups + g] = ahead[top:top + tall, h * LANES:(h + 1) * LANES]
+        else:
+            for h in range(blocks):
+                wrg_ref[i * blocks + h, pl.ds(pl.multiple_of(j * part_ff, part_ff), part_ff), :] = back[:, h * LANES:(h + 1) * LANES]
+            for h in range(part_ff // LANES):
+                weg_ref[j * (part_ff // LANES) + h, rows, :] = ahead[:, h * LANES:(h + 1) * LANES]
         return carry
 
-    lax.fori_loop(0, width // 256, grads, 0)
-
-    @pl.when(j == pl.num_programs(0) - 1)
+    if links:
+        @pl.when(j > 0)
+        def _():
+            finish(j - 1)
+
+    lax.fori_loop(0, width // 384, grads, 0)
+    if links:
+        for copy in copies(j):
+            copy.start()
+
+    @pl.when(j == last)
     def _():
         def body(i, carry):
             rows = at(i)
@@ -386,38 +551,60 @@
             return carry
 
         lax.fori_loop(0, width // 256, weights, 0)
-
-
-def mlp(mix, tok, cot, wo, bo, g2, s2, we, be, wr, br, part_ff=1024):
+        if links:
+            finish(j)
+
+
+def single(*shape):
+    return pl.BlockSpec(shape, lambda *_: (0,) * len(shape), pipeline_mode=pl.Buffered(1))
+
+
+def mlp(links, mix, tok, cot, wo, bo, g2, s2, we, be, wr, br, part_ff=768):
     total, width = tok.shape
     ff = we.shape[1]
-    part_ff = min(part_ff, ff)
     sds = jax.ShapeDtypeStruct
     blocks = width // LANES
+    parts = ff // part_ff
+    scratch = [pltpu.VMEM((total, width), f32)] * 3 + [pltpu.VMEM((total, width), bf)]
+    scratch += [pltpu.VMEM((width, total), bf)] * 2 + [pltpu.VMEM((total, part_ff), bf)] * 2
+    if links:
+        rows_n = links[0]
+        pairs = rows_n // 2
+        ahead = (ff // LANES, pairs, width // rows_n, LANES)
+        back = (blocks, parts, pairs // parts, ff // rows_n, LANES)
+        for shape in ((part_ff // LANES, *ahead[1:]), (blocks, *back[2:])):
+            scratch.append(pltpu.VMEM((2, *shape), bf))
+        for shape in ((part_ff // LANES, *ahead[1:]), (blocks, *back[2:])):
+            scratch.append(pltpu.VMEM((2, *shape), bf))
+        scratch += [pltpu.SemaphoreType.DMA((2,)), pltpu.SemaphoreType.DMA((2, 2))]
+    else:
+        ahead, back = (ff // LANES, width, LANES), (blocks, ff, LANES)
+    side = dict(collective_id=1, has_side_effects=True) if links else {}
     return pl.pallas_call(
-        mlp_kernel, grid=(ff // part_ff,),
+        functools.partial(mlp_kernel, links), grid=(parts,),
         in_specs=[whole_spec(a) for a in (mix, tok, cot, wo, bo, g2, s2)]
             + [pl.BlockSpec((width, part_ff), lambda j: (0, j)), whole_spec(be), pl.BlockSpec((part_ff, width), lambda j: (j, 0)),
                 whole_spec(br)],
-        out_specs=[fixed_spec(total, width), fixed_spec(total, width), fixed_spec(blocks, width, LANES),
-            pl.BlockSpec((part_ff // LANES, width, LANES), lambda j: (j, 0, 0)),
-            pl.BlockSpec((blocks, part_ff, LANES), lambda j: (0, j, 0)), pl.BlockSpec((1, part_ff), lambda j: (0, j)),
-            fixed_spec(8, width)],
-        out_shape=[sds((total, width), bf), sds((total, width), bf), sds((blocks, width, LANES), bf),
-            sds((ff // LANES, width, LANES), bf), sds((blocks, ff, LANES), bf), sds((1, ff), f32), sds((8, width), f32)],
-        scratch_shapes=[pltpu.VMEM((total, width), f32)] * 3 + [pltpu.VMEM((total, width), bf)]
-            + [pltpu.VMEM((width, total), bf)] * 2 + [pltpu.VMEM((total, part_ff), bf)] * 2,
-        compiler_params=pltpu.CompilerParams(vmem_limit_bytes=VMEM_BYTES),
+        out_specs=[single(total, width), single(total, width), single(blocks, width, LANES), single(*ahead), single(*back),
+            pl.BlockSpec((1, part_ff), lambda j: (0, j)), single(8, width)],
+        out_shape=[sds((total, width), bf), sds((total, width), bf), sds((blocks, width, LANES), bf), sds(ahead, bf),
+            sds(back, bf), sds((1, ff), f32), sds((8, width), f32)],
+        scratch_shapes=scratch,
+        compiler_params=pltpu.CompilerParams(vmem_limit_bytes=VMEM_BYTES, **side),
         cost_estimate=pl.CostEstimate(
             flops=12 * total * width * ff + 4 * total * width * width, bytes_accessed=30 * total * width,
             transcendentals=total * ff),
         name="mlp")(mix, tok, cot, wo, bo, g2, s2, we, be, wr, br)
 
 
-def backward_kernel(dat_ref, tok_ref, seg_ref, g1_ref, wo_ref, long_ref, mixed_ref, proj_ref, trans_ref, spec_ref, nt_ref,
+def backward_kernel(links, plan, *refs):
+    moved = len(plan)
+    grads, refs = refs[:moved], refs[moved:]
+    (dat_ref, tok_ref, seg_ref, g1_ref, wo_ref, long_ref, mixed_ref, proj_ref, trans_ref, spec_ref, nt_ref,
         wg_ref, wi_ref, wv_ref, swg_ref, swi_ref, swv_ref, skip_ref, state_ref, zt_ref, iw_ref, ow_ref, eo_ref, io_ref,
         oo_ref, fw_ref, rate_ref, t0, t3, t1, t2, u0, u3, u1, u2,
-        tg_ref, wgrad_ref, sg_ref, vec_ref, gew_ref, giw_ref, gow_ref, gfw_ref, gsm_ref, dn, de3, dp_s, ds_s):
+        tg_ref, wgrad_ref, sg_ref, vec_ref, gew_ref, giw_ref, gow_ref, gfw_ref, gsm_ref) = refs[:44]
+    outs, (dn, de3, dp_s, ds_s, *pair) = refs[44:44 + moved], refs[44 + moved:]
     c = pl.program_id(0)
     r = pl.program_id(1)
     chunks = pl.num_programs(0)
@@ -438,6 +625,51 @@
         dn[...] = jnp.zeros_like(dn)
         de3[...] = jnp.zeros_like(de3)
         vec_ref[...] = jnp.zeros_like(vec_ref)
+
+    core = ("rows", 0)
+    jobs = []
+    if links:
+        pair_s, pair_got, pair_send, pair_recv = pair[:4]
+        rest = list(pair[4:])
+        for (alive, order), grad, out in zip(plan, grads, outs):
+            m = len(order)
+            jobs.append(Halving(grad, (0, grad.shape[alive.index(None)]), alive, order, rest[:2 * m - 1] + [out] + rest[2 * m - 1:2 * m + 1],
+                rest[2 * m + 1]))
+            rest = rest[2 * m + 2:]
+
+        def pair_copy(k):
+            mine, there = partner(core)
+            slot = lax.rem(k, 2)
+            return pltpu.make_async_remote_copy(
+                src_ref=pair_s.at[1 - mine], dst_ref=pair_got.at[slot], send_sem=pair_send, recv_sem=pair_recv.at[slot],
+                device_id=there, device_id_type=MESH)
+
+        def pair_finish(k):
+            pair_copy(k).wait()
+            mine, _ = partner(core)
+            slot = lax.rem(k, 2)
+            for i in range(3):
+                for h in range(wide // LANES):
+                    wgrad_ref[i, k * (wide // LANES) + h] = (
+                        pair_s[mine, i, h].astype(f32) + pair_got[slot, i, h].astype(f32)).astype(bf)
+
+        step = c * pl.num_programs(1) + r
+
+        def advance(when, stage):
+            @pl.when(step == when)
+            def _():
+                for job in jobs:
+                    if stage > 0:
+                        job.finish(stage - 1)
+                    if stage < len(job.order):
+                        job.start(stage)
+
+        @pl.when(step == 0)
+        def _():
+            meet([core] + list(dict.fromkeys(s for _, order in plan for s in order)))
+
+        for stage, when in enumerate(MOMENTS[:-1]):
+            advance(when, stage)
 
     def add(off, v):
         ds_s[off:off + v.shape[0], :] += v
@@ -486,10 +718,24 @@
 
     @pl.when(r == last_row)
     def _():
+        if links:
+            @pl.when(c > 0)
+            def _():
+                pair_finish(c - 1)
+
         for i in range(3):
             part = nn(nt_ref[...], dp_s[i]).astype(bf)
             for h in range(wide // LANES):
-                wgrad_ref[i, h] = part[:, h * LANES:(h + 1) * LANES]
+                if links:
+                    tall = pair_s.shape[4]
+                    for g in range(pair_s.shape[3]):
+                        for k in range(2):
+                            top = (2 * g + k) * tall
+                            pair_s[k, i, h, g] = part[top:top + tall, h * LANES:(h + 1) * LANES]
+                else:
+                    wgrad_ref[i, c * (wide // LANES) + h] = part[:, h * LANES:(h + 1) * LANES]
+        if links:
+            pair_copy(c).start()
         first = lax.broadcasted_iota(jnp.int32, (half, wide), 0) == 0
         extra = ds_s[6 * n:6 * n + half]
         ds_s[0:half] = jnp.where(first, 0.5, 1.0) * (ds_s[0:half] + jnp.where(first, 0.0, extra))
@@ -534,9 +780,16 @@
         g = g * column(eo_ref)
         gsm_ref[5] = flat(g)
         gew_ref[...] = nt(zt_ref[...], g, HI)
-
-
-def backward_mixer(dat, tok, segments, g1, wo, longc, mixed, proj, trans, spec, ntr, wm, sw, skip, state, filt, zt, rates,
+        if links:
+            pair_finish(c)
+            for job in jobs:
+                job.finish(len(job.order) - 1)
+
+
+MOMENTS = (0, 3, 5, 6)
+
+
+def backward_mixer(links, weg, wrg, dat, tok, segments, g1, wo, longc, mixed, proj, trans, spec, ntr, wm, sw, skip, state, filt, zt, rates,
         tabs, tabst):
     rows_here, length = segments.shape
     total, width = tok.shape
@@ -545,10 +798,28 @@
     ew, eb, eo, iw, ib, io, ow, ob, oo, fw = filt
     hidden = fw.shape[0]
     sds = jax.ShapeDtypeStruct
+    plan, grads, moved, scratch = [], [], [], []
+    wide_blocks = width // LANES
+    wm_shape = (3, wide_blocks, width, LANES)
+    if links:
+        rows_n, pos_n = links
+        alive = [d for d in alive_dims(rows_n, pos_n) if d != ("rows", 0)]
+        pair = (3, CHUNK // LANES, rows_n // 2, width // rows_n, LANES)
+        wm_shape = (3, wide_blocks, *pair[2:])
+        scratch = [pltpu.VMEM((2, *pair), bf), pltpu.VMEM((2, *pair), bf), pltpu.SemaphoreType.DMA, pltpu.SemaphoreType.DMA((2,))]
+        for grad, rows_of, first in ((weg, width, "pos"), (wrg, wrg.shape[1] * wrg.shape[2] * wrg.shape[3] * 2, "rows")):
+            grad = grad.reshape(grad_shape(grad.shape[0], rows_of, rows_n, pos_n, False))
+            order = order_of(rows_n, pos_n, first)[1:-1]
+            left = job_shapes(grad.shape, grad.shape[alive.index(None)], alive, order)
+            plan.append((alive, order))
+            grads.append(grad)
+            moved.append(left[-1])
+            scratch += job_scratch(left, False) + [pltpu.SemaphoreType.DMA]
+    side = dict(collective_id=2, has_side_effects=True) if links else {}
     late = lambda c, r: (jnp.where(c == count - 1, r, 0), 0)
-    ins = [dat, tok, segments, g1, wo, longc, mixed, proj, trans, spec, ntr, wm, wm, wm, sw, sw, sw, skip, state, zt,
+    ins = [*grads, dat, tok, segments, g1, wo, longc, mixed, proj, trans, spec, ntr, wm, wm, wm, sw, sw, sw, skip, state, zt,
         iw, ow, eo, io, oo, fw, rates, *tabs, *tabst]
-    specs = [whole_spec(dat), pl.BlockSpec((length, width), late), whole_spec(segments), whole_spec(g1),
+    specs = [pl.BlockSpec(memory_space=pl.ANY) for g in grads] + [whole_spec(dat), pl.BlockSpec((length, width), late, pipeline_mode=pl.Buffered(1)), whole_spec(segments), whole_spec(g1),
         pl.BlockSpec((CHUNK, width), lambda c, r: (c, 0)), part_spec(length), stack_spec(3, length), stack_spec(3, length),
         pl.BlockSpec((1, DOCS, 2 * length, CHUNK), lambda c, r: (r, 0, 0, c)), column_spec(2 * length + n // 2, 0, count),
         whole_spec(ntr)]
@@ -556,30 +827,22 @@
     specs += [whole_spec(a) for a in (skip, state, zt, iw, ow, eo, io, oo)]
     specs += [column_spec(hidden, 0, count), column_spec(1, 0, count)] + [whole_spec(a) for a in (*tabs, *tabst)]
     return pl.pallas_call(
-        backward_kernel, grid=(count, rows_here), in_specs=specs,
-        out_specs=[pl.BlockSpec((length, width), late),
-            pl.BlockSpec((3, CHUNK // LANES, width, LANES), lambda c, r: (0, c, 0, 0)),
+        functools.partial(backward_kernel, links, plan), grid=(count, rows_here), in_specs=specs,
+        out_specs=[pl.BlockSpec((length, width), late, pipeline_mode=pl.Buffered(1)),
+            single(*wm_shape),
             pl.BlockSpec((3, 8, CHUNK), lambda c, r: (0, 0, c)), fixed_spec(8, width), fixed_spec(zt.shape[0], hidden),
-            fixed_spec(hidden, hidden), fixed_spec(hidden, hidden), column_spec(hidden, 0, count), fixed_spec(6, 8, hidden)],
-        out_shape=[sds((total, width), bf), sds((3, width // LANES, width, LANES), bf), sds((3, 8, width), f32),
+            fixed_spec(hidden, hidden), fixed_spec(hidden, hidden), column_spec(hidden, 0, count), fixed_spec(6, 8, hidden)]
+            + [single(*s) for s in moved],
+        out_shape=[sds((total, width), bf), sds(wm_shape, bf), sds((3, 8, width), f32),
             sds((8, width), f32), sds((zt.shape[0], hidden), f32), sds((hidden, hidden), f32), sds((hidden, hidden), f32),
-            sds((hidden, width), f32), sds((6, 8, hidden), f32)],
+            sds((hidden, width), f32), sds((6, 8, hidden), f32)]
+            + [sds(s, bf) for s in moved],
         scratch_shapes=[pltpu.VMEM((total, width), f32), pltpu.VMEM((hidden, length), f32), pltpu.VMEM((3, total, CHUNK), bf),
-            pltpu.VMEM((6 * n + n // 2, CHUNK), f32)],
-        compiler_params=pltpu.CompilerParams(vmem_limit_bytes=VMEM_BYTES),
+            pltpu.VMEM((6 * n + n // 2, CHUNK), f32)] + scratch,
+        compiler_params=pltpu.CompilerParams(vmem_limit_bytes=VMEM_BYTES, **side),
         cost_estimate=pl.CostEstimate(
             flops=total * width * (14 * width + 4 * 2 * 5 * n), bytes_accessed=50 * total * width, transcendentals=0),
         name="mixer_backward")(*ins)
-
-
-def bits_of(n):
-    return n.bit_length() - 1
-
-
-def order_of(rows_n, pos_n, first):
-    rows = [("rows", b) for b in range(1, bits_of(rows_n))]
-    pos = [("pos", b) for b in range(bits_of(pos_n))]
-    return [("rows", 0)] + (pos + rows if first == "pos" else rows[:1] + pos + rows[1:])
 
 
 def scatter_blocks(grad, rows_n, pos_n, first):
@@ -592,7 +855,7 @@
     high = height // rows_n
     rbits, pbits = bits_of(rows_n), bits_of(pos_n)
     acc = grad.reshape((2,) * pbits + (blocks // pos_n,) + (2,) * rbits + (high, wide))
-    alive = [("pos", b) for b in reversed(range(pbits))] + [None] + [("rows", b) for b in reversed(range(rbits))]
+    alive = alive_dims(rows_n, pos_n)
     for axis, bit in order_of(rows_n, pos_n, first):
         dim = alive.index((axis, bit))
         mine = (lax.axis_index(axis) >> bit) & 1
@@ -644,64 +907,6 @@
         pk[at["small"] + k:at["small"] + k + 1, 0:hidden] = gsm[k, 0:1, :]
 
 
-class Halving:
-    def __init__(self, ref, blocks, alive, order, got, sums, send_sem, recv_sem):
-        self.ref, self.blocks, self.alive, self.order = ref, blocks, list(alive), order
-        self.got, self.sums, self.send_sem, self.recv_sem = got, sums, send_sem, recv_sem
-        self.copy = None
-
-    def pick(self, dim, which):
-        start, count = self.blocks
-        index = [slice(None)] * len(self.alive)
-        index[self.alive.index(None)] = pl.ds(start, count)
-        index[dim] = which
-        return tuple(index)
-
-    def start(self, stage):
-        axis, bit = self.order[stage]
-        dim = self.alive.index((axis, bit))
-        place = lax.axis_index(axis)
-        mine = (place // (1 << bit)) % 2
-        self.keep = self.pick(dim, mine)
-        self.copy = pltpu.make_async_remote_copy(
-            src_ref=self.ref.at[self.pick(dim, 1 - mine)], dst_ref=self.got[stage], send_sem=self.send_sem.at[stage],
-            recv_sem=self.recv_sem.at[stage], device_id={axis: place + (1 - 2 * mine) * (1 << bit)}, device_id_type=MESH)
-        self.copy.start()
-        self.alive.pop(dim)
-
-    def finish(self, stage):
-        self.copy.wait()
-        kept, got, out = self.ref.at[self.keep], self.got[stage], self.sums[stage]
-        split = self.alive.index(None)
-
-        def add(lead):
-            def body(b, carry):
-                at = lead + (b,)
-                out[at] = (kept[at].astype(f32) + got[at].astype(f32)).astype(bf)
-                return carry
-
-            lax.fori_loop(0, self.blocks[1], body, 0)
-
-        leads = [()]
-        for d in range(split):
-            leads = [lead + (k,) for lead in leads for k in range(2)]
-        for lead in leads:
-            add(lead)
-        self.ref, self.blocks = out, (0, self.blocks[1])
-
-
-def job_shapes(shape, blocks, alive, order):
-    dims = list(alive)
-    now = [blocks if d is None else 2 for d in dims] + list(shape[-2:])
-    out = []
-    for step in order:
-        k = dims.index(step)
-        dims.pop(k)
-        now.pop(k)
-        out.append(tuple(now))
-    return out
-
-
 def exchange_kernel(sizes, at, plan, count, *refs):
     rows_n, pos_n = sizes
     n = rows_n * pos_n
@@ -716,8 +921,7 @@
     jobs = []
     for (src, blocks, alive, order), out in zip(plan, outs):
         m = len(order)
-        got, sums = rest[:m], rest[m:2 * m - 1] + [out]
-        jobs.append(Halving(grads[src], blocks, alive, order, got, sums, rest[2 * m - 1], rest[2 * m]))
+        jobs.append(Halving(grads[src], blocks, alive, order, rest[:2 * m - 1] + [out] + rest[2 * m - 1:2 * m + 1]))
         rest = rest[2 * m + 1:]
     me = lax.axis_index("rows") * pos_n + lax.axis_index("pos")
     chunk = pk.shape[0] // n
@@ -786,8 +990,7 @@
     for src, (start, blocks), alive, order in plan:
         left = job_shapes(grads[src].shape, blocks, alive, order)
         shapes.append(jax.ShapeDtypeStruct(left[-1], bf))
-        scratch += [pltpu.VMEM(s, bf) for s in left] + [pltpu.VMEM(s, bf) for s in left[:-1]]
-        scratch += [pltpu.SemaphoreType.DMA((len(order),))] * 2
+        scratch += job_scratch(left, False)
     return pl.pallas_call(
         functools.partial(exchange_kernel, sizes, at, plan, len(grads)), out_shape=shapes,
         in_specs=[vm] * (9 + len(grads)), out_specs=[vm] * len(shapes), scratch_shapes=scratch,
@@ -867,30 +1070,35 @@
     proj, mixed, longc, mix, trans, spec, state, ntr = forward_mixer(
         tok, segments, first_gain, first_shift, mixer_weight, mixer_bias, short_weight, short_bias, skip_gain, filt, zt, rates,
         tabs, tabst)
+    direct = rows_n * pos_n <= 32 and width % (16 * rows_n) == 0 and width // LANES % pos_n == 0 and ff // rows_n * 4 == width
+    links = sizes if direct else None
     out, dat, wog, weg, wrg, beg, vec2 = mlp(
-        mix, tok, cot, output_weight, output_bias, second_gain, second_shift, expand_weight, expand_bias, reduce_weight,
+        links, mix, tok, cot, output_weight, output_bias, second_gain, second_shift, expand_weight, expand_bias, reduce_weight,
         reduce_bias)
-    tgrad, wmg, sgrad, vec1, gew, giw, gow, gfw, gsm = backward_mixer(
-        dat, tok, segments, first_gain, output_weight, longc, mixed, proj, trans, spec, ntr, mixer_weight, short_weight,
-        skip_gain, state, filt, zt, rates, tabs, tabst)
-    wmg = wmg.reshape(3 * width // LANES, width, LANES)
-    grads = [wmg, wog, weg, wrg]
+    tgrad, wmg, sgrad, vec1, gew, giw, gow, gfw, gsm, *early = backward_mixer(
+        links, weg, wrg, dat, tok, segments, first_gain, output_weight, longc, mixed, proj, trans, spec, ntr, mixer_weight,
+        short_weight, skip_gain, state, filt, zt, rates, tabs, tabst)
     small = (beg, vec2, sgrad, vec1, gew, giw, gow, gfw, gsm)
     at, used = pack_places(width, hidden, emb, ff)
-    direct = rows_n * pos_n <= 32 and all(g.shape[0] % pos_n == 0 and g.shape[1] % (16 * rows_n) == 0 for g in grads)
+    blocks_m, blocks_o = 3 * width // LANES, width // LANES
     if direct:
-        rbits, pbits = bits_of(rows_n), bits_of(pos_n)
-        alive = [("pos", b) for b in reversed(range(pbits))] + [None] + [("rows", b) for b in reversed(range(rbits))]
-        grads = [g.reshape((2,) * pbits + (g.shape[0] // pos_n,) + (2,) * rbits + (g.shape[1] // rows_n, LANES)) for g in grads]
+        alive = alive_dims(rows_n, pos_n)
+        core = [("rows", 0)]
+        paired = [d for d in alive if d not in core]
         by_pos, by_rows = order_of(rows_n, pos_n, "pos"), order_of(rows_n, pos_n, "rows")
-        count = [g.shape[pbits] for g in grads]
-        cut = (count[0] + 1) // 2
-        plan = [(0, (0, cut), alive, by_pos), (0, (cut, count[0] - cut), alive, by_rows), (1, (0, count[1]), alive, by_rows),
-            (2, (0, count[2]), alive, by_pos), (3, (0, count[3]), alive, by_rows)]
+        half_m = blocks_m // pos_n
+        cut = (half_m + 1) // 2
+        grads = [wmg.reshape(grad_shape(blocks_m, width, rows_n, pos_n, False)),
+            wog.reshape(grad_shape(blocks_o, width, rows_n, pos_n, True)), *early]
+        left = [d for d in alive if d is None or d in by_pos[-1:]]
+        plan = [(0, (0, cut), paired, by_pos[1:]), (0, (cut, half_m - cut), paired, by_rows[1:]),
+            (1, (0, blocks_o // pos_n), alive, by_rows), (2, (0, early[0].shape[0]), left, by_pos[-1:]),
+            (3, (0, early[1].shape[0]), left, by_pos[-1:])]
         packed, m_a, m_b, o_part, e_part, r_part = exchange(sizes, at, used, small, grads, plan)
         blocks = [[m_a, m_b], [o_part], [e_part], [r_part]]
     else:
         packed = lax.psum(pack_only(at, used, small), ("rows", "pos"))
+        grads = [wmg.reshape(blocks_m, width, LANES), wog, weg, wrg]
         blocks = [[scatter_blocks(g, rows_n, pos_n, f)] for g, f in zip(grads, ("pos", "rows", "pos", "rows"))]
     (fg, fs, mb, sw, sb, ew, eb, eo, iw, ib, io, ow, ob, oo, fw, sk, obias, sg, ss, eb2, rb, m_grad, o_grad, e_grad, r_grad) = unpack(
         at, packed, blocks, width, hidden, emb, ff)

time: 303 us -> 266 us (0.88)
  Pallas kernels: 302 us -> 260 us
  local copies, waits for them, and re-layouts: 0 us -> 4.78 us
    pallas_call x1, Pallas kernels: 113 us -> 52.9 us  [exchange(): pl.pallas_call(functools.partial(exchange_kernel, sizes, at, plan, len(gr...]
    pallas_call x2, Pallas kernels: 140 us -> 157 us  [the longest x1 78.6 us: backward_mixer(): pl.pallas_call(functools.partial(backward_kernel, links, plan), grid=(cou...]
    unnamed x0 -> x4, local copies, waits for them, and re-layouts: none -> 4.78 us
where the time goes in v3:
time: 266 us; the launch traced here: 265 us
  Pallas kernels  260 us (98%)
  local copies, waits for them, and re-layouts  4.78 us (2%)
    pallas_call x1, Pallas kernels, backward_mixer(): pl.pallas_call(functools.partial(backward_kernel, links, plan), grid=(cou...  78.6 us
    pallas_call x1, Pallas kernels, mlp(): pl.pallas_call(functools.partial(mlp_kernel, links), grid=(parts,), in_sp...  78.5 us
    pallas_call x1, Pallas kernels, exchange(): pl.pallas_call(functools.partial(exchange_kernel, sizes, at, plan, len(gr...  52.9 us
    pallas_call x1, Pallas kernels, forward_mixer(): pl.pallas_call(forward_kernel, grid=(count, rows_here), in_specs=specs, o...  47.7 us

profile of v3, /device:TPU:0, one launch (start us, length us, event | category | flops | bytes accessed | tf_op | source)
XLA Modules:
  0.0 265.5 jit_solution(12748772449657787124)
XLA Ops:
  0.7 47.7 %mixer_forward.1 = (bf16[3,1536,768]{2,1,0:T(8,128)(2,1)}, bf16[3,1536,768]{2,1,0:T(8,128)(2,1)}, bf16[1536,768]{1,0:T(8,128)(2,1)}, bf16[1536,768]{1,0:T(8,128)...) custom-call(bf16[1536,768]{1,0:T(8,128)(2,1)} %bitcast.13, ...), custom_call_target="tpu_custom_call" | custom-call | flops 17515413504 | bytes 47185920 | tf_op jit(solution)/shard_map/mixer_forward/pallas_call | solution.py:385
  48.4 78.5 %mlp.1 = (bf16[1536,768]{1,0:T(8,128)(2,1)}, bf16[1536,768]{1,0:T(8,128)(2,1)}, bf16[6,768,128]{2,1,0:T(8,128)(2,1)}, bf16[24,8,48,128]{3,2,1,0:T(8,128)(2,1)}, ...) custom-call(bf16[1536,768]{1,0:T(8,128)(2,1)} %get-tuple-element.84.mix_ref, ...), custom_call_target="tpu_custom_call" | custom-call | flops 47110422528 | bytes 35389440 | tf_op jit(solution)/shard_map/mlp/pallas_call | solution.py:583
  126.9 78.6 %mixer_backward.1 = (bf16[1536,768]{1,0:T(8,128)(2,1)}, bf16[3,6,8,48,128]{4,3,2,1,0:T(8,128)(2,1)}, f32[3,8,768]{2,1,0:T(8,128)}, f32[8,768]{1,0:T(8,128)}, f32...) custom-call(bf16[2,12,2,2,2,48,128]{6,5,4,3,2,1,0:T(8,128)(2,1)} %bi, ...), custom_call_target="tpu_custom_call" | custom-call | flops 24763170816 | bytes 58982400 | tf_op jit(solution)/shard_map/mixer_backward/pallas_call | solution.py:829
  205.5 52.9 %exchange.1 = (f32[256,384]{1,0:T(8,128)}, bf16[5,48,128]{2,1,0:T(8,128)(2,1)}, bf16[4,48,128]{2,1,0:T(8,128)(2,1)}, bf16[3,48,128]{2,1,0:T(8,128)(2,1)}, bf16[1...) custom-call(f32[1,3072]{1,0:T(1,128)} %get-tuple-element.97.refs_0_, f32[8,768]{1,0:T(8,128)} %get-tuple-element.98.refs_1_, ...), custom_call_target="tpu_custom_call" | custom-call | tf_op jit(solution)/shard_map/exchange/pallas_call | solution.py:994
  258.4 2.3 unpack.1
  260.7 0.0 copy-start
  260.7 3.4 %copy.67 = bf16[2,768,768]{2,1,0:T(8,128)(2,1)} copy(bf16[2,768,768]{2,1,0:T(8,128)(2,1)} %bitcast.8) | data formatting | bytes 4718592
  264.1 0.0 copy-done
  264.1 1.4 copy.68
Async XLA Ops:
  260.7 3.4 %copy-start = (bf16[1536,768]{1,0:T(8,128)(2,1)S(1)}, bf16[1536,768]{1,0:T(8,128)(2,1)}, u32[]{:S(2)}) copy-start(bf16[1536,768]{1,0:T(8,128)(2,1)} %get-tuple-element.96) | copy-start | bytes 7077892

commit v4 on v3

--- a/solution.py
+++ b/solution.py
@@ -34,6 +34,12 @@
     return lax.dot_general(a, b, (((0,), (0,)), ((), ())), precision=precision, preferred_element_type=f32)
 
 
+def three_pass(dot, a, b):
+    ah, bh = a.astype(bf), b.astype(bf)
+    al, bl = (a - ah.astype(f32)).astype(bf), (b - bh.astype(f32)).astype(bf)
+    return dot(ah, bh) + dot(ah, bl) + dot(al, bh)
+
+
 def norm_stats(x):
     mean = jnp.mean(x, axis=-1, keepdims=True)
     centered = x - mean
@@ -139,6 +145,18 @@
     return t < edge, one, two
 
 
+def interleave(streams, lag=1):
+    streams = list(streams)
+    waiting = [lag * k for k in range(len(streams))]
+    while streams:
+        for k in range(len(streams)):
+            if waiting[k] > 0:
+                waiting[k] -= 1
+            elif next(streams[k], streams) is streams:
+                waiting[k] = None
+        streams, waiting = [s for s, w in zip(streams, waiting) if w is not None], [w for w in waiting if w is not None]
+
+
 def specs_of(length, n):
     return ((0, 0, n // 2), (1, n, n // 2), (2, 2 * n, n), (3, 4 * n, n))
 
@@ -151,6 +169,15 @@
     rows = [("rows", b) for b in range(1, bits_of(rows_n))]
     pos = [("pos", b) for b in range(bits_of(pos_n))]
     return [("rows", 0)] + (pos + rows if first == "pos" else rows[:1] + pos + rows[1:])
+
+
+def three_orders(rows_n, pos_n):
+    pos = [("pos", b) for b in range(bits_of(pos_n))]
+    near = [("rows", b) for b in range(1, bits_of(rows_n) - 1)]
+    far = [("rows", bits_of(rows_n) - 1)]
+    ring = pos + near
+    turn = lambda k: ring[k:] + ring[:k]
+    return turn(0) + far, turn(len(pos)) + far, turn(len(ring) - 1) + far
 
 
 def alive_dims(rows_n, pos_n):
@@ -256,27 +283,26 @@
 def forward_kernel(tok_ref, seg_ref, g1_ref, s1_ref, wg_ref, wi_ref, wv_ref, mb_ref, swg_ref, swi_ref, swv_ref, sb_ref,
         skip_ref, zt_ref, ew_ref, eb_ref, eo_ref, iw_ref, ib_ref, io_ref, ow_ref, ob_ref, oo_ref, fw_ref, rate_ref,
         t0, t3, t1, t2, u0, u3, u1, u2,
-        proj_ref, mixed_ref, long_ref, mix_ref, trans_ref, spec_ref, state_ref, nt_ref, normed, padded):
+        proj_ref, mixed_ref, long_ref, mix_ref, trans_ref, low_ref, state_ref, nt_ref, normed, padded, spec_ref):
     c = pl.program_id(0)
-    r = pl.program_id(1)
-    length, width = tok_ref.shape
+    rows_here, length = seg_ref.shape
+    width = tok_ref.shape[1]
     n = length // 3
     half = n // 2
     wide = fw_ref.shape[1]
-    rows = pl.ds(pl.multiple_of(r * length, length), length)
     tables = ((t0, u0), (t3, u3), (t1, u1), (t2, u2))
 
     @pl.when(c == 0)
     def _():
         step = 256
-        for i in range(length // step):
+        for i in range(tok_ref.shape[0] // step):
             part = slice(i * step, (i + 1) * step)
             xhat, _ = norm_stats(tok_ref[part, :].astype(f32))
             low = (xhat * as_row(g1_ref) + as_row(s1_ref)).astype(bf)
-            normed[pl.ds(pl.multiple_of(r * length + i * step, step), step), :] = low
+            normed[part, :] = low
             nt_ref[:, part] = low.T
 
-    @pl.when(jnp.logical_and(c == 0, r == 0))
+    @pl.when(c == 0)
     def _():
         padded[...] = jnp.zeros_like(padded)
         padded[0:ew_ref.shape[0], :] = ew_ref[...]
@@ -296,52 +322,76 @@
         state_ref[7] = c3
         state_ref[8] = pre
 
-    @pl.when(r == 0)
-    def _():
-        kernel = tn(state_ref[6], fw_ref[...], HI) * window(length, rate_ref[...])
+    def spectrum():
+        kernel = three_pass(tn, state_ref[6], fw_ref[...]) * window(length, rate_ref[...])
         k = kernel.astype(bf).astype(f32)
         y0, y3, y1, y2 = spread(k[0:n], k[n:2 * n], k[2 * n:])
+        yield
         first = lax.broadcasted_iota(jnp.int32, (half, wide), 0) == 0
         q0 = nn(t0[...], y0)
         spec_ref[0:half] = q0[0:half] * jnp.where(first, 0.5, 1.0)
         spec_ref[half:n] = jnp.where(first, 0.0, q0[half:])
         spec_ref[6 * n:6 * n + half] = jnp.where(first, 0.5 * q0[half:], q0[0:half])
         spec_ref[n:2 * n] = nn(t3[...], y3)
+        yield
         spec_ref[2 * n:4 * n] = nn(t1[...], y1)
         spec_ref[4 * n:6 * n] = nn(t2[...], y2)
-
-    edge, one, two = token_masks(seg_ref[pl.ds(r, 1), :], length, wide)
-    low = normed[rows, :]
-    mixed = []
-    for i, (w, sw) in enumerate(((wg_ref, swg_ref), (wi_ref, swi_ref), (wv_ref, swv_ref))):
-        at = pl.ds(pl.multiple_of(i * width + c * wide, wide), wide)
-        p = nn(low, w[...]) + mb_ref[at].reshape(1, wide)
-        proj_ref[i] = p.astype(bf)
-        m = (sb_ref[at].reshape(1, wide) + sw[0:1, :] * p + sw[1:2, :] * jnp.where(one, pltpu.roll(p, 1, 0), 0.0)
-            + sw[2:3, :] * jnp.where(two, pltpu.roll(p, 2, 0), 0.0))
-        mixed_ref[i] = m.astype(bf)
-        mixed.append(m)
-    inner = mixed[2] * mixed[1]
-    inner_low = inner.astype(bf).astype(f32)
-    conv = None
-    for d in range(DOCS):
-        x = jnp.where(edge, inner_low, 0.0) if d == 0 else jnp.where(edge, 0.0, inner_low)
-        ys = spread(x[0:n], x[n:2 * n], x[2 * n:])
-        parts = []
-        for s, off, m in specs_of(length, n):
+        yield
+        low_ref[...] = spec_ref[...].astype(bf)
+
+    mixed = [[None] * 3 for _ in range(rows_here)]
+    inner = [None] * rows_here
+    masks = [token_masks(seg_ref[r:r + 1, :], length, wide) for r in range(rows_here)]
+
+    def project(r):
+        rows = slice(r * length, (r + 1) * length)
+        edge, one, two = masks[r]
+        for i, (w, sw) in enumerate(((wg_ref, swg_ref), (wi_ref, swi_ref), (wv_ref, swv_ref))):
+            at = pl.ds(pl.multiple_of(i * width + c * wide, wide), wide)
+            p = nn(normed[rows, :], w[...]) + mb_ref[at].reshape(1, wide)
+            yield
+            proj_ref[i, rows, :] = p.astype(bf)
+            m = (sb_ref[at].reshape(1, wide) + sw[0:1, :] * p + sw[1:2, :] * jnp.where(one, pltpu.roll(p, 1, 0), 0.0)
+                + sw[2:3, :] * jnp.where(two, pltpu.roll(p, 2, 0), 0.0))
+            mixed_ref[i, rows, :] = m.astype(bf)
+            mixed[r][i] = m
+        inner[r] = mixed[r][2] * mixed[r][1]
+
+    def convolve(r):
+        rows = slice(r * length, (r + 1) * length)
+        edge = masks[r][0]
+        inner_low = inner[r].astype(bf).astype(f32)
+        xs = [jnp.where(edge, inner_low, 0.0), jnp.where(edge, 0.0, inner_low)]
+        ys = [jnp.concatenate(pair_of, 1) for pair_of in zip(*(spread(x[0:n], x[n:2 * n], x[2 * n:]) for x in xs))]
+        parts = {}
+        for s, off, m in specs_of(length, n)[::-1]:
             t, u = tables[s]
             p = nn(t[...], ys[s])
-            trans_ref[0, d, off:off + 2 * m, :] = p.astype(bf)
-            pa, pb = p[:m], p[m:]
+            yield
             qa, qb = spec_ref[off:off + m], spec_ref[off + m:off + 2 * m]
             qc = spec_ref[6 * n:6 * n + m] if s == 0 else qa
-            prod = jnp.concatenate([(pa * qa - pb * qb).astype(bf), (pa * qb + pb * qc).astype(bf)], 0)
-            parts.append(nn(u[...], prod))
-        y = jnp.concatenate(gather(*parts), 0)
-        conv = y if d == 0 else jnp.where(edge, conv, y)
-    longconv = conv * (1.0 / length) + skip_ref[pl.ds(pl.multiple_of(c * wide, wide), wide)].reshape(1, wide) * inner
-    long_ref[...] = longconv.astype(bf)
-    mix_ref[...] = (mixed[0] * longconv).astype(bf)
+            prod = []
+            for d in range(DOCS):
+                mine = p[:, d * wide:(d + 1) * wide]
+                trans_ref[r, d, off:off + 2 * m, :] = mine.astype(bf)
+                pa, pb = mine[:m], mine[m:]
+                prod.append(jnp.concatenate([(pa * qa - pb * qb).astype(bf), (pa * qb + pb * qc).astype(bf)], 0))
+            parts[s] = nn(u[...], jnp.concatenate(prod, 1))
+            yield
+        y = jnp.concatenate(gather(*(parts[s] for s in range(4))), 0)
+        conv = jnp.where(edge, y[:, :wide], y[:, wide:])
+        longconv = conv * (1.0 / length) + skip_ref[pl.ds(pl.multiple_of(c * wide, wide), wide)].reshape(1, wide) * inner[r]
+        long_ref[rows, :] = longconv.astype(bf)
+        mix_ref[rows, :] = (mixed[r][0] * longconv).astype(bf)
+
+    def row_stream(r):
+        yield from project(r)
+        yield from convolve(r)
+
+    interleave([spectrum()] + [row_stream(r) for r in range(rows_here)], LAG)
+
+
+LAG = 2
 
 
 def whole_spec(a):
@@ -353,15 +403,15 @@
 
 
 def column_spec(rows, k, count):
-    return pl.BlockSpec((rows, CHUNK), lambda c, r: (0, k * count + c))
+    return pl.BlockSpec((rows, CHUNK), lambda c, r=0: (0, k * count + c))
 
 
 def part_spec(length):
-    return pl.BlockSpec((length, CHUNK), lambda c, r: (r, c))
+    return pl.BlockSpec((length, CHUNK), lambda c, r=0: (r, c))
 
 
 def stack_spec(count, length):
-    return pl.BlockSpec((count, length, CHUNK), lambda c, r: (0, r, c))
+    return pl.BlockSpec((count, length, CHUNK), lambda c, r=0: (0, r, c))
 
 
 def vector_chunk():
@@ -377,21 +427,20 @@
     hidden = fw.shape[0]
     sds = jax.ShapeDtypeStruct
     ins = [tok, segments, g1, s1, wm, wm, wm, mb, sw, sw, sw, sb, skip, zt, *filt, rates, *tabs, *tabst]
-    specs = [pl.BlockSpec((length, width), lambda c, r: (jnp.where(c == 0, r, rows_here - 1), 0))]
-    specs += [whole_spec(a) for a in (segments, g1, s1)]
+    specs = [whole_spec(a) for a in (tok, segments, g1, s1)]
     specs += [column_spec(width, k, count) for k in range(3)] + [whole_spec(mb)] + [column_spec(3, k, count) for k in range(3)]
     specs += [whole_spec(sb), whole_spec(skip), whole_spec(zt)] + [whole_spec(a) for a in filt[:-1]]
     specs += [column_spec(hidden, 0, count), column_spec(1, 0, count)] + [whole_spec(a) for a in (*tabs, *tabst)]
     return pl.pallas_call(
-        forward_kernel, grid=(count, rows_here), in_specs=specs,
-        out_specs=[stack_spec(3, length), stack_spec(3, length), part_spec(length), part_spec(length),
-            pl.BlockSpec((1, DOCS, 2 * length, CHUNK), lambda c, r: (r, 0, 0, c)), column_spec(2 * length + n // 2, 0, count),
-            fixed_spec(9, hidden, length),
-            pl.BlockSpec((width, length), lambda c, r: (0, jnp.where(c == 0, r, rows_here - 1)))],
+        forward_kernel, grid=(count,), in_specs=specs,
+        out_specs=[stack_spec(3, total), stack_spec(3, total), part_spec(total), part_spec(total),
+            pl.BlockSpec((rows_here, DOCS, 2 * length, CHUNK), lambda c: (0, 0, 0, c)), column_spec(2 * length + n // 2, 0, count),
+            fixed_spec(9, hidden, length), fixed_spec(width, total)],
         out_shape=[sds((3, total, width), bf), sds((3, total, width), bf), sds((total, width), bf), sds((total, width), bf),
-            sds((rows_here, DOCS, 2 * length, width), bf), sds((2 * length + n // 2, width), f32),
+            sds((rows_here, DOCS, 2 * length, width), bf), sds((2 * length + n // 2, width), bf),
             sds((9, hidden, length), f32), sds((width, total), bf)],
-        scratch_shapes=[pltpu.VMEM((total, width), bf), pltpu.VMEM((zt.shape[0], hidden), f32)],
+        scratch_shapes=[pltpu.VMEM((total, width), bf), pltpu.VMEM((zt.shape[0], hidden), f32),
+            pltpu.VMEM((2 * length + n // 2, CHUNK), f32)],
         compiler_params=pltpu.CompilerParams(vmem_limit_bytes=VMEM_BYTES),
         cost_estimate=pl.CostEstimate(
             flops=total * width * (6 * width + 4 * 2 * 5 * n), bytes_accessed=40 * total * width, transcendentals=0),
@@ -597,9 +646,9 @@
         name="mlp")(mix, tok, cot, wo, bo, g2, s2, we, be, wr, br)
 
 
-def backward_kernel(links, plan, *refs):
+def backward_kernel(links, plan, sources, *refs):
     moved = len(plan)
-    grads, refs = refs[:moved], refs[moved:]
+    grads, refs = refs[:sources], refs[sources:]
     (dat_ref, tok_ref, seg_ref, g1_ref, wo_ref, long_ref, mixed_ref, proj_ref, trans_ref, spec_ref, nt_ref,
         wg_ref, wi_ref, wv_ref, swg_ref, swi_ref, swv_ref, skip_ref, state_ref, zt_ref, iw_ref, ow_ref, eo_ref, io_ref,
         oo_ref, fw_ref, rate_ref, t0, t3, t1, t2, u0, u3, u1, u2,
@@ -631,9 +680,9 @@
     if links:
         pair_s, pair_got, pair_send, pair_recv = pair[:4]
         rest = list(pair[4:])
-        for (alive, order), grad, out in zip(plan, grads, outs):
+        for (src, blocks, alive, order, _), out in zip(plan, outs):
             m = len(order)
-            jobs.append(Halving(grad, (0, grad.shape[alive.index(None)]), alive, order, rest[:2 * m - 1] + [out] + rest[2 * m - 1:2 * m + 1],
+            jobs.append(Halving(grads[src], blocks, alive, order, rest[:2 * m - 1] + [out] + rest[2 * m - 1:2 * m + 1],
                 rest[2 * m + 1]))
             rest = rest[2 * m + 2:]
 
@@ -655,21 +704,23 @@
 
         step = c * pl.num_programs(1) + r
 
-        def advance(when, stage):
-            @pl.when(step == when)
-            def _():
-                for job in jobs:
-                    if stage > 0:
-                        job.finish(stage - 1)
-                    if stage < len(job.order):
-                        job.start(stage)
-
         @pl.when(step == 0)
         def _():
-            meet([core] + list(dict.fromkeys(s for _, order in plan for s in order)))
-
-        for stage, when in enumerate(MOMENTS[:-1]):
-            advance(when, stage)
+            meet([core] + list(dict.fromkeys(s for job in plan for s in job[3] if s != core)))
+
+        def advance(job, stage):
+            if stage > 0:
+                job.finish(stage - 1)
+            if stage < len(job.order):
+                job.start(stage)
+
+        for now in range(MOMENTS):
+            due = [(job, entry[4].index(now)) for job, entry in zip(jobs, plan) if now in entry[4]]
+            if due:
+                @pl.when(step == now)
+                def _(due=due):
+                    for job, stage in due:
+                        advance(job, stage)
 
     def add(off, v):
         ds_s[off:off + v.shape[0], :] += v
@@ -691,8 +742,8 @@
             t, u = tables[s]
             g = nn(t[...], ys[s])
             ga, gb = g[:m], g[m:]
-            qa, qb = spec_ref[off:off + m], spec_ref[off + m:off + 2 * m]
-            qc = spec_ref[6 * n:6 * n + m] if s == 0 else qa
+            qa, qb = spec_ref[off:off + m].astype(f32), spec_ref[off + m:off + 2 * m].astype(f32)
+            qc = spec_ref[6 * n:6 * n + m].astype(f32) if s == 0 else qa
             pa, pb = trans_ref[0, d, off:off + m, :].astype(f32), trans_ref[0, d, off + m:off + 2 * m, :].astype(f32)
             back = jnp.concatenate([(ga * qa + gb * qb).astype(bf), (gb * qc - ga * qb).astype(bf)], 0)
             if s == 0:
@@ -786,10 +837,10 @@
                 job.finish(len(job.order) - 1)
 
 
-MOMENTS = (0, 3, 5, 6)
-
-
-def backward_mixer(links, weg, wrg, dat, tok, segments, g1, wo, longc, mixed, proj, trans, spec, ntr, wm, sw, skip, state, filt, zt, rates,
+MOMENTS = 6
+
+
+def backward_mixer(links, weg, wrg, wog, dat, tok, segments, g1, wo, longc, mixed, proj, trans, spec, ntr, wm, sw, skip, state, filt, zt, rates,
         tabs, tabst):
     rows_here, length = segments.shape
     total, width = tok.shape
@@ -807,12 +858,19 @@
         pair = (3, CHUNK // LANES, rows_n // 2, width // rows_n, LANES)
         wm_shape = (3, wide_blocks, *pair[2:])
         scratch = [pltpu.VMEM((2, *pair), bf), pltpu.VMEM((2, *pair), bf), pltpu.SemaphoreType.DMA, pltpu.SemaphoreType.DMA((2,))]
-        for grad, rows_of, first in ((weg, width, "pos"), (wrg, wrg.shape[1] * wrg.shape[2] * wrg.shape[3] * 2, "rows")):
-            grad = grad.reshape(grad_shape(grad.shape[0], rows_of, rows_n, pos_n, False))
-            order = order_of(rows_n, pos_n, first)[1:-1]
-            left = job_shapes(grad.shape, grad.shape[alive.index(None)], alive, order)
-            plan.append((alive, order))
-            grads.append(grad)
+        full = alive_dims(rows_n, pos_n)
+        rows_of = wrg.shape[1] * wrg.shape[2] * wrg.shape[3] * 2
+        grads = [weg.reshape(grad_shape(weg.shape[0], width, rows_n, pos_n, False)),
+            wrg.reshape(grad_shape(wrg.shape[0], rows_of, rows_n, pos_n, False)),
+            wog.reshape(grad_shape(wog.shape[0], width, rows_n, pos_n, True))]
+        e_blocks, r_blocks, o_blocks = (g.shape[bits_of(pos_n)] for g in grads)
+        first, second, third = three_orders(rows_n, pos_n)
+        cut_e, cut_r = 2 * e_blocks // 3, 2 * r_blocks // 3
+        plan = [(0, (0, cut_e), alive, first, (0, 3, 4, 5)), (1, (0, cut_r), alive, second, (0, 3, 4, 5)),
+            (0, (cut_e, e_blocks - cut_e), alive, third, (0, 3, 4, 5)), (1, (cut_r, r_blocks - cut_r), alive, third, (0, 3, 4, 5)),
+            (2, (0, o_blocks), full, [("rows", 0)] + first, (0, 1, 3, 4, 5))]
+        for src, (_, blocks), dims, order, _ in plan:
+            left = job_shapes(grads[src].shape, blocks, dims, order)
             moved.append(left[-1])
             scratch += job_scratch(left, False) + [pltpu.SemaphoreType.DMA]
     side = dict(collective_id=2, has_side_effects=True) if links else {}
@@ -827,7 +885,7 @@
     specs += [whole_spec(a) for a in (skip, state, zt, iw, ow, eo, io, oo)]
     specs += [column_spec(hidden, 0, count), column_spec(1, 0, count)] + [whole_spec(a) for a in (*tabs, *tabst)]
     return pl.pallas_call(
-        functools.partial(backward_kernel, links, plan), grid=(count, rows_here), in_specs=specs,
+        functools.partial(backward_kernel, links, plan, len(grads)), grid=(count, rows_here), in_specs=specs,
         out_specs=[pl.BlockSpec((length, width), late, pipeline_mode=pl.Buffered(1)),
             single(*wm_shape),
             pl.BlockSpec((3, 8, CHUNK), lambda c, r: (0, 0, c)), fixed_spec(8, width), fixed_spec(zt.shape[0], hidden),
@@ -909,25 +967,29 @@
 
 def exchange_kernel(sizes, at, plan, count, *refs):
     rows_n, pos_n = sizes
-    n = rows_n * pos_n
     small = refs[:9]
     grads = refs[9:9 + count]
     pos = 9 + count
     packed_out = refs[pos]
     outs = refs[pos + 1:pos + 1 + len(plan)]
     scratch = list(refs[pos + 1 + len(plan):])
-    pk, rbuf, red, gath, ss1, rs1, ss2, rs2 = scratch[:8]
-    rest = scratch[8:]
+    pk, from_twin, half, rbuf, red, gath, ss1, rs1, ss2, rs2, pair_sems = scratch[:11]
+    rest = scratch[11:]
     jobs = []
     for (src, blocks, alive, order), out in zip(plan, outs):
         m = len(order)
         jobs.append(Halving(grads[src], blocks, alive, order, rest[:2 * m - 1] + [out] + rest[2 * m - 1:2 * m + 1]))
         rest = rest[2 * m + 1:]
-    me = lax.axis_index("rows") * pos_n + lax.axis_index("pos")
-    chunk = pk.shape[0] // n
+    n = rows_n * pos_n // 2
+    side = pk.shape[0] // 2
+    chunk = side // n
+    place = lax.axis_index("rows")
+    core = lax.rem(place, 2)
+    me = (place // 2) * pos_n + lax.axis_index("pos")
+    twin = {"rows": place + 1 - 2 * core}
 
     def ident(t):
-        return {"rows": t // pos_n, "pos": t % pos_n}
+        return {"rows": (t // pos_n) * 2 + core, "pos": t % pos_n}
 
     def each(f):
         def body(k, carry):
@@ -936,45 +998,67 @@
 
         lax.fori_loop(1, n, body, 0)
 
-    def part(t):
+    def own(t):
         return pl.ds(pl.multiple_of(t * chunk, chunk), chunk)
 
+    def at_side(which, t=None):
+        if t is None:
+            return pl.ds(pl.multiple_of(which * side, side), side)
+        return pl.ds(pl.multiple_of(which * side + t * chunk, chunk), chunk)
+
     barrier = pltpu.get_barrier_semaphore()
+    pl.semaphore_signal(barrier, inc=1, device_id=twin, device_id_type=MESH)
     each(lambda t: pl.semaphore_signal(barrier, inc=1, device_id=ident(t), device_id_type=MESH))
     pk[...] = jnp.zeros_like(pk)
     pack_small(at, pk, *small)
-    pl.semaphore_wait(barrier, n - 1)
+    pl.semaphore_wait(barrier, n)
+
+    to_twin = pltpu.make_async_remote_copy(
+        src_ref=pk.at[at_side(1 - core), :], dst_ref=from_twin, send_sem=pair_sems.at[0], recv_sem=pair_sems.at[1],
+        device_id=twin, device_id_type=MESH)
+    back_twin = pltpu.make_async_remote_copy(
+        src_ref=gath.at[at_side(core), :], dst_ref=gath.at[at_side(core), :], send_sem=pair_sems.at[2],
+        recv_sem=pair_sems.at[3], device_id=twin, device_id_type=MESH)
 
     def scatter(t, slot):
         return pltpu.make_async_remote_copy(
-            src_ref=pk.at[part(t), :], dst_ref=rbuf.at[slot], send_sem=ss1.at[t], recv_sem=rs1.at[slot], device_id=ident(t),
+            src_ref=half.at[own(t), :], dst_ref=rbuf.at[slot], send_sem=ss1.at[t], recv_sem=rs1.at[slot], device_id=ident(t),
             device_id_type=MESH)
 
     def publish(t, slot):
         return pltpu.make_async_remote_copy(
-            src_ref=red, dst_ref=gath.at[part(slot), :], send_sem=ss2.at[t], recv_sem=rs2.at[slot], device_id=ident(t),
-            device_id_type=MESH)
-
-    for job in jobs:
-        job.start(0)
-    each(lambda t: scatter(t, me).start())
-    rbuf[me] = pk[part(me), :]
-    stages = max(len(job.order) for job in jobs)
-    for stage in range(stages):
+            src_ref=red, dst_ref=gath.at[at_side(core, slot), :], send_sem=ss2.at[t], recv_sem=rs2.at[slot],
+            device_id=ident(t), device_id_type=MESH)
+
+    def advance(stage):
         for job in jobs:
             if stage < len(job.order):
                 job.finish(stage)
                 if stage + 1 < len(job.order):
                     job.start(stage + 1)
-        if stage == 0:
-            each(lambda t: scatter(t, t).wait())
-            total = rbuf[0]
-            for s in range(1, n):
-                total = total + rbuf[s]
-            red[...] = total
-            gath[part(me), :] = total
-            each(lambda t: publish(t, me).start())
+
+    to_twin.start()
+    for job in jobs:
+        job.start(0)
+    to_twin.wait()
+    half[...] = pk[at_side(core), :] + from_twin[...]
+    each(lambda t: scatter(t, me).start())
+    rbuf[me] = half[own(me), :]
+    advance(0)
+    each(lambda t: scatter(t, t).wait())
+    total = rbuf[0]
+    for s in range(1, n):
+        total = total + rbuf[s]
+    red[...] = total
+    gath[at_side(core, me), :] = total
+    each(lambda t: publish(t, me).start())
+    stages = max(len(job.order) for job in jobs)
+    for stage in range(1, stages - 1):
+        advance(stage)
     each(lambda t: publish(t, t).wait())
+    back_twin.start()
+    advance(stages - 1)
+    back_twin.wait()
     packed_out[...] = gath[...]
 
 
@@ -984,8 +1068,9 @@
     total = -(-used // (8 * n)) * 8 * n
     chunk = total // n
     vm = pl.BlockSpec(memory_space=pltpu.VMEM)
-    scratch = [pltpu.VMEM((total, PACK), f32), pltpu.VMEM((n, chunk, PACK), f32), pltpu.VMEM((chunk, PACK), f32),
-        pltpu.VMEM((total, PACK), f32)] + [pltpu.SemaphoreType.DMA((n,))] * 4
+    tall = lambda rows: pltpu.VMEM((rows, PACK), f32)
+    scratch = [tall(total), tall(total // 2), tall(total // 2), pltpu.VMEM((n // 2, chunk, PACK), f32), tall(chunk), tall(total)]
+    scratch += [pltpu.SemaphoreType.DMA((n // 2,))] * 4 + [pltpu.SemaphoreType.DMA((4,))]
     shapes = [jax.ShapeDtypeStruct((total, PACK), f32)]
     for src, (start, blocks), alive, order in plan:
         left = job_shapes(grads[src].shape, blocks, alive, order)
@@ -998,12 +1083,20 @@
         name="exchange")(*small, *grads)
 
 
-def unpack(at, packed, blocks, width, hidden, emb, ff):
+def unpack(at, packed, results, blocks, width, hidden, emb, ff):
     per = width // PACK
     counts = [len(parts) for parts in blocks]
     flat = [p for parts in blocks for p in parts]
 
     def kernel(pk, *refs):
+        copies = []
+        if results:
+            sems, refs = refs[-1], refs[:-1]
+            m = len(results)
+            copies = [pltpu.make_async_copy(a, b, sems.at[k]) for k, (a, b) in enumerate(zip(refs[:m], refs[-m:]))]
+            refs = refs[m:-m]
+        for copy in copies:
+            copy.start()
         ins = list(refs[:len(flat)])
         fg, fs, mb, sw, sb, ew, eb, eo, iw, ib, io, ow, ob, oo, fw, sk, obias, sg, ss, eb2, rb = refs[len(flat):len(flat) + 21]
         outs = refs[len(flat) + 21:]
@@ -1042,15 +1135,21 @@
                 for b in range(src.shape[0]):
                     out[:, lane:lane + src.shape[2]] = src[b].astype(f32)
                     lane += src.shape[2]
+        for copy in copies:
+            copy.wait()
 
     s = lambda *d: jax.ShapeDtypeStruct(d, f32)
     shapes = [s(width), s(width), s(3 * width), s(3, 3 * width), s(3 * width), s(emb, hidden), s(hidden), s(hidden),
         s(hidden, hidden), s(hidden), s(hidden), s(hidden, hidden), s(hidden), s(hidden), s(hidden, width), s(width), s(width),
         s(width), s(width), s(ff), s(width)]
     shapes += [s(parts[0].shape[1], sum(p.shape[0] for p in parts) * parts[0].shape[2]) for parts in blocks]
+    shapes += [jax.ShapeDtypeStruct(a.shape, a.dtype) for a in results]
     vm = pl.BlockSpec(memory_space=pltpu.VMEM)
+    far = [pl.BlockSpec(memory_space=pl.ANY)] * len(results)
     return pl.pallas_call(
-        kernel, out_shape=shapes, in_specs=[vm] * (1 + len(flat)), out_specs=[vm] * len(shapes), name="unpack")(packed, *flat)
+        kernel, out_shape=shapes, in_specs=[vm] + far + [vm] * len(flat), out_specs=[vm] * (len(shapes) - len(results)) + far,
+        scratch_shapes=[pltpu.SemaphoreType.DMA((len(results),))] if results else [],
+        compiler_params=pltpu.CompilerParams(vmem_limit_bytes=VMEM_BYTES), name="unpack")(packed, *results, *flat)
 
 
 def on_device(sizes, tokens, segments, cotangent, first_gain, first_shift, mixer_weight, mixer_bias, short_weight, short_bias,
@@ -1070,38 +1169,33 @@
     proj, mixed, longc, mix, trans, spec, state, ntr = forward_mixer(
         tok, segments, first_gain, first_shift, mixer_weight, mixer_bias, short_weight, short_bias, skip_gain, filt, zt, rates,
         tabs, tabst)
-    direct = rows_n * pos_n <= 32 and width % (16 * rows_n) == 0 and width // LANES % pos_n == 0 and ff // rows_n * 4 == width
+    direct = rows_n * pos_n == 32 and pos_n == 2 and width % (16 * rows_n) == 0 and width // LANES % pos_n == 0 and ff // rows_n * 4 == width
     links = sizes if direct else None
     out, dat, wog, weg, wrg, beg, vec2 = mlp(
         links, mix, tok, cot, output_weight, output_bias, second_gain, second_shift, expand_weight, expand_bias, reduce_weight,
         reduce_bias)
     tgrad, wmg, sgrad, vec1, gew, giw, gow, gfw, gsm, *early = backward_mixer(
-        links, weg, wrg, dat, tok, segments, first_gain, output_weight, longc, mixed, proj, trans, spec, ntr, mixer_weight,
+        links, weg, wrg, wog, dat, tok, segments, first_gain, output_weight, longc, mixed, proj, trans, spec, ntr, mixer_weight,
         short_weight, skip_gain, state, filt, zt, rates, tabs, tabst)
     small = (beg, vec2, sgrad, vec1, gew, giw, gow, gfw, gsm)
     at, used = pack_places(width, hidden, emb, ff)
     blocks_m, blocks_o = 3 * width // LANES, width // LANES
     if direct:
-        alive = alive_dims(rows_n, pos_n)
-        core = [("rows", 0)]
-        paired = [d for d in alive if d not in core]
-        by_pos, by_rows = order_of(rows_n, pos_n, "pos"), order_of(rows_n, pos_n, "rows")
-        half_m = blocks_m // pos_n
-        cut = (half_m + 1) // 2
-        grads = [wmg.reshape(grad_shape(blocks_m, width, rows_n, pos_n, False)),
-            wog.reshape(grad_shape(blocks_o, width, rows_n, pos_n, True)), *early]
-        left = [d for d in alive if d is None or d in by_pos[-1:]]
-        plan = [(0, (0, cut), paired, by_pos[1:]), (0, (cut, half_m - cut), paired, by_rows[1:]),
-            (1, (0, blocks_o // pos_n), alive, by_rows), (2, (0, early[0].shape[0]), left, by_pos[-1:]),
-            (3, (0, early[1].shape[0]), left, by_pos[-1:])]
-        packed, m_a, m_b, o_part, e_part, r_part = exchange(sizes, at, used, small, grads, plan)
-        blocks = [[m_a, m_b], [o_part], [e_part], [r_part]]
+        paired = [d for d in alive_dims(rows_n, pos_n) if d != ("rows", 0)]
+        third = blocks_m // pos_n // 3
+        grads = [wmg.reshape(grad_shape(blocks_m, width, rows_n, pos_n, False))]
+        plan = [(0, (k * third, third), paired, order) for k, order in enumerate(three_orders(rows_n, pos_n))]
+        packed, *m_parts = exchange(sizes, at, used, small, grads, plan)
+        e_a, r_a, e_b, r_b, o_part = early
+        blocks = [m_parts, [o_part], [e_a, e_b], [r_a, r_b]]
     else:
         packed = lax.psum(pack_only(at, used, small), ("rows", "pos"))
         grads = [wmg.reshape(blocks_m, width, LANES), wog, weg, wrg]
         blocks = [[scatter_blocks(g, rows_n, pos_n, f)] for g, f in zip(grads, ("pos", "rows", "pos", "rows"))]
-    (fg, fs, mb, sw, sb, ew, eb, eo, iw, ib, io, ow, ob, oo, fw, sk, obias, sg, ss, eb2, rb, m_grad, o_grad, e_grad, r_grad) = unpack(
-        at, packed, blocks, width, hidden, emb, ff)
+    (fg, fs, mb, sw, sb, ew, eb, eo, iw, ib, io, ow, ob, oo, fw, sk, obias, sg, ss, eb2, rb, m_grad, o_grad, e_grad, r_grad, *results) = unpack(
+        at, packed, [], blocks, width, hidden, emb, ff)
+    if results:
+        out, tgrad = results
     return (out.reshape(tokens.shape), tgrad.reshape(tokens.shape), fg, fs, m_grad, mb, sw, sb, ew, eb, eo, iw, ib, io, ow, ob,
         oo, fw, sk, o_grad, obias, sg, ss, e_grad, eb2, r_grad, rb)
 

time: 266 us -> 246 us (0.925); the launches traced: 265 us -> 242 us
  Pallas kernels: 260 us -> 237 us
    pallas_call x1, Pallas kernels: 52.9 us -> 30.2 us  [exchange(): pl.pallas_call(functools.partial(exchange_kernel, sizes, at, plan, len(gr...]
where the time goes in v4:
time: 246 us; the launch traced here: 242 us
  Pallas kernels  237 us (96%)
  local copies, waits for them, and re-layouts  4.78 us (2%)
    pallas_call x1, Pallas kernels, backward_mixer(): pl.pallas_call(functools.partial(backward_kernel, links, plan, len(grads)...  89.6 us
    pallas_call x1, Pallas kernels, mlp(): pl.pallas_call(functools.partial(mlp_kernel, links), grid=(parts,), in_sp...  78.6 us
    pallas_call x1, Pallas kernels, forward_mixer(): pl.pallas_call(forward_kernel, grid=(count,), in_specs=specs, out_specs=[...  35.9 us
    pallas_call x1, Pallas kernels, exchange(): pl.pallas_call(functools.partial(exchange_kernel, sizes, at, plan, len(gr...  30.2 us

profile of v4, /device:TPU:0, one launch (start us, length us, event | category | flops | bytes accessed | tf_op | source)
XLA Modules:
  0.0 242.3 jit_solution(14959500128380824557)
XLA Ops:
  0.7 35.9 %mixer_forward.1 = (bf16[3,1536,768]{2,1,0:T(8,128)(2,1)}, bf16[3,1536,768]{2,1,0:T(8,128)(2,1)}, bf16[1536,768]{1,0:T(8,128)(2,1)}, bf16[1536,768]{1,0:T(8,128)...) custom-call(bf16[1536,768]{1,0:T(8,128)(2,1)} %bitcast.12, ...), custom_call_target="tpu_custom_call" | custom-call | flops 17515413504 | bytes 47185920 | tf_op jit(solution)/shard_map/mixer_forward/pallas_call | solution.py:434
  36.6 78.6 %mlp.1 = (bf16[1536,768]{1,0:T(8,128)(2,1)}, bf16[1536,768]{1,0:T(8,128)(2,1)}, bf16[6,768,128]{2,1,0:T(8,128)(2,1)}, bf16[24,8,48,128]{3,2,1,0:T(8,128)(2,1)}, ...) custom-call(bf16[1536,768]{1,0:T(8,128)(2,1)} %get-tuple-element.85.mix_ref, ...), custom_call_target="tpu_custom_call" | custom-call | flops 47110422528 | bytes 35389440 | tf_op jit(solution)/shard_map/mlp/pallas_call | solution.py:632
  115.2 89.6 %mixer_backward.1 = (bf16[1536,768]{1,0:T(8,128)(2,1)}, bf16[3,6,8,48,128]{4,3,2,1,0:T(8,128)(2,1)}, f32[3,8,768]{2,1,0:T(8,128)}, f32[8,768]{1,0:T(8,128)}, f32...) custom-call(bf16[2,12,2,2,2,48,128]{6,5,4,3,2,1,0:T(8,128)(2,1)} %bi, ...), custom_call_target="tpu_custom_call" | custom-call | flops 24763170816 | bytes 58982400 | tf_op jit(solution)/shard_map/mixer_backward/pallas_call | solution.py:887
  204.8 30.2 %exchange.1 = (f32[256,384]{1,0:T(8,128)}, bf16[3,48,128]{2,1,0:T(8,128)(2,1)}, bf16[3,48,128]{2,1,0:T(8,128)(2,1)}, bf16[3,48,128]{2,1,0:T(8,128)(2,1)}) custom-call(f32[1,3072]{1,0:T(1,128)} %get-tuple-element.99.refs_0_, f32[8,768]{1,0:T(8,128)} %get-tuple-element.100.refs_1_, f32[3,8,768]{2,1,0:T(8,128)} %get-tuple-element.101.refs_2_, ...), custom_call_target="tpu_custom_call" | custom-call | tf_op jit(solution)/shard_map/exchange/pallas_call | solution.py:1079
  235.0 2.3 unpack.1
  237.3 0.0 copy-start
  237.3 3.4 %copy.67 = bf16[2,768,768]{2,1,0:T(8,128)(2,1)} copy(bf16[2,768,768]{2,1,0:T(8,128)(2,1)} %bitcast.8) | data formatting | bytes 4718592
  240.7 0.0 copy-done
  240.7 1.4 copy.68
Async XLA Ops:
  237.3 3.4 %copy-start = (bf16[1536,768]{1,0:T(8,128)(2,1)S(1)}, bf16[1536,768]{1,0:T(8,128)(2,1)}, u32[]{:S(2)}) copy-start(bf16[1536,768]{1,0:T(8,128)(2,1)} %get-tuple-element.98) | copy-start | bytes 7077892

commit v5 on v4

--- a/solution.py
+++ b/solution.py
@@ -192,11 +192,14 @@
     return mine, {axis: place + (1 - 2 * mine) * (1 << bit)}
 
 
-def meet(steps):
+def greet(steps):
     barrier = pltpu.get_barrier_semaphore()
     for step in steps:
         pl.semaphore_signal(barrier, inc=1, device_id=partner(step)[1], device_id_type=MESH)
-    pl.semaphore_wait(barrier, len(steps))
+
+
+def meet(steps):
+    pl.semaphore_wait(pltpu.get_barrier_semaphore(), len(steps))
 
 
 class Halving:
@@ -500,7 +503,7 @@
     @pl.when(j == 0)
     def _():
         if links:
-            meet([core])
+            greet([core])
 
         def body(i, carry):
             rows = at(i)
@@ -566,6 +569,10 @@
 
     lax.fori_loop(0, width // 384, grads, 0)
     if links:
+        @pl.when(j == 0)
+        def _():
+            meet([core])
+
         for copy in copies(j):
             copy.start()
 
@@ -649,11 +656,11 @@
 def backward_kernel(links, plan, sources, *refs):
     moved = len(plan)
     grads, refs = refs[:sources], refs[sources:]
-    (dat_ref, tok_ref, seg_ref, g1_ref, wo_ref, long_ref, mixed_ref, proj_ref, trans_ref, spec_ref, nt_ref,
-        wg_ref, wi_ref, wv_ref, swg_ref, swi_ref, swv_ref, skip_ref, state_ref, zt_ref, iw_ref, ow_ref, eo_ref, io_ref,
+    (dat_ref, tok_ref, seg_ref, g1_ref, wo_ref, long_ref, mixed_ref, proj_ref, trans_ref, spec_ref, nt_far,
+        wg_ref, wi_ref, wv_ref, swg_ref, swi_ref, swv_ref, skip_ref, state_far, zt_ref, iw_ref, ow_ref, eo_ref, io_ref,
         oo_ref, fw_ref, rate_ref, t0, t3, t1, t2, u0, u3, u1, u2,
         tg_ref, wgrad_ref, sg_ref, vec_ref, gew_ref, giw_ref, gow_ref, gfw_ref, gsm_ref) = refs[:44]
-    outs, (dn, de3, dp_s, ds_s, *pair) = refs[44:44 + moved], refs[44 + moved:]
+    outs, (dn, de3, dp_s, ds_s, nt_ref, state_ref, late_sems, *pair) = refs[44:44 + moved], refs[44 + moved:]
     c = pl.program_id(0)
     r = pl.program_id(1)
     chunks = pl.num_programs(0)
@@ -663,6 +670,13 @@
     half = n // 2
     rows = pl.ds(pl.multiple_of(r * length, length), length)
     tables = ((t0, u0), (t3, u3), (t1, u1), (t2, u2))
+
+    late_copies = [pltpu.make_async_copy(a, b, late_sems.at[k]) for k, (a, b) in enumerate(((nt_far, nt_ref), (state_far, state_ref)))]
+
+    @pl.when(jnp.logical_and(c == 0, r == 0))
+    def _():
+        for copy in late_copies:
+            copy.start()
 
     @pl.when(r == 0)
     def _():
@@ -704,9 +718,15 @@
 
         step = c * pl.num_programs(1) + r
 
+        partners = [core] + list(dict.fromkeys(s for job in plan for s in job[3] if s != core))
+
         @pl.when(step == 0)
         def _():
-            meet([core] + list(dict.fromkeys(s for job in plan for s in job[3] if s != core)))
+            greet(partners)
+
+        @pl.when(step == 0)
+        def _():
+            meet(partners)
 
         def advance(job, stage):
             if stage > 0:
@@ -767,6 +787,11 @@
         dp_s[i, rows, :] = dp
         dn[rows, :] += nt(dp, w[...])
 
+    @pl.when(jnp.logical_and(c == 0, r == last_row))
+    def _():
+        for copy in late_copies:
+            copy.wait()
+
     @pl.when(r == last_row)
     def _():
         if links:
@@ -880,13 +905,13 @@
     specs = [pl.BlockSpec(memory_space=pl.ANY) for g in grads] + [whole_spec(dat), pl.BlockSpec((length, width), late, pipeline_mode=pl.Buffered(1)), whole_spec(segments), whole_spec(g1),
         pl.BlockSpec((CHUNK, width), lambda c, r: (c, 0)), part_spec(length), stack_spec(3, length), stack_spec(3, length),
         pl.BlockSpec((1, DOCS, 2 * length, CHUNK), lambda c, r: (r, 0, 0, c)), column_spec(2 * length + n // 2, 0, count),
-        whole_spec(ntr)]
+        pl.BlockSpec(memory_space=pl.ANY)]
     specs += [column_spec(width, k, count) for k in range(3)] + [column_spec(3, k, count) for k in range(3)]
-    specs += [whole_spec(a) for a in (skip, state, zt, iw, ow, eo, io, oo)]
+    specs += [whole_spec(skip), pl.BlockSpec(memory_space=pl.ANY)] + [whole_spec(a) for a in (zt, iw, ow, eo, io, oo)]
     specs += [column_spec(hidden, 0, count), column_spec(1, 0, count)] + [whole_spec(a) for a in (*tabs, *tabst)]
     return pl.pallas_call(
         functools.partial(backward_kernel, links, plan, len(grads)), grid=(count, rows_here), in_specs=specs,
-        out_specs=[pl.BlockSpec((length, width), late, pipeline_mode=pl.Buffered(1)),
+        out_specs=[pl.BlockSpec((length, width), late),
             single(*wm_shape),
             pl.BlockSpec((3, 8, CHUNK), lambda c, r: (0, 0, c)), fixed_spec(8, width), fixed_spec(zt.shape[0], hidden),
             fixed_spec(hidden, hidden), fixed_spec(hidden, hidden), column_spec(hidden, 0, count), fixed_spec(6, 8, hidden)]
@@ -896,7 +921,8 @@
             sds((hidden, width), f32), sds((6, 8, hidden), f32)]
             + [sds(s, bf) for s in moved],
         scratch_shapes=[pltpu.VMEM((total, width), f32), pltpu.VMEM((hidden, length), f32), pltpu.VMEM((3, total, CHUNK), bf),
-            pltpu.VMEM((6 * n + n // 2, CHUNK), f32)] + scratch,
+            pltpu.VMEM((6 * n + n // 2, CHUNK), f32), pltpu.VMEM(ntr.shape, bf), pltpu.VMEM(state.shape, f32),
+            pltpu.SemaphoreType.DMA((2,))] + scratch,
         compiler_params=pltpu.CompilerParams(vmem_limit_bytes=VMEM_BYTES, **side),
         cost_estimate=pl.CostEstimate(
             flops=total * width * (14 * width + 4 * 2 * 5 * n), bytes_accessed=50 * total * width, transcendentals=0),
@@ -1089,14 +1115,15 @@
     flat = [p for parts in blocks for p in parts]
 
     def kernel(pk, *refs):
-        copies = []
-        if results:
-            sems, refs = refs[-1], refs[:-1]
-            m = len(results)
-            copies = [pltpu.make_async_copy(a, b, sems.at[k]) for k, (a, b) in enumerate(zip(refs[:m], refs[-m:]))]
-            refs = refs[m:-m]
-        for copy in copies:
-            copy.start()
+        m = len(results)
+        for a, b in zip(refs[:m], refs[len(refs) - m:]):
+            b[...] = a[...]
+
+        @pl.when(pl.program_id(0) == 0)
+        def _():
+            small(pk, *refs[m:len(refs) - m])
+
+    def small(pk, *refs):
         ins = list(refs[:len(flat)])
         fg, fs, mb, sw, sb, ew, eb, eo, iw, ib, io, ow, ob, oo, fw, sk, obias, sg, ss, eb2, rb = refs[len(flat):len(flat) + 21]
         outs = refs[len(flat) + 21:]
@@ -1135,20 +1162,18 @@
                 for b in range(src.shape[0]):
                     out[:, lane:lane + src.shape[2]] = src[b].astype(f32)
                     lane += src.shape[2]
-        for copy in copies:
-            copy.wait()
 
     s = lambda *d: jax.ShapeDtypeStruct(d, f32)
     shapes = [s(width), s(width), s(3 * width), s(3, 3 * width), s(3 * width), s(emb, hidden), s(hidden), s(hidden),
         s(hidden, hidden), s(hidden), s(hidden), s(hidden, hidden), s(hidden), s(hidden), s(hidden, width), s(width), s(width),
         s(width), s(width), s(ff), s(width)]
     shapes += [s(parts[0].shape[1], sum(p.shape[0] for p in parts) * parts[0].shape[2]) for parts in blocks]
-    shapes += [jax.ShapeDtypeStruct(a.shape, a.dtype) for a in results]
-    vm = pl.BlockSpec(memory_space=pltpu.VMEM)
-    far = [pl.BlockSpec(memory_space=pl.ANY)] * len(results)
+    steps = 6 if results else 1
+    whole = lambda a: pl.BlockSpec(a.shape, lambda i: (0,) * len(a.shape))
+    part = [pl.BlockSpec((a.shape[0] // steps, a.shape[1]), lambda i: (i, 0)) for a in results]
     return pl.pallas_call(
-        kernel, out_shape=shapes, in_specs=[vm] + far + [vm] * len(flat), out_specs=[vm] * (len(shapes) - len(results)) + far,
-        scratch_shapes=[pltpu.SemaphoreType.DMA((len(results),))] if results else [],
+        kernel, grid=(steps,), out_shape=shapes + [jax.ShapeDtypeStruct(a.shape, a.dtype) for a in results],
+        in_specs=[whole(packed)] + part + [whole(a) for a in flat], out_specs=[whole(a) for a in shapes] + part,
         compiler_params=pltpu.CompilerParams(vmem_limit_bytes=VMEM_BYTES), name="unpack")(packed, *results, *flat)
 
 
@@ -1193,7 +1218,7 @@
         grads = [wmg.reshape(blocks_m, width, LANES), wog, weg, wrg]
         blocks = [[scatter_blocks(g, rows_n, pos_n, f)] for g, f in zip(grads, ("pos", "rows", "pos", "rows"))]
     (fg, fs, mb, sw, sb, ew, eb, eo, iw, ib, io, ow, ob, oo, fw, sk, obias, sg, ss, eb2, rb, m_grad, o_grad, e_grad, r_grad, *results) = unpack(
-        at, packed, [], blocks, width, hidden, emb, ff)
+        at, packed, [out, tgrad] if direct else [], blocks, width, hidden, emb, ff)
     if results:
         out, tgrad = results
     return (out.reshape(tokens.shape), tgrad.reshape(tokens.shape), fg, fs, m_grad, mb, sw, sb, ew, eb, eo, iw, ib, io, ow, ob,

time: 246 us -> 242 us (0.984)
  local copies, waits for them, and re-layouts: 4.78 us -> 0 us
    unnamed x4 -> x0, local copies, waits for them, and re-layouts: 4.78 us -> none
    pallas_call x1, Pallas kernels: 2.29 us -> 6.86 us  [unpack(): pl.pallas_call(kernel, grid=(steps,), out_shape=shapes + [jax.ShapeDtypeS...]
    pallas_call x1, Pallas kernels: 89.6 us -> 86.7 us  [backward_mixer(): pl.pallas_call(functools.partial(backward_kernel, links, plan, len(grads)...]
where the time goes in v5:
time: 242 us; the launch traced here: 239 us
  Pallas kernels  238 us (98%)
    pallas_call x1, Pallas kernels, backward_mixer(): pl.pallas_call(functools.partial(backward_kernel, links, plan, len(grads)...  86.7 us
    pallas_call x1, Pallas kernels, mlp(): pl.pallas_call(functools.partial(mlp_kernel, links), grid=(parts,), in_sp...  78.2 us
    pallas_call x1, Pallas kernels, forward_mixer(): pl.pallas_call(forward_kernel, grid=(count,), in_specs=specs, out_specs=[...  35.9 us
    pallas_call x1, Pallas kernels, exchange(): pl.pallas_call(functools.partial(exchange_kernel, sizes, at, plan, len(gr...  30.4 us
    pallas_call x1, Pallas kernels, unpack(): pl.pallas_call(kernel, grid=(steps,), out_shape=shapes + [jax.ShapeDtypeS...  6.86 us

profile of v5, /device:TPU:0, one launch (start us, length us, event | category | flops | bytes accessed | tf_op | source)
XLA Modules:
  0.0 239.0 jit_solution(2327675590422421965)
XLA Ops:
  0.7 35.9 %mixer_forward.1 = (bf16[3,1536,768]{2,1,0:T(8,128)(2,1)}, bf16[3,1536,768]{2,1,0:T(8,128)(2,1)}, bf16[1536,768]{1,0:T(8,128)(2,1)}, bf16[1536,768]{1,0:T(8,128)...) custom-call(bf16[1536,768]{1,0:T(8,128)(2,1)} %bitcast.10, ...), custom_call_target="tpu_custom_call" | custom-call | flops 17515413504 | bytes 47185920 | tf_op jit(solution)/shard_map/mixer_forward/pallas_call | solution.py:437
  36.6 78.2 %mlp.1 = (bf16[1536,768]{1,0:T(8,128)(2,1)}, bf16[1536,768]{1,0:T(8,128)(2,1)}, bf16[6,768,128]{2,1,0:T(8,128)(2,1)}, bf16[24,8,48,128]{3,2,1,0:T(8,128)(2,1)}, ...) custom-call(bf16[1536,768]{1,0:T(8,128)(2,1)} %get-tuple-element.87.mix_ref, ...), custom_call_target="tpu_custom_call" | custom-call | flops 47110422528 | bytes 35389440 | tf_op jit(solution)/shard_map/mlp/pallas_call | solution.py:639
  114.8 86.7 %mixer_backward.1 = (bf16[1536,768]{1,0:T(8,128)(2,1)}, bf16[3,6,8,48,128]{4,3,2,1,0:T(8,128)(2,1)}, f32[3,8,768]{2,1,0:T(8,128)}, f32[8,768]{1,0:T(8,128)}, f32...) custom-call(bf16[2,12,2,2,2,48,128]{6,5,4,3,2,1,0:T(8,128)(2,1)} %bi, ...), custom_call_target="tpu_custom_call" | custom-call | flops 24763170816 | bytes 58982400 | tf_op jit(solution)/shard_map/mixer_backward/pallas_call | solution.py:912
  201.5 30.4 %exchange.1 = (f32[256,384]{1,0:T(8,128)}, bf16[3,48,128]{2,1,0:T(8,128)(2,1)}, bf16[3,48,128]{2,1,0:T(8,128)(2,1)}, bf16[3,48,128]{2,1,0:T(8,128)(2,1)}) custom-call(f32[1,3072]{1,0:T(1,128)} %get-tuple-element.88.refs_0_, f32[8,768]{1,0:T(8,128)} %get-tuple-element.89.refs_1_, f32[3,8,768]{2,1,0:T(8,128)} %get-tuple-element.101.refs_2_, ...), custom_call_target="tpu_custom_call" | custom-call | tf_op jit(solution)/shard_map/exchange/pallas_call | solution.py:1105
  231.9 6.9 %unpack.1 = (f32[768]{0:T(1024)}, f32[768]{0:T(1024)}, f32[2304]{0:T(1024)}, f32[3,2304]{1,0:T(4,128)}, f32[2304]{0:T(1024)}, /*index=5*/f32[33,64]{1,0:T(8,128)...) custom-call(f32[256,384]{1,0:T(8,128)} %get-tuple-element.109.pk, ...), custom_call_target="tpu_custom_call" | custom-call | tf_op jit(solution)/shard_map/unpack/pallas_call | solution.py:1174

commit v6 on v5

--- a/solution.py
+++ b/solution.py
@@ -1168,7 +1168,7 @@
         s(hidden, hidden), s(hidden), s(hidden), s(hidden, hidden), s(hidden), s(hidden), s(hidden, width), s(width), s(width),
         s(width), s(width), s(ff), s(width)]
     shapes += [s(parts[0].shape[1], sum(p.shape[0] for p in parts) * parts[0].shape[2]) for parts in blocks]
-    steps = 6 if results else 1
+    steps = 2 if results else 1
     whole = lambda a: pl.BlockSpec(a.shape, lambda i: (0,) * len(a.shape))
     part = [pl.BlockSpec((a.shape[0] // steps, a.shape[1]), lambda i: (i, 0)) for a in results]
     return pl.pallas_call(

time: 242 us -> 240 us (level)
  no operation moved by 1% of the time
where the time goes in v6:
time: 240 us; the launch traced here: 237 us
  Pallas kernels  236 us (98%)
    pallas_call x1, Pallas kernels, backward_mixer(): pl.pallas_call(functools.partial(backward_kernel, links, plan, len(grads)...  86.8 us
    pallas_call x1, Pallas kernels, mlp(): pl.pallas_call(functools.partial(mlp_kernel, links), grid=(parts,), in_sp...  78.2 us
    pallas_call x1, Pallas kernels, forward_mixer(): pl.pallas_call(forward_kernel, grid=(count,), in_specs=specs, out_specs=[...  35.9 us
    pallas_call x1, Pallas kernels, exchange(): pl.pallas_call(functools.partial(exchange_kernel, sizes, at, plan, len(gr...  30.4 us
    pallas_call x1, Pallas kernels, unpack(): pl.pallas_call(kernel, grid=(steps,), out_shape=shapes + [jax.ShapeDtypeS...  4.85 us

profile of v6, /device:TPU:0, one launch (start us, length us, event | category | flops | bytes accessed | tf_op | source)
XLA Modules:
  0.0 237.0 jit_solution(12259066629832880601)
XLA Ops:
  0.7 35.9 %mixer_forward.1 = (bf16[3,1536,768]{2,1,0:T(8,128)(2,1)}, bf16[3,1536,768]{2,1,0:T(8,128)(2,1)}, bf16[1536,768]{1,0:T(8,128)(2,1)}, bf16[1536,768]{1,0:T(8,128)...) custom-call(bf16[1536,768]{1,0:T(8,128)(2,1)} %bitcast.10, ...), custom_call_target="tpu_custom_call" | custom-call | flops 17515413504 | bytes 47185920 | tf_op jit(solution)/shard_map/mixer_forward/pallas_call | solution.py:437
  36.6 78.2 %mlp.1 = (bf16[1536,768]{1,0:T(8,128)(2,1)}, bf16[1536,768]{1,0:T(8,128)(2,1)}, bf16[6,768,128]{2,1,0:T(8,128)(2,1)}, bf16[24,8,48,128]{3,2,1,0:T(8,128)(2,1)}, ...) custom-call(bf16[1536,768]{1,0:T(8,128)(2,1)} %get-tuple-element.87.mix_ref, ...), custom_call_target="tpu_custom_call" | custom-call | flops 47110422528 | bytes 35389440 | tf_op jit(solution)/shard_map/mlp/pallas_call | solution.py:639
  114.8 86.8 %mixer_backward.1 = (bf16[1536,768]{1,0:T(8,128)(2,1)}, bf16[3,6,8,48,128]{4,3,2,1,0:T(8,128)(2,1)}, f32[3,8,768]{2,1,0:T(8,128)}, f32[8,768]{1,0:T(8,128)}, f32...) custom-call(bf16[2,12,2,2,2,48,128]{6,5,4,3,2,1,0:T(8,128)(2,1)} %bi, ...), custom_call_target="tpu_custom_call" | custom-call | flops 24763170816 | bytes 58982400 | tf_op jit(solution)/shard_map/mixer_backward/pallas_call | solution.py:912
  201.6 30.4 %exchange.1 = (f32[256,384]{1,0:T(8,128)}, bf16[3,48,128]{2,1,0:T(8,128)(2,1)}, bf16[3,48,128]{2,1,0:T(8,128)(2,1)}, bf16[3,48,128]{2,1,0:T(8,128)(2,1)}) custom-call(f32[1,3072]{1,0:T(1,128)} %get-tuple-element.88.refs_0_, f32[8,768]{1,0:T(8,128)} %get-tuple-element.89.refs_1_, f32[3,8,768]{2,1,0:T(8,128)} %get-tuple-element.101.refs_2_, ...), custom_call_target="tpu_custom_call" | custom-call | tf_op jit(solution)/shard_map/exchange/pallas_call | solution.py:1105
  232.0 4.8 %unpack.1 = (f32[768]{0:T(1024)}, f32[768]{0:T(1024)}, f32[2304]{0:T(1024)}, f32[3,2304]{1,0:T(4,128)}, f32[2304]{0:T(1024)}, /*index=5*/f32[33,64]{1,0:T(8,128)...) custom-call(f32[256,384]{1,0:T(8,128)} %get-tuple-element.109.pk, ...), custom_call_target="tpu_custom_call" | custom-call | tf_op jit(solution)/shard_map/unpack/pallas_call | solution.py:1174
